TPU v7x, 32 devices: a whole 2x2x4 slice. The times are simulated.
32 devices in a mesh: dp: 8 (over y, x, core), tp: 4 (over z).
Axes of the slice: x: 2, y: 2, z: 4, core: 2. Of those that a mesh axis runs over, the one named last changes fastest.
Arguments:
- tokens: bfloat16 [4, 1024, 16, 768], P(None, 'tp', 'dp'), may hold values from -6 to 6
- lengths: int32 [4, 16], P(None, 'dp'), may hold values from 128 to 1024, as said below
- cotangent: bfloat16 [4, 1024, 16, 768], P(None, 'tp', 'dp'), may hold values from -6 to 6
- norm1_gain: bfloat16 [768], P('dp'), may hold values from 0.25 to 1.75
- norm1_bias: bfloat16 [768], P('dp'), may hold values from -1.5 to 1.5
- in_weight: bfloat16 [768, 3, 768], P('dp', None, 'tp'), may hold values from -0.21875 to 0.21875
- in_bias: bfloat16 [3, 768], P(None, 'dp'), may hold values from -4 to 4
- filter_base: bfloat16 [2, 2048, 768], P(None, 'dp', 'tp'), may hold values from -5 to 5
- filter_mod: bfloat16 [2, 2048, 768], P(None, 'dp', 'tp'), may hold values from -5 to 5
- out_weight: bfloat16 [768, 768], P('tp', 'dp'), may hold values from -0.4375 to 0.4375
- out_bias: bfloat16 [768], P('dp'), may hold values from -1.5 to 1.5
- norm2_gain: bfloat16 [768], P('dp'), may hold values from 0.25 to 1.75
- norm2_bias: bfloat16 [768], P('dp'), may hold values from -1.5 to 1.5
- gate_weight: bfloat16 [768, 3072], P(None, 'tp'), may hold values from -0.21875 to 0.21875
- up_weight: bfloat16 [768, 3072], P(None, 'tp'), may hold values from -0.21875 to 0.21875
- down_weight: bfloat16 [3072, 768], P('tp'), may hold values from -0.21875 to 0.21875
- down_bias: bfloat16 [768], P('dp'), may hold values from -1.5 to 1.5
Outputs:
- layer_out: bfloat16 [4, 1024, 16, 768], P(None, 'tp', 'dp')
- input_grad: bfloat16 [4, 1024, 16, 768], P(None, 'tp', 'dp')
- grad_norm1_gain: float32 [768], P(('dp', 'tp'))
- grad_norm1_bias: float32 [768], P(('dp', 'tp'))
- grad_in_weight: float32 [768, 3, 768], P('dp', None, 'tp')
- grad_in_bias: float32 [3, 768], P(None, ('dp', 'tp'))
- grad_filter_base: float32 [2, 2048, 768], P(None, 'dp', 'tp')
- grad_filter_mod: float32 [2, 2048, 768], P(None, 'dp', 'tp')
- grad_out_weight: float32 [768, 768], P('tp', 'dp')
- grad_out_bias: float32 [768], P(('dp', 'tp'))
- grad_norm2_gain: float32 [768], P(('dp', 'tp'))
- grad_norm2_bias: float32 [768], P(('dp', 'tp'))
- grad_gate_weight: float32 [768, 3072], P(None, 'tp')
- grad_up_weight: float32 [768, 3072], P(None, 'tp')
- grad_down_weight: float32 [3072, 768], P('tp')
- grad_down_bias: float32 [768], P(('dp', 'tp'))
Inputs may be any that keep to these rules, and one draw needn't show every extreme that they name: `lengths`: in each micro-batch every group of 2 consecutive sequences holds one of exactly 1024 tokens, and one sequence has exactly 128.
All inputs are finite; a program needn't handle non-finite values.
Results may differ from a plain program's by a relative error of at most 0.023.
Values may be sent and summed in bfloat16 or wider, within the bound.
A program may use at most 384 MiB of HBM per device.

v0:
```python
import math

import jax
import jax.numpy as jnp
from jax import lax
from jax.sharding import PartitionSpec as P

EPSILON = 1e-05


def layer_norm(inputs, weight_gain, weight_shift):
    centre = jnp.mean(inputs, axis=-1, keepdims=True)
    centred = inputs - centre
    spread = jnp.mean(centred * centred, axis=-1, keepdims=True)
    return centred * lax.rsqrt(spread + EPSILON) * weight_gain + weight_shift


def transform_table(slot_len):
    frequency = jnp.arange(2 * slot_len, dtype=jnp.int32)[:, None]
    position = jnp.arange(slot_len, dtype=jnp.int32)[None, :]
    angles = (frequency * position % (2 * slot_len)).astype(jnp.float32) * (math.pi / slot_len)
    return jnp.stack([jnp.cos(angles), -jnp.sin(angles)])


def body(
    tokens,
    lengths,
    cotangent,
    norm1_gain,
    norm1_bias,
    in_weight,
    in_bias,
    filter_base,
    filter_mod,
    out_weight,
    out_bias,
    norm2_gain,
    norm2_bias,
    gate_weight,
    up_weight,
    down_weight,
    down_bias,
):
    micro_count, local_slots, group_seqs, model_width = tokens.shape
    tp_size = lax.axis_size("tp")
    tp_place = lax.axis_index("tp")
    slot_len = local_slots * tp_size
    channels = in_weight.shape[2]
    transform_rows = transform_table(slot_len).astype(jnp.bfloat16)
    conv_scale = 0.5 / slot_len
    positions = jnp.arange(slot_len, dtype=jnp.int32)
    own_positions = tp_place * local_slots + jnp.arange(local_slots, dtype=jnp.int32)

    def mixer_weights():
        return (
            lax.all_gather(norm1_gain, "dp", axis=0, tiled=True),
            lax.all_gather(norm1_bias, "dp", axis=0, tiled=True),
            lax.all_gather(norm2_gain, "dp", axis=0, tiled=True),
            lax.all_gather(norm2_bias, "dp", axis=0, tiled=True),
            lax.all_gather(out_bias, "dp", axis=0, tiled=True),
            lax.all_gather(down_bias, "dp", axis=0, tiled=True),
            lax.all_gather(in_bias, "dp", axis=1, tiled=True),
            lax.all_gather(in_weight, "dp", axis=0, tiled=True),
            lax.all_gather(filter_base, "dp", axis=1, tiled=True),
            lax.all_gather(filter_mod, "dp", axis=1, tiled=True),
            lax.all_gather(out_weight, "dp", axis=1, tiled=True),
        )

    filter_shape = (2, 2 * slot_len, channels)
    total_gain_one = jnp.zeros((model_width,), jnp.float32)
    total_bias_one = jnp.zeros((model_width,), jnp.float32)
    total_gain_two = jnp.zeros((model_width,), jnp.float32)
    total_bias_two = jnp.zeros((model_width,), jnp.float32)
    total_out_bias = jnp.zeros((model_width,), jnp.float32)
    total_down_bias = jnp.zeros((model_width,), jnp.float32)
    total_in_bias = jnp.zeros((3, channels), jnp.float32)
    total_in_weight = jnp.zeros((model_width, 3, channels), jnp.float32)
    total_base = jnp.zeros(filter_shape, jnp.float32)
    total_mod = jnp.zeros(filter_shape, jnp.float32)
    total_out_weight = jnp.zeros((channels, model_width), jnp.float32)
    total_gate = jnp.zeros(gate_weight.shape, jnp.float32)
    total_up = jnp.zeros(up_weight.shape, jnp.float32)
    total_down = jnp.zeros(down_weight.shape, jnp.float32)
    layer_outputs = []
    input_grads = []
    for batch_index in range(micro_count):
        inputs = tokens[batch_index].astype(jnp.float32)
        seq_lengths = lengths[batch_index]
        valid_own = (own_positions[:, None] < seq_lengths[None, :]).astype(jnp.float32)[:, :, None]
        valid_full = (positions[:, None] < seq_lengths[None, :]).astype(jnp.float32)[:, :, None]
        length_float = seq_lengths.astype(jnp.float32)[:, None]
        fetched = mixer_weights()
        in_bias_own = lax.dynamic_slice_in_dim(fetched[6], tp_place * channels, channels, 1).astype(
            jnp.float32
        )
        in_local = fetched[7]
        base_full = fetched[8].astype(jnp.float32)
        mod_full = fetched[9].astype(jnp.float32)
        out_local = fetched[10]
        normed_one, pull_one = jax.vjp(
            layer_norm, inputs, fetched[0].astype(jnp.float32), fetched[1].astype(jnp.float32)
        )
        normed_low = normed_one.astype(jnp.bfloat16)
        normed_full = lax.all_gather(normed_low, "tp", axis=0, tiled=True)
        projected = jnp.einsum(
            "tbd,dge->tbge", normed_full, in_local, preferred_element_type=jnp.float32
        )
        projected = projected + in_bias_own
        values = projected[:, :, 0]
        gating = projected[:, :, 1]
        condition = projected[:, :, 2]
        masked_values = (values * valid_full).astype(jnp.bfloat16)
        spectrum = jnp.einsum(
            "rkt,tbc->rkbc", transform_rows, masked_values, preferred_element_type=jnp.float32
        )
        mixing = jnp.tanh(jnp.sum(condition * valid_full, axis=0) / length_float)
        filter_real = base_full[0][:, None, :] + mixing[None] * mod_full[0][:, None, :]
        filter_imag = base_full[1][:, None, :] + mixing[None] * mod_full[1][:, None, :]
        spec_real = spectrum[0]
        spec_imag = spectrum[1]
        product = jnp.stack(
            [
                filter_real * spec_real - filter_imag * spec_imag,
                filter_real * spec_imag + filter_imag * spec_real,
            ],
            axis=0,
        ).astype(jnp.bfloat16)
        conv_out = (
            jnp.einsum("rkt,rkbc->tbc", transform_rows, product, preferred_element_type=jnp.float32)
            * conv_scale
        )
        gated_values = (conv_out * gating).astype(jnp.bfloat16)
        branch = lax.psum_scatter(
            jnp.einsum(
                "tbc,ce->tbe", gated_values, out_local, preferred_element_type=jnp.float32
            ).astype(jnp.bfloat16),
            "tp",
            scatter_dimension=0,
            tiled=True,
        ).astype(jnp.float32) + fetched[4].astype(jnp.float32)
        middle = inputs + valid_own * branch
        normed_two, pull_two = jax.vjp(
            layer_norm, middle, fetched[2].astype(jnp.float32), fetched[3].astype(jnp.float32)
        )
        rows_low = normed_two.astype(jnp.bfloat16)
        bias_down_full = fetched[5].astype(jnp.float32)
        rows_full = lax.all_gather(rows_low, "tp", axis=0, tiled=True)
        gate_pre = jnp.einsum(
            "tbd,df->tbf", rows_full, gate_weight, preferred_element_type=jnp.float32
        )
        up_pre = jnp.einsum("tbd,df->tbf", rows_full, up_weight, preferred_element_type=jnp.float32)
        activated, gelu_pull = jax.vjp(jax.nn.gelu, gate_pre)
        hidden = (activated * up_pre).astype(jnp.bfloat16)
        feed_out = (
            lax.psum_scatter(
                jnp.einsum(
                    "tbf,fd->tbd", hidden, down_weight, preferred_element_type=jnp.float32
                ).astype(jnp.bfloat16),
                "tp",
                scatter_dimension=0,
                tiled=True,
            ).astype(jnp.float32)
            + bias_down_full
        )
        layer_outputs.append((middle + valid_own * feed_out).astype(jnp.bfloat16))
        upstream = cotangent[batch_index].astype(jnp.float32)
        feed_grad = (valid_own * upstream).astype(jnp.bfloat16)
        total_down_bias = total_down_bias + jnp.sum(feed_grad, axis=(0, 1), dtype=jnp.float32)
        grad_full = lax.all_gather(feed_grad, "tp", axis=0, tiled=True)
        total_down = total_down + jnp.einsum(
            "tbf,tbd->fd", hidden, grad_full, preferred_element_type=jnp.float32
        )
        hidden_grad = jnp.einsum(
            "tbd,fd->tbf", grad_full, down_weight, preferred_element_type=jnp.float32
        )
        gate_grad = gelu_pull(hidden_grad * up_pre)[0].astype(jnp.bfloat16)
        up_grad = (hidden_grad * activated).astype(jnp.bfloat16)
        total_gate = total_gate + jnp.einsum(
            "tbd,tbf->df", rows_full, gate_grad, preferred_element_type=jnp.float32
        )
        total_up = total_up + jnp.einsum(
            "tbd,tbf->df", rows_full, up_grad, preferred_element_type=jnp.float32
        )
        normed_two_grad = lax.psum_scatter(
            (
                jnp.einsum(
                    "tbf,df->tbd", gate_grad, gate_weight, preferred_element_type=jnp.float32
                )
                + jnp.einsum("tbf,df->tbd", up_grad, up_weight, preferred_element_type=jnp.float32)
            ).astype(jnp.bfloat16),
            "tp",
            scatter_dimension=0,
            tiled=True,
        ).astype(jnp.float32)
        middle_from_norm, gain_two_grad, bias_two_grad = pull_two(normed_two_grad)
        total_gain_two = total_gain_two + gain_two_grad
        total_bias_two = total_bias_two + bias_two_grad
        middle_grad = upstream + middle_from_norm
        fetched_back = mixer_weights()
        in_back = fetched_back[7]
        mod_back = fetched_back[9].astype(jnp.float32)
        out_back = fetched_back[10]
        branch_grad = (valid_own * middle_grad).astype(jnp.bfloat16)
        total_out_bias = total_out_bias + jnp.sum(branch_grad, axis=(0, 1), dtype=jnp.float32)
        branch_full = lax.all_gather(branch_grad, "tp", axis=0, tiled=True)
        total_out_weight = total_out_weight + jnp.einsum(
            "tbc,tbe->ce", gated_values, branch_full, preferred_element_type=jnp.float32
        )
        gated_grad = jnp.einsum(
            "tbe,ce->tbc", branch_full, out_back, preferred_element_type=jnp.float32
        )
        conv_grad = (gated_grad * gating).astype(jnp.bfloat16)
        gating_grad = gated_grad * conv_out
        product_grad = (
            jnp.einsum(
                "rkt,tbc->rkbc", transform_rows, conv_grad, preferred_element_type=jnp.float32
            )
            * conv_scale
        )
        grad_real = product_grad[0]
        grad_imag = product_grad[1]
        spectrum_grad = jnp.stack(
            [
                filter_real * grad_real + filter_imag * grad_imag,
                filter_real * grad_imag - filter_imag * grad_real,
            ],
            axis=0,
        ).astype(jnp.bfloat16)
        filter_grad_real = grad_real * spec_real + grad_imag * spec_imag
        filter_grad_imag = grad_imag * spec_real - grad_real * spec_imag
        total_base = total_base + jnp.stack(
            [jnp.sum(filter_grad_real, axis=1), jnp.sum(filter_grad_imag, axis=1)]
        )
        total_mod = total_mod + jnp.stack(
            [
                jnp.sum(mixing[None] * filter_grad_real, axis=1),
                jnp.sum(mixing[None] * filter_grad_imag, axis=1),
            ]
        )
        mixing_grad = jnp.sum(
            mod_back[0][:, None, :] * filter_grad_real + mod_back[1][:, None, :] * filter_grad_imag,
            axis=0,
        )
        values_grad = valid_full * jnp.einsum(
            "rkt,rkbc->tbc", transform_rows, spectrum_grad, preferred_element_type=jnp.float32
        )
        condition_grad = valid_full * (mixing_grad * (1.0 - mixing * mixing) / length_float)[None]
        projected_grad = jnp.stack([values_grad, gating_grad, condition_grad], axis=2).astype(
            jnp.bfloat16
        )
        total_in_bias = total_in_bias + jnp.sum(projected_grad, axis=(0, 1), dtype=jnp.float32)
        total_in_weight = total_in_weight + jnp.einsum(
            "tbd,tbge->dge", normed_full, projected_grad, preferred_element_type=jnp.float32
        )
        normed_grad = lax.psum_scatter(
            jnp.einsum(
                "tbge,dge->tbd", projected_grad, in_back, preferred_element_type=jnp.float32
            ).astype(jnp.bfloat16),
            "tp",
            scatter_dimension=0,
            tiled=True,
        ).astype(jnp.float32)
        input_from_norm, gain_one_grad, bias_one_grad = pull_one(normed_grad)
        total_gain_one = total_gain_one + gain_one_grad
        total_bias_one = total_bias_one + bias_one_grad
        input_grads.append((middle_grad + input_from_norm).astype(jnp.bfloat16))
    in_bias_padded = lax.dynamic_update_slice(
        jnp.zeros((3, model_width), jnp.float32), total_in_bias, (jnp.int32(0), tp_place * channels)
    )
    vector_shards = (
        lax.psum_scatter(total_gain_one, ("dp", "tp"), scatter_dimension=0, tiled=True),
        lax.psum_scatter(total_bias_one, ("dp", "tp"), scatter_dimension=0, tiled=True),
        lax.psum_scatter(total_gain_two, ("dp", "tp"), scatter_dimension=0, tiled=True),
        lax.psum_scatter(total_bias_two, ("dp", "tp"), scatter_dimension=0, tiled=True),
        lax.psum_scatter(total_out_bias, ("dp", "tp"), scatter_dimension=0, tiled=True),
        lax.psum_scatter(total_down_bias, ("dp", "tp"), scatter_dimension=0, tiled=True),
        lax.psum_scatter(in_bias_padded, ("dp", "tp"), scatter_dimension=1, tiled=True),
    )
    mixer_shards = (
        lax.psum_scatter(
            total_in_weight.astype(jnp.bfloat16), "dp", scatter_dimension=0, tiled=True
        ).astype(jnp.float32),
        lax.psum_scatter(
            total_base.astype(jnp.bfloat16), "dp", scatter_dimension=1, tiled=True
        ).astype(jnp.float32),
        lax.psum_scatter(
            total_mod.astype(jnp.bfloat16), "dp", scatter_dimension=1, tiled=True
        ).astype(jnp.float32),
        lax.psum_scatter(
            total_out_weight.astype(jnp.bfloat16), "dp", scatter_dimension=1, tiled=True
        ).astype(jnp.float32),
    )
    local_gate, local_up, local_down = (total_gate, total_up, total_down)
    summed_gate, summed_up, summed_down = (
        lax.psum(local_gate.astype(jnp.bfloat16), "dp").astype(jnp.float32),
        lax.psum(local_up.astype(jnp.bfloat16), "dp").astype(jnp.float32),
        lax.psum(local_down.astype(jnp.bfloat16), "dp").astype(jnp.float32),
    )
    return (
        jnp.stack(layer_outputs),
        jnp.stack(input_grads),
        vector_shards[0],
        vector_shards[1],
        mixer_shards[0],
        vector_shards[6],
        mixer_shards[1],
        mixer_shards[2],
        mixer_shards[3],
        vector_shards[4],
        vector_shards[2],
        vector_shards[3],
        summed_gate,
        summed_up,
        summed_down,
        vector_shards[5],
    )


def solution(mesh):
    in_specs = (
        P(None, "tp", "dp", None),
        P(None, "dp"),
        P(None, "tp", "dp", None),
        P("dp"),
        P("dp"),
        P("dp", None, "tp"),
        P(None, "dp"),
        P(None, "dp", "tp"),
        P(None, "dp", "tp"),
        P("tp", "dp"),
        P("dp"),
        P("dp"),
        P("dp"),
        P(None, "tp"),
        P(None, "tp"),
        P("tp", None),
        P("dp"),
    )
    out_specs = (
        P(None, "tp", "dp", None),
        P(None, "tp", "dp", None),
        P(("dp", "tp")),
        P(("dp", "tp")),
        P("dp", None, "tp"),
        P(None, ("dp", "tp")),
        P(None, "dp", "tp"),
        P(None, "dp", "tp"),
        P("tp", "dp"),
        P(("dp", "tp")),
        P(("dp", "tp")),
        P(("dp", "tp")),
        P(None, "tp"),
        P(None, "tp"),
        P("tp", None),
        P(("dp", "tp")),
    )
    return jax.shard_map(body, mesh=mesh, in_specs=in_specs, out_specs=out_specs, check_vma=False)
```

profile of v0, /device:TPU:0, one launch (start us, length us, event | category | flops | bytes accessed | tf_op | source)
XLA Modules:
  0.0 2392.5 jit_solution(8264562869986577405)
XLA Ops:
  203.2 57.4 %all-gather.32.cloned.1.call-done = bf16[1024,2,768]{2,0,1:T(8,128)(2,1)} async-done(((bf16[256,2,768]{2,0,1:T(8,128)(2,1)}), bf16[1024,2,768]{2,0,1:T(8,128)(2,1)}) %all-gather.32.cloned.1.call-update) | async-done | bytes 3145744 | tf_op jit(solution)/shard_map/all_gather | solution.py:104
  388.1 60.5 %reduce-scatter.24.cloned.1.call-done = bf16[256,2,768]{2,0,1:T(8,128)(2,1)} async-done(((bf16[1024,2,768]{2,0,1:T(8,128)(2,1)}), bf16[256,2,768]{2,0,1:T(8,128)(2,1)}) %reduce-scatter.24.cloned.1.call-update) | async-done | bytes 786448 | tf_op jit(solution)/shard_map/reduce_scatter | solution.py:133
  448.6 63.2 %reduce-scatter.36.cloned.1.call-done = bf16[256,2,768]{2,0,1:T(8,128)(2,1)} async-done(((bf16[1024,2,768]{2,0,1:T(8,128)(2,1)}), bf16[256,2,768]{2,0,1:T(8,128)(2,1)}) %reduce-scatter.36.cloned.1.call-update) | async-done | bytes 786448 | tf_op jit(solution)/shard_map/reduce_scatter | solution.py:133
  532.4 49.3 %all-gather.30.cloned.1.call-done = bf16[1024,2,768]{2,0,1:T(8,128)(2,1)} async-done(((bf16[256,2,768]{2,0,1:T(8,128)(2,1)}), bf16[1024,2,768]{2,0,1:T(8,128)(2,1)}) %all-gather.30.cloned.1.call-update) | async-done | bytes 3145744 | tf_op jit(solution)/shard_map/all_gather | solution.py:147
  589.1 56.9 %all-gather.44.cloned.1.call-done = bf16[1024,2,768]{2,0,1:T(8,128)(2,1)} async-done(((bf16[256,2,768]{2,0,1:T(8,128)(2,1)}), bf16[1024,2,768]{2,0,1:T(8,128)(2,1)}) %all-gather.44.cloned.1.call-update) | async-done | bytes 3145744 | tf_op jit(solution)/shard_map/all_gather | solution.py:169
  707.2 63.2 %reduce-scatter.44.cloned.1.call-done = bf16[256,2,768]{2,0,1:T(8,128)(2,1)} async-done(((bf16[1024,2,768]{2,0,1:T(8,128)(2,1)}), bf16[256,2,768]{2,0,1:T(8,128)(2,1)}) %reduce-scatter.44.cloned.1.call-update) | async-done | bytes 786448 | tf_op jit(solution)/shard_map/reduce_scatter | solution.py:184
  778.4 63.0 %all-gather.38.cloned.1.call-done = bf16[1024,2,768]{2,0,1:T(8,128)(2,1)} async-done(((bf16[256,2,768]{2,0,1:T(8,128)(2,1)}), bf16[1024,2,768]{2,0,1:T(8,128)(2,1)}) %all-gather.38.cloned.1.call-update) | async-done | bytes 3145744 | tf_op jit(solution)/shard_map/all_gather | solution.py:147
  853.5 52.1 %all-gather.52.cloned.1.call-done = bf16[1024,2,768]{2,0,1:T(8,128)(2,1)} async-done(((bf16[256,2,768]{2,0,1:T(8,128)(2,1)}), bf16[1024,2,768]{2,0,1:T(8,128)(2,1)}) %all-gather.52.cloned.1.call-update) | async-done | bytes 3145744 | tf_op jit(solution)/shard_map/all_gather | solution.py:169
  928.1 54.9 %reduce-scatter.52.cloned.1.call-done = bf16[256,2,768]{2,0,1:T(8,128)(2,1)} async-done(((bf16[1024,2,768]{2,0,1:T(8,128)(2,1)}), bf16[256,2,768]{2,0,1:T(8,128)(2,1)}) %reduce-scatter.52.cloned.1.call-update) | async-done | bytes 786448 | tf_op jit(solution)/shard_map/reduce_scatter | solution.py:184
  995.0 61.7 %all-gather.26.cloned.1.call-done = bf16[1024,2,768]{2,0,1:T(8,128)(2,1)} async-done(((bf16[256,2,768]{2,0,1:T(8,128)(2,1)}), bf16[1024,2,768]{2,0,1:T(8,128)(2,1)}) %all-gather.26.cloned.1.call-update) | async-done | bytes 3145744 | tf_op jit(solution)/shard_map/all_gather | solution.py:147
  1068.7 52.1 %all-gather.40.cloned.1.call-done = bf16[1024,2,768]{2,0,1:T(8,128)(2,1)} async-done(((bf16[256,2,768]{2,0,1:T(8,128)(2,1)}), bf16[1024,2,768]{2,0,1:T(8,128)(2,1)}) %all-gather.40.cloned.1.call-update) | async-done | bytes 3145744 | tf_op jit(solution)/shard_map/all_gather | solution.py:169
  1139.8 45.4 %all-gather.34.cloned.1.call-done = bf16[1024,2,768]{2,0,1:T(8,128)(2,1)} async-done(((bf16[256,2,768]{2,0,1:T(8,128)(2,1)}), bf16[1024,2,768]{2,0,1:T(8,128)(2,1)}) %all-gather.34.cloned.1.call-update) | async-done | bytes 3145744 | tf_op jit(solution)/shard_map/all_gather | solution.py:147
  1197.3 52.1 %all-gather.48.cloned.1.call-done = bf16[1024,2,768]{2,0,1:T(8,128)(2,1)} async-done(((bf16[256,2,768]{2,0,1:T(8,128)(2,1)}), bf16[1024,2,768]{2,0,1:T(8,128)(2,1)}) %all-gather.48.cloned.1.call-update) | async-done | bytes 3145744 | tf_op jit(solution)/shard_map/all_gather | solution.py:169
  1315.8 57.5 %reduce-scatter.48.cloned.1.call-done = bf16[256,2,768]{2,0,1:T(8,128)(2,1)} async-done(((bf16[1024,2,768]{2,0,1:T(8,128)(2,1)}), bf16[256,2,768]{2,0,1:T(8,128)(2,1)}) %reduce-scatter.48.cloned.1.call-update) | async-done | bytes 786448 | tf_op jit(solution)/shard_map/reduce_scatter | solution.py:184
  1397.4 41.5 %all-gather.46.cloned.1.call-done = bf16[1024,2,768]{2,0,1:T(8,128)(2,1)} async-done(((bf16[256,2,768]{2,0,1:T(8,128)(2,1)}), bf16[1024,2,768]{2,0,1:T(8,128)(2,1)}) %all-gather.46.cloned.1.call-update) | async-done | bytes 3145744 | tf_op jit(solution)/shard_map/all_gather | solution.py:205
  1579.6 50.3 %all-gather.42.cloned.1.call-done = bf16[1024,2,768]{2,0,1:T(8,128)(2,1)} async-done(((bf16[256,2,768]{2,0,1:T(8,128)(2,1)}), bf16[1024,2,768]{2,0,1:T(8,128)(2,1)}) %all-gather.42.cloned.1.call-update) | async-done | bytes 3145744 | tf_op jit(solution)/shard_map/all_gather | solution.py:205
  1870.2 61.0 %reduce-scatter.46.cloned.1.call-done = bf16[256,2,768]{2,0,1:T(8,128)(2,1)} async-done(((bf16[1024,2,768]{2,0,1:T(8,128)(2,1)}), bf16[256,2,768]{2,0,1:T(8,128)(2,1)}) %reduce-scatter.46.cloned.1.call-update) | async-done | bytes 786448 | tf_op jit(solution)/shard_map/reduce_scatter | solution.py:255
  1931.2 62.6 %reduce-scatter.42.cloned.1.call-done = bf16[256,2,768]{2,0,1:T(8,128)(2,1)} async-done(((bf16[1024,2,768]{2,0,1:T(8,128)(2,1)}), bf16[256,2,768]{2,0,1:T(8,128)(2,1)}) %reduce-scatter.42.cloned.1.call-update) | async-done | bytes 786448 | tf_op jit(solution)/shard_map/reduce_scatter | solution.py:255
  1993.7 62.7 %reduce-scatter.50.cloned.1.call-done = bf16[256,2,768]{2,0,1:T(8,128)(2,1)} async-done(((bf16[1024,2,768]{2,0,1:T(8,128)(2,1)}), bf16[256,2,768]{2,0,1:T(8,128)(2,1)}) %reduce-scatter.50.cloned.1.call-update) | async-done | bytes 786448 | tf_op jit(solution)/shard_map/reduce_scatter | solution.py:255
  2063.7 55.5 %reduce-scatter.54.cloned.1.call-done = bf16[256,2,768]{2,0,1:T(8,128)(2,1)} async-done(((bf16[1024,2,768]{2,0,1:T(8,128)(2,1)}), bf16[256,2,768]{2,0,1:T(8,128)(2,1)}) %reduce-scatter.54.cloned.1.call-update) | async-done | bytes 786448 | tf_op jit(solution)/shard_map/reduce_scatter | solution.py:255
  2127.0 47.2 %all-reduce.13 = (f32[768]{0:T(1024)}, f32[768]{0:T(1024)}, f32[3,768]{1,0:T(4,128)}, f32[768]{0:T(1024)}, f32[768]{0:T(1024)}, /*index=5*/f32[768]{0:T(1024)}, f32[768]{0:T(1024)}) all-reduce(f32[768]{0:T(1024)} %add_add_fusion.14, f32[768]{0:T(1024)S(1)} %add_add_fusion.13, ...), channel_id=18, replica_groups=mesh['dp'=8,'tp'=4] {'dp','tp'}, use_global_device_ids=true, to_apply=%region_60.61.clone | all-reduce | flops 6912 | bytes 55296
  2192.2 53.0 %reduce-scatter.30.cloned.1.call-done = bf16[256,2,768]{2,0,1:T(8,128)(2,1)} async-done(((bf16[1024,2,768]{2,0,1:T(8,128)(2,1)}), bf16[256,2,768]{2,0,1:T(8,128)(2,1)}) %reduce-scatter.30.cloned.1.call-update) | async-done | bytes 786448 | tf_op jit(solution)/shard_map/reduce_scatter | solution.py:155
  2249.4 58.6 %reduce-scatter.34.cloned.1.call-done = bf16[256,2,768]{2,0,1:T(8,128)(2,1)} async-done(((bf16[1024,2,768]{2,0,1:T(8,128)(2,1)}), bf16[256,2,768]{2,0,1:T(8,128)(2,1)}) %reduce-scatter.34.cloned.1.call-update) | async-done | bytes 786448 | tf_op jit(solution)/shard_map/reduce_scatter | solution.py:155
  2312.0 59.0 %reduce-scatter.38.cloned.1.call-done = bf16[256,2,768]{2,0,1:T(8,128)(2,1)} async-done(((bf16[1024,2,768]{2,0,1:T(8,128)(2,1)}), bf16[256,2,768]{2,0,1:T(8,128)(2,1)}) %reduce-scatter.38.cloned.1.call-update) | async-done | bytes 786448 | tf_op jit(solution)/shard_map/reduce_scatter | solution.py:155
  (957 shorter events, 1032.9 us)
Async XLA Ops:
  60.7 199.8 %all-gather.32.cloned.1.call-start = ((), (), s32[]{:S(2)}) async-start(), calls=%async_computation.30 | async-start | bytes 3932160 | tf_op jit(solution)/shard_map/all_gather | solution.py:104
  61.3 262.8 %all-gather.22.cloned.1.call-start = ((), (), s32[]{:S(2)}) async-start(), calls=%async_computation.21 | async-start | bytes 3932160 | tf_op jit(solution)/shard_map/all_gather | solution.py:104
  61.9 324.1 %reduce-scatter.28.cloned.1.call-start = ((), (), s32[]{:S(2)}) async-start(), calls=%async_computation.27 | async-start | bytes 3932160 | tf_op jit(solution)/shard_map/reduce_scatter | solution.py:133
  359.9 221.8 %all-gather.30.cloned.1.call-start = ((), (), s32[]{:S(2)}) async-start(), calls=%async_computation.28 | async-start | bytes 3932160 | tf_op jit(solution)/shard_map/all_gather | solution.py:147
  518.8 188.4 %reduce-scatter.32.cloned.1.call-start = ((), (), s32[]{:S(2)}) async-start(), calls=%async_computation.31 | async-start | bytes 3932160 | tf_op jit(solution)/shard_map/reduce_scatter | solution.py:133
  531.9 238.4 %reduce-scatter.44.cloned.1.call-start = ((), (), s32[]{:S(2)}) async-start(), calls=%async_computation.43 | async-start | bytes 3932160 | tf_op jit(solution)/shard_map/reduce_scatter | solution.py:184
  669.7 171.7 %all-gather.38.cloned.1.call-start = ((), (), s32[]{:S(2)}) async-start(), calls=%async_computation.36 | async-start | bytes 3932160 | tf_op jit(solution)/shard_map/all_gather | solution.py:147
  778.4 204.6 %reduce-scatter.52.cloned.1.call-start = ((), (), s32[]{:S(2)}) async-start(), calls=%async_computation.51 | async-start | bytes 3932160 | tf_op jit(solution)/shard_map/reduce_scatter | solution.py:184
  993.6 191.6 %all-gather.34.cloned.1.call-start = ((), (), s32[]{:S(2)}) async-start(), calls=%async_computation.32 | async-start | bytes 3932160 | tf_op jit(solution)/shard_map/all_gather | solution.py:147
  994.4 255.0 %all-gather.48.cloned.1.call-start = ((), (), s32[]{:S(2)}) async-start(), calls=%async_computation.46 | async-start | bytes 3932160 | tf_op jit(solution)/shard_map/all_gather | solution.py:169
  995.0 315.7 %reduce-scatter.40.cloned.1.call-start = ((), (), s32[]{:S(2)}) async-start(), calls=%async_computation.39 | async-start | bytes 3932160 | tf_op jit(solution)/shard_map/reduce_scatter | solution.py:184
  1139.6 233.7 %reduce-scatter.48.cloned.1.call-start = ((), (), s32[]{:S(2)}) async-start(), calls=%async_computation.47 | async-start | bytes 3932160 | tf_op jit(solution)/shard_map/reduce_scatter | solution.py:184
  1272.6 256.9 %all-gather.54.cloned.1.call-start = ((), (), s32[]{:S(2)}) async-start(), calls=%async_computation.52 | async-start | bytes 3932160 | tf_op jit(solution)/shard_map/all_gather | solution.py:205
  1381.0 185.3 %all-gather.50.cloned.1.call-start = ((), (), s32[]{:S(2)}) async-start(), calls=%async_computation.48 | async-start | bytes 3932160 | tf_op jit(solution)/shard_map/all_gather | solution.py:205
  1497.1 309.2 %all-reduce.18.cloned.1.call-start = ((), (), s32[]{:S(2)}) async-start(), calls=%async_computation.58 | async-start | bytes 7077888 | tf_op jit(solution)/shard_map/psum | solution.py:295
  1525.8 291.1 %reduce-scatter.62.cloned.1.call-start = ((), (), s32[]{:S(2)}) async-start(), calls=%async_computation.57 | async-start | bytes 442368
  1752.1 179.1 %reduce-scatter.46.cloned.1.call-start = ((), (), s32[]{:S(2)}) async-start(), calls=%async_computation.45 | async-start | bytes 3932160 | tf_op jit(solution)/shard_map/reduce_scatter | solution.py:255
  1758.6 235.1 %reduce-scatter.42.cloned.1.call-start = ((), (), s32[]{:S(2)}) async-start(), calls=%async_computation.41 | async-start | bytes 3932160 | tf_op jit(solution)/shard_map/reduce_scatter | solution.py:255
  1766.0 290.4 %reduce-scatter.50.cloned.1.call-start = ((), (), s32[]{:S(2)}) async-start(), calls=%async_computation.49 | async-start | bytes 3932160 | tf_op jit(solution)/shard_map/reduce_scatter | solution.py:255
  1772.1 347.1 %reduce-scatter.54.cloned.1.call-start = ((), (), s32[]{:S(2)}) async-start(), calls=%async_computation.53 | async-start | bytes 3932160 | tf_op jit(solution)/shard_map/reduce_scatter | solution.py:255
  1778.3 409.7 %reduce-scatter.26.cloned.1.call-start = ((), (), s32[]{:S(2)}) async-start(), calls=%async_computation.25 | async-start | bytes 3932160 | tf_op jit(solution)/shard_map/reduce_scatter | solution.py:155
  1785.1 460.2 %reduce-scatter.30.cloned.1.call-start = ((), (), s32[]{:S(2)}) async-start(), calls=%async_computation.29 | async-start | bytes 3932160 | tf_op jit(solution)/shard_map/reduce_scatter | solution.py:155
  1791.3 516.6 %reduce-scatter.34.cloned.1.call-start = ((), (), s32[]{:S(2)}) async-start(), calls=%async_computation.33 | async-start | bytes 3932160 | tf_op jit(solution)/shard_map/reduce_scatter | solution.py:155
  1797.6 573.5 %reduce-scatter.38.cloned.1.call-start = ((), (), s32[]{:S(2)}) async-start(), calls=%async_computation.37 | async-start | bytes 3932160 | tf_op jit(solution)/shard_map/reduce_scatter | solution.py:155
  (323 other events, 15606.7 us)
Sparse Core Ops, SparseCore 0:
  68.6 63.5 all-gather.35
  134.1 62.1 all-gather.27
  198.3 62.1 all-gather.31
  261.9 62.1 all-gather.21
  388.3 60.2 reduce-scatter.23
  451.5 60.2 reduce-scatter.35
  518.2 63.4 all-gather.29
  583.9 62.1 all-gather.43
  710.0 60.2 reduce-scatter.43
  777.9 63.4 all-gather.37
  843.4 62.1 all-gather.51
  993.2 63.4 all-gather.25
  1058.7 62.1 all-gather.39
  1123.0 62.1 all-gather.33
  1187.2 62.1 all-gather.47
  1313.0 60.2 reduce-scatter.47
  1375.4 63.4 all-gather.45
  1440.4 62.1 all-gather.53
  1504.1 62.1 all-gather.49
  1567.7 62.1 all-gather.41
  1633.4 72.8 all-reduce.17
  2121.4 61.2 reduce-scatter.25
  2247.6 60.2 reduce-scatter.33
  2310.8 60.2 reduce-scatter.37
  (15 shorter events, 737.2 us)
where the time goes:
time: 2400 us; the launch traced here: 2390 us
  waiting for transfers between devices  1500 us (62%)
  matrix products  408 us (17%)
  other arithmetic  279 us (12%)
  blocking collectives  105 us (4%)
  local copies, waits for them, and re-layouts  78.4 us (3%)
    reduce_scatter x4, waiting for transfers between devices, body(): lax.psum_scatter(jnp.einsum('tbge,dge->tbd', projected_grad, in_back, pre...  242 us
    all_gather x4, waiting for transfers between devices, body(): rows_full = lax.all_gather(rows_low, 'tp', axis=0, tiled=True)  219 us
    all_gather x4, waiting for transfers between devices, body(): grad_full = lax.all_gather(feed_grad, 'tp', axis=0, tiled=True)  213 us
    reduce_scatter x4, waiting for transfers between devices, body(): lax.psum_scatter((jnp.einsum('tbf,df->tbd', gate_grad, gate_weight, prefe...  212 us
    reduce_scatter x4, waiting for transfers between devices, body(): lax.psum_scatter(jnp.einsum('tbc,ce->tbe', gated_values, out_local, prefe...  178 us
    reduce_scatter x4, waiting for transfers between devices, body(): lax.psum_scatter(jnp.einsum('tbf,fd->tbd', hidden, down_weight, preferred...  171 us
    all_gather x4, waiting for transfers between devices, body(): branch_full = lax.all_gather(branch_grad, 'tp', axis=0, tiled=True)  115 us
    another operation x10, other arithmetic  97.8 us
  transfers between devices with their start and end apart: 39, of which 31 were waited for; matrix products, arithmetic and copies ran while one was open for 29% of the time, Pallas kernels for 0%

commit v1 on v0

v1 whole, which is shorter than its diff:
```python
import functools
import math

import jax
import jax.numpy as jnp
import numpy as np
from jax import lax
from jax.experimental import pallas as pl
from jax.experimental.pallas import tpu as pltpu
from jax.sharding import PartitionSpec as P

EPSILON = 1e-05
BF = jnp.bfloat16
F32 = jnp.float32
GELU_A = math.sqrt(2.0 / math.pi)
GELU_B = 0.044715


def packed_table(slot_len):
    frequency = np.arange(slot_len, dtype=np.int64)[:, None]
    position = np.arange(slot_len, dtype=np.int64)[None, :]
    angles = (frequency * position % (2 * slot_len)).astype(np.float32) * np.float32(math.pi / slot_len)
    top = np.cos(angles)
    low = -np.sin(angles)
    low[0] = 1.0 - 2.0 * (np.arange(slot_len) % 2)
    return np.concatenate([top, low]).astype(np.float32).astype(jnp.bfloat16)


def shift(x, axis, step):
    n = lax.axis_size(axis)
    return lax.ppermute(x, axis, [(i, (i + step) % n) for i in range(n)])


def exchange(pieces, place, n):
    out = [(place, lax.dynamic_index_in_dim(pieces, place, 0, keepdims=False))]
    for step in range(1, n):
        block = lax.dynamic_index_in_dim(pieces, (place + step) % n, 0, keepdims=False)
        out.append(((place + n - step) % n, shift(block, "tp", step)))
    return out


def mm(a, b):
    return lax.dot_general(a, b, (((1,), (0,)), ((), ())), preferred_element_type=F32)


def mm_nt(a, b):
    return lax.dot_general(a, b, (((1,), (1,)), ((), ())), preferred_element_type=F32)


def mm_tn(a, b):
    return lax.dot_general(a, b, (((0,), (0,)), ((), ())), preferred_element_type=F32)


def mean_of(v):
    return jnp.sum(v, axis=-1, keepdims=True) * (1.0 / v.shape[-1])


def standardize(v):
    centred = v - mean_of(v)
    inverse = lax.rsqrt(mean_of(centred * centred) + EPSILON)
    return centred * inverse, inverse


def norm_back(e, gain, s, q):
    eg = e * gain
    return q * (eg - mean_of(eg) - s * mean_of(eg * s))


def gelu_parts(v):
    square = v * v
    th = jnp.tanh(v * (GELU_A + (GELU_A * GELU_B) * square))
    rise = 0.5 + 0.5 * th
    act = v * rise
    slope = rise + act * (1.0 - th) * (GELU_A + (3.0 * GELU_A * GELU_B) * square)
    return act, slope


def live(rows, first, count):
    at = lax.broadcasted_iota(jnp.int32, (rows, 1), 0) + first
    return jnp.where(at < count, 1.0, 0.0)


def joined(ref):
    v = ref[...]
    return v.reshape(-1, v.shape[-1])


def two_part_dot(a, b, dims):
    high = a.astype(BF)
    low = (a - high.astype(F32)).astype(BF)
    return lax.dot_general(high, b, (dims, ((), ())), preferred_element_type=F32) + lax.dot_general(
        low, b, (dims, ((), ())), preferred_element_type=F32
    )


def top_row(v, rows=8):
    r = lax.broadcasted_iota(jnp.int32, (rows, v.shape[1]), 0)
    return jnp.where(r == 0, jnp.broadcast_to(v, (rows, v.shape[1])), 0.0)


def project_kernel(tile, lens, x, wv, wg, wc, vec, n1, values, gating, nsum, mixing):
    s, t = pl.program_id(0), pl.program_id(1)
    count = lens[s]
    valid = live(tile, t * tile, count)
    std, _ = standardize(x[0].astype(F32))
    normed = (std * vec[0:1] + vec[1:2]).astype(BF)
    n1[0] = normed
    values[0] = ((mm(normed, joined(wv)) + vec[6:7]) * valid).astype(BF)
    gating[0] = (mm(normed, joined(wg)) + vec[7:8]).astype(BF)
    part = top_row(jnp.sum(normed.astype(F32) * valid, axis=0, keepdims=True))

    @pl.when(t == 0)
    def _():
        nsum[0] = part

    @pl.when(t > 0)
    def _():
        nsum[0] += part

    @pl.when(t == pl.num_programs(1) - 1)
    def _():
        length = count.astype(F32)
        cond = two_part_dot(nsum[0], joined(wc), ((1,), (0,))) + length * vec[8:9]
        mixing[0] = jnp.tanh(cond / length)


def filters_of(refs, slots, mix):
    base_r, base_i, mod_r, mod_i = [jnp.concatenate([ref[j] for j in slots]).astype(F32) for ref in refs]
    return base_r + mix * mod_r, base_i + mix * mod_i, mod_r, mod_i


def spectral_kernel(slots, scale, values, gating, mixing, table, table_t, f0, f1, f2, f3, spec, conv, gated):
    v = mm(table[...], values[0])
    n = v.shape[0] // 2
    spec[0] = v.astype(BF)
    sr, si = v[:n], v[n:]
    fr, fi, _, _ = filters_of((f0, f1, f2, f3), slots, mixing[0, 0:1])
    edge = lax.broadcasted_iota(jnp.int32, (n, 1), 0) == 0
    fr2 = jnp.where(edge, fi, fr)
    fi = jnp.where(edge, 0.0, fi)
    prod = jnp.concatenate([(fr * sr - fi * si).astype(BF), (fr2 * si + fi * sr).astype(BF)])
    out = mm(table_t[...], prod) * scale
    conv[0] = out.astype(BF)
    gated[0] = (out * gating[0].astype(F32)).astype(BF)


def feed_kernel(tile, n_tp, lens, x, gated, w_out, wg, wu, wd, vec, middle, n2, act, side, hidden, out):
    s, t = pl.program_id(0), pl.program_id(1)
    valid = live(tile, t * tile, lens[s])
    mid = x[0].astype(F32) + valid * (mm_nt(gated[0], joined(w_out)) + vec[4:5])
    middle[0] = mid
    std, _ = standardize(mid)
    normed = (std * vec[2:3] + vec[3:4]).astype(BF)
    n2[0] = normed
    feed = jnp.zeros(mid.shape, F32)
    for p in range(n_tp):
        gate = mm(normed, joined(wg.at[:, p]))
        up = mm(normed, joined(wu.at[:, p]))
        a, slope = gelu_parts(gate)
        act[0, p] = a.astype(BF)
        side[0, p] = (up * slope).astype(BF)
        h = (a * up).astype(BF)
        hidden[0, p] = h
        feed += mm(h, joined(wd.at[:, p]))
    out[0] = (mid + valid * (feed + vec[5:6])).astype(BF)


def feed_back_kernel(tile, tiles, lens, cot, n2, act, side, hidden, wg, wu, wd, e_out, d_gate, d_up, d_down, e_acc, acc_g, acc_u, acc_d):
    p, u = pl.program_id(0), pl.program_id(1)
    last = pl.num_programs(1) - 1
    valid = live(tile, lax.rem(u, tiles) * tile, lens[u // tiles])
    fg = (cot[0].astype(F32) * valid).astype(BF)
    hg = mm_nt(fg, joined(wd.at[:, 0]))
    gg = (hg * side[0, 0].astype(F32)).astype(BF)
    ug = (hg * act[0, 0].astype(F32)).astype(BF)
    part = mm_nt(gg, joined(wg.at[:, 0])) + mm_nt(ug, joined(wu.at[:, 0]))

    @pl.when(p == 0)
    def _():
        e_acc[u] = part

    @pl.when(p > 0)
    def _():
        e_acc[u] += part

    e_out[0] = e_acc[u]
    normed = n2[0]
    parts = (mm_tn(normed, gg), mm_tn(normed, ug), mm_tn(hidden[0, 0], fg))

    @pl.when(u == 0)
    def _():
        for acc, v in zip((acc_g, acc_u, acc_d), parts):
            acc[...] = v

    @pl.when(u > 0)
    def _():
        for acc, v in zip((acc_g, acc_u, acc_d), parts):
            acc[...] += v

    @pl.when(u == last)
    def _():
        for acc, out in zip((acc_g, acc_u, acc_d), (d_gate, d_up, d_down)):
            out[:, 0] = acc[...].astype(BF).reshape(out.shape[0], out.shape[2], out.shape[3])


def branch_back_kernel(tile, lens, e, middle, cot, gated, gating, conv, w_out, vec, mg_out, cg, gtg, d_out, sums, acc):
    s, t = pl.program_id(0), pl.program_id(1)
    begin = (s == 0) & (t == 0)
    end = (s == pl.num_programs(0) - 1) & (t == pl.num_programs(1) - 1)
    valid = live(tile, t * tile, lens[s])
    up = cot[0].astype(F32)
    fg = (up * valid).astype(BF).astype(F32)
    std, inverse = standardize(middle[0])
    grad = e[0]
    mg = up + norm_back(grad, vec[2:3], std, inverse)
    mg_out[0] = mg
    bgr = (mg * valid).astype(BF)
    ggr = mm(bgr, joined(w_out))
    cg[0] = (ggr * gating[0].astype(F32)).astype(BF)
    gtg[0] = (ggr * conv[0].astype(F32)).astype(BF)
    part = mm_tn(bgr, gated[0])
    rows = [grad * std, grad, bgr.astype(F32), fg]
    rows = [jnp.sum(r, axis=0, keepdims=True) for r in rows]

    @pl.when(begin)
    def _():
        acc[...] = part
        sums[...] = jnp.zeros(sums.shape, F32)

    @pl.when(jnp.logical_not(begin))
    def _():
        acc[...] += part

    for i, r in enumerate(rows):
        sums[i : i + 1] += r

    @pl.when(end)
    def _():
        d_out[...] = acc[...].astype(BF).reshape(d_out.shape)


def spectral_back_kernel(slots, scale, lens, cg, spec, mixing, table, table_t, f0, f1, f2, f3, vg, fgrad, cgv, acc):
    s = pl.program_id(1)
    count = lens[s]
    v = mm(table[...], cg[0]) * scale
    n = v.shape[0] // 2
    pr, pi = v[:n], v[n:]
    mix = mixing[0, 0:1]
    fr, fi, mod_r, mod_i = filters_of((f0, f1, f2, f3), slots, mix)
    edge = lax.broadcasted_iota(jnp.int32, (n, 1), 0) == 0
    fr2 = jnp.where(edge, fi, fr)
    fi = jnp.where(edge, 0.0, fi)
    sg = jnp.concatenate([(fr * pr + fi * pi).astype(BF), (fr2 * pi - fi * pr).astype(BF)])
    sr, si = spec[0, :n].astype(F32), spec[0, n:].astype(F32)
    both = pi * si
    dr = pr * sr + jnp.where(edge, 0.0, both)
    di = jnp.where(edge, both, pi * sr - pr * si)
    mixg = jnp.sum(mod_r * dr + mod_i * di, axis=0, keepdims=True)
    step = mixg * (1.0 - mix * mix) / count.astype(F32)
    cgv[0] = top_row(step.astype(BF).astype(F32))
    vg[0] = (mm(table_t[...], sg) * live(n, 0, count)).astype(BF)
    parts = (dr, di, mix * dr, mix * di)

    @pl.when(s == 0)
    def _():
        for i, part in enumerate(parts):
            acc[i] = part

    @pl.when(s > 0)
    def _():
        for i, part in enumerate(parts):
            acc[i] += part

    @pl.when(s == pl.num_programs(1) - 1)
    def _():
        size = n // len(slots)
        for j in range(len(slots)):
            k = slots.index(j)
            for i in range(4):
                fgrad[j, pl.ds(i * size, size)] = acc[i, pl.ds(k * size, size)].astype(BF)


def input_back_kernel(tile, lens, vg, gtg, n1, x, mg, nsum, cgv, wv, wg, wc, d_out, sums_in, vec, ig, d_in, sums, acc_v, acc_g, acc_c):
    s, t = pl.program_id(0), pl.program_id(1)
    begin = (s == 0) & (t == 0)
    end = (s == pl.num_programs(0) - 1) & (t == pl.num_programs(1) - 1)
    count = lens[s]
    valid = live(tile, t * tile, count)
    cvec = mm_nt(cgv[0].astype(BF), joined(wc))[0:1]
    vgb, gtb = vg[0], gtg[0]
    e = mm_nt(vgb, joined(wv)) + mm_nt(gtb, joined(wg)) + valid * cvec
    std, inverse = standardize(x[0].astype(F32))
    ig[0] = (mg[0] + norm_back(e, vec[0:1], std, inverse)).astype(BF)
    normed = n1[0]
    part_v, part_g = mm_tn(normed, vgb), mm_tn(normed, gtb)
    rows = [e * std, e, vgb.astype(F32), gtb.astype(F32)]
    rows = [jnp.sum(r, axis=0, keepdims=True) for r in rows]

    @pl.when(begin)
    def _():
        acc_v[...] = part_v
        acc_g[...] = part_g
        acc_c[...] = jnp.zeros(acc_c.shape, F32)
        sums[...] = jnp.zeros(sums.shape, F32)
        sums[2:6] = sums_in[0:4]

    @pl.when(jnp.logical_not(begin))
    def _():
        acc_v[...] += part_v
        acc_g[...] += part_g

    for i, r in zip((0, 1, 6, 7), rows):
        sums[i : i + 1] += r

    @pl.when(t == 0)
    def _():
        acc_c[...] += two_part_dot(nsum[0], cgv[0].astype(BF), ((0,), (0,)))
        sums[8:9] += cgv[0, 0:1] * count.astype(F32)

    @pl.when(end)
    def _():
        r = d_out.shape[1]
        shape = (d_in.shape[0], r, d_in.shape[2])
        for i, acc in enumerate((acc_v, acc_g, acc_c)):
            d_in[:, i * r : (i + 1) * r] = acc[...].astype(BF).reshape(shape)
        d_in[:, 3 * r :] = d_out[...]


def call(kernel, grid, lens, ins, in_specs, outs, out_specs, scratch, flops, name, limit=56):
    spec = pltpu.PrefetchScalarGridSpec(
        num_scalar_prefetch=1, grid=grid, in_specs=in_specs, out_specs=out_specs, scratch_shapes=scratch
    )
    moved = sum(math.prod(v.shape) * v.dtype.itemsize for v in list(ins) + list(outs))
    return pl.pallas_call(
        kernel,
        grid_spec=spec,
        out_shape=tuple(outs),
        compiler_params=pltpu.CompilerParams(
            dimension_semantics=("arbitrary",) * len(grid), vmem_limit_bytes=limit * 1024 * 1024
        ),
        cost_estimate=pl.CostEstimate(flops=int(flops), bytes_accessed=int(moved), transcendentals=0),
        name=name,
    )(lens, *ins)


def once(block, index):
    return pl.BlockSpec(block, lambda *_: index, pipeline_mode=pl.Buffered(1))


def shape_of(shape, dtype):
    return jax.ShapeDtypeStruct(shape, dtype)


def project(x, lens, aw, vec):
    own, n, width = x.shape
    tile = min(512, n)
    nd, r = aw.shape[0], width // aw.shape[0]
    tok = pl.BlockSpec((1, tile, width), lambda s, t, *_: (s, t, 0))
    one = pl.BlockSpec((1, 8, width), lambda s, t, *_: (s, 0, 0))
    weights = [once((nd, r, width), (0, g, 0)) for g in range(3)]
    sd = shape_of(x.shape, BF)
    row = shape_of((own, 8, width), F32)
    return call(
        functools.partial(project_kernel, tile),
        (own, n // tile),
        lens,
        [x, aw, aw, aw, vec],
        [tok] + weights + [once(vec.shape, (0, 0))],
        [sd, sd, sd, row, row],
        (tok, tok, tok, one, one),
        [],
        4 * own * n * width * width,
        "project",
    )


def filter_specs(fw, n_dp, rows, cb, first):
    return [
        pl.BlockSpec((n_dp, rows, cb), lambda *g, i=i: (0, first + i, g[0])) for i in range(4)
    ]


def spectral(values, gating, mixing, lens, table, table_t, fw, first, rows, slots, scale):
    own, n, width = values.shape
    cb = min(256, width)
    n_dp = fw.shape[0]
    tok = pl.BlockSpec((1, n, cb), lambda c, s, *_: (s, 0, c))
    both = pl.BlockSpec((1, 2 * n, cb), lambda c, s, *_: (s, 0, c))
    one = pl.BlockSpec((1, 8, cb), lambda c, s, *_: (s, 0, c))

    def kernel(lens, *refs):
        spectral_kernel(slots, scale, *refs)

    return call(
        kernel,
        (width // cb, own),
        lens,
        [values, gating, mixing, table, table_t] + [fw] * 4,
        [tok, tok, one, once(table.shape, (0, 0)), once(table_t.shape, (0, 0))] + filter_specs(fw, n_dp, rows, cb, first),
        [shape_of((own, 2 * n, width), BF), shape_of(values.shape, BF), shape_of(values.shape, BF)],
        (both, tok, tok),
        [],
        8 * own * n * n * width,
        "spectral",
    )


def feed(x, gated, lens, aw, ffw, vec):
    own, n, width = x.shape
    tile = min(512, n)
    nd, n_tp, _, hid = ffw[0].shape
    r = width // aw.shape[0]
    tok = pl.BlockSpec((1, tile, width), lambda s, t, *_: (s, t, 0))
    wide = pl.BlockSpec((1, n_tp, tile, hid), lambda s, t, *_: (s, 0, t, 0))
    ws = [once(shape, (0, 0, at, 0)) for _, shape, at in ffw[1]]
    big = shape_of((own, n_tp, n, hid), BF)
    return call(
        functools.partial(feed_kernel, tile, n_tp),
        (own, n // tile),
        lens,
        [x, gated, aw] + [w for w, _, _ in ffw[1]] + [vec],
        [tok, tok, once((aw.shape[0], r, width), (0, 3, 0))] + ws + [once(vec.shape, (0, 0))],
        [shape_of(x.shape, F32), shape_of(x.shape, BF), big, big, big, shape_of(x.shape, BF)],
        (tok, tok, wide, wide, wide, tok),
        [],
        2 * own * n * width * (width + 3 * n_tp * hid),
        "feed",
        limit=60,
    )


def feed_back(cot, n2, act, side, hidden, lens, ffw):
    own, n, width = cot.shape
    n_tp, hid = act.shape[1], act.shape[3]
    tile = min(512, n)
    tiles = n // tile
    tok = pl.BlockSpec((1, tile, width), lambda p, u, *_: (u // tiles, lax.rem(u, tiles), 0))
    wide = pl.BlockSpec((1, 1, tile, hid), lambda p, u, *_: (u // tiles, p, lax.rem(u, tiles), 0))
    ws = [
        pl.BlockSpec((shape[0], 1) + shape[2:], lambda p, u, *_, at=at: (0, p, at, 0)) for _, shape, at in ffw[1]
    ]
    d_specs = [pl.BlockSpec((shape[0], 1) + shape[2:], lambda p, u, *_: (0, p, 0, 0)) for _, shape, _ in ffw[1]]
    d_shapes = [shape_of(shape, BF) for _, shape, _ in ffw[1]]
    final = n_tp - 1
    e_spec = pl.BlockSpec(
        (1, tile, width),
        lambda p, u, *_: (jnp.where(p == final, u // tiles, 0), jnp.where(p == final, lax.rem(u, tiles), 0), 0),
    )
    return call(
        functools.partial(feed_back_kernel, tile, tiles),
        (n_tp, own * tiles),
        lens,
        [cot, n2, act, side, hidden] + [w for w, _, _ in ffw[1]],
        [tok, tok, wide, wide, wide] + ws,
        [shape_of(cot.shape, F32)] + d_shapes,
        (e_spec, *d_specs),
        [
            pltpu.VMEM((own * tiles, tile, width), F32),
            pltpu.VMEM((width, hid), F32),
            pltpu.VMEM((width, hid), F32),
            pltpu.VMEM((hid, width), F32),
        ],
        12 * own * n * width * n_tp * hid,
        "feed_back",
        limit=60,
    )


def branch_back(e, middle, cot, gated, gating, conv, lens, aw, vec):
    own, n, width = cot.shape
    tile = min(512, n)
    nd, r = aw.shape[0], width // aw.shape[0]
    tok = pl.BlockSpec((1, tile, width), lambda s, t, *_: (s, t, 0))
    return call(
        functools.partial(branch_back_kernel, tile),
        (own, n // tile),
        lens,
        [e, middle, cot, gated, gating, conv, aw, vec],
        [tok] * 6 + [once((nd, r, width), (0, 3, 0)), once(vec.shape, (0, 0))],
        [
            shape_of(cot.shape, F32),
            shape_of(cot.shape, BF),
            shape_of(cot.shape, BF),
            shape_of((nd, r, width), BF),
            shape_of((8, width), F32),
        ],
        (tok, tok, tok, pl.BlockSpec((nd, r, width), lambda *_: (0, 0, 0)), pl.BlockSpec((8, width), lambda *_: (0, 0))),
        [pltpu.VMEM((width, width), F32)],
        4 * own * n * width * width,
        "branch_back",
    )


def spectral_back(cg, spec, mixing, lens, table, table_t, fw, first, rows, slots, scale):
    own, n, width = cg.shape
    cb = min(256, width)
    n_dp = fw.shape[0]
    tok = pl.BlockSpec((1, n, cb), lambda c, s, *_: (s, 0, c))
    both = pl.BlockSpec((1, 2 * n, cb), lambda c, s, *_: (s, 0, c))
    one = pl.BlockSpec((1, 8, cb), lambda c, s, *_: (s, 0, c))
    return call(
        functools.partial(spectral_back_kernel, slots, scale),
        (width // cb, own),
        lens,
        [cg, spec, mixing, table, table_t] + [fw] * 4,
        [tok, both, one, once(table.shape, (0, 0)), once(table_t.shape, (0, 0))] + filter_specs(fw, n_dp, rows, cb, first),
        [shape_of(cg.shape, BF), shape_of((n_dp, 4 * rows, width), BF), shape_of((own, 8, width), F32)],
        (tok, pl.BlockSpec((n_dp, 4 * rows, cb), lambda c, s, *_: (0, 0, c)), one),
        [pltpu.VMEM((4, n, cb), F32)],
        8 * own * n * n * width,
        "spectral_back",
    )


def input_back(vg, gtg, n1, x, mg, nsum, cgv, lens, aw, d_out, sums, vec):
    own, n, width = x.shape
    tile = min(512, n)
    nd, r = aw.shape[0], width // aw.shape[0]
    tok = pl.BlockSpec((1, tile, width), lambda s, t, *_: (s, t, 0))
    one = pl.BlockSpec((1, 8, width), lambda s, t, *_: (s, 0, 0))
    weights = [once((nd, r, width), (0, g, 0)) for g in range(3)]
    return call(
        functools.partial(input_back_kernel, tile),
        (own, n // tile),
        lens,
        [vg, gtg, n1, x, mg, nsum, cgv, aw, aw, aw, d_out, sums, vec],
        [tok] * 5 + [one] * 2 + weights + [once((nd, r, width), (0, 0, 0)), once((8, width), (0, 0)), once(vec.shape, (0, 0))],
        [shape_of(x.shape, BF), shape_of((nd, 4 * r, width), BF), shape_of((16, width), F32)],
        (tok, pl.BlockSpec((nd, 4 * r, width), lambda *_: (0, 0, 0)), pl.BlockSpec((16, width), lambda *_: (0, 0))),
        [pltpu.VMEM((width, width), F32)] * 3,
        8 * own * n * width * width,
        "input_back",
    )


MESH = pl.DeviceIdType.MESH


def flip(index, step):
    return index + step - 2 * step * ((index // step) % 2)


def bit_orders(n_dp):
    bits = [1 << b for b in range(1, (n_dp - 1).bit_length())]
    return bits, bits[::-1]


def greet(d, z, n_dp, n_tp):
    barrier = pltpu.get_barrier_semaphore()
    count = 0
    step = 1
    while step < n_dp:
        pl.semaphore_signal(barrier, inc=1, device_id=(flip(d, step), z), device_id_type=MESH)
        step *= 2
        count += 1
    for k in range(1, n_tp):
        pl.semaphore_signal(barrier, inc=1, device_id=(d, lax.rem(z + k, n_tp)), device_id_type=MESH)
        count += 1
    pl.semaphore_wait(barrier, count)


def remote(src, dst, send, recv, target):
    copy = pltpu.make_async_remote_copy(
        src_ref=src, dst_ref=dst, send_sem=send, recv_sem=recv, device_id=target, device_id_type=MESH
    )
    copy.start()
    return copy


class Spread:
    def __init__(self, part, order, d, z, send, recv):
        self.part, self.order, self.d, self.z = part, order, d, z
        self.send, self.recv = send, recv
        self.held, self.used, self.flying, self.stage = [d], 0, [], 0
        self.all = []

    def start(self):
        step = self.order[self.stage]
        target = (flip(self.d, step), self.z)
        self.flying = []
        for slot in self.held:
            ref = self.part(slot)
            self.flying.append(remote(ref, ref, self.send.at[self.used], self.recv.at[self.used], target))
            self.used += 1
        self.all += self.flying

    def wait(self):
        step = self.order[self.stage]
        for copy in self.flying:
            copy.wait_recv()
        self.held = self.held + [flip(slot, step) for slot in self.held]
        self.stage += 1

    def drain(self):
        for copy in self.all:
            copy.wait_send()


def chunk_of(rows):
    return next((c for c in (128, 96, 64, 48, 32, 16) if rows % c == 0), rows)


def add_rows(dst, src):
    rows = dst.shape[0]
    size = chunk_of(rows)

    @pl.loop(0, rows // size)
    def _(i):
        at = pl.ds(i * size, size)
        dst[at] = (dst[at].astype(F32) + src[at].astype(F32)).astype(BF)


def lane_place(rows, cols, offset):
    r = lax.broadcasted_iota(jnp.int32, (rows, cols), 0)
    c = lax.broadcasted_iota(jnp.int32, (rows, cols), 1)
    return jnp.where(c - r == offset, 1.0, 0.0).astype(BF)


def gather_kernel(
    n_dp, n_tp, cut, ff_in, a_in, vec_in, x_in, ff_out, a_out, x_out, a_z, a_nat, z_send, z_recv, s_send, s_recv, local
):
    d, z = lax.axis_index("dp"), lax.axis_index("tp")
    rows, ch = a_in.shape
    width = a_nat.shape[1]
    greet(d, z, n_dp, n_tp)
    own_ff = pltpu.make_async_copy(ff_in, ff_out.at[d, z], local.at[0])
    own_ff.start()
    own_a = pltpu.make_async_copy(a_in, a_z.at[z], local.at[1])
    own_a.start()
    za, zf = [], []
    for k in range(1, n_tp):
        target = (d, lax.rem(z + k, n_tp))
        za.append(remote(a_in, a_z.at[z], z_send.at[0, k - 1], z_recv.at[0, k - 1], target))
    for k in range(1, n_tp):
        target = (d, lax.rem(z + k, n_tp))
        zf.append(remote(ff_in, ff_out.at[d, z], z_send.at[1, k - 1], z_recv.at[1, k - 1], target))
    size = x_in.shape[2]
    here = pl.ds(z * size, size)
    own_x = pltpu.make_async_copy(x_in.at[z], x_out.at[:, here], local.at[3])
    own_x.start()
    zx = []
    for k in range(1, n_tp):
        peer = lax.rem(z + k, n_tp)
        zx.append(remote(x_in.at[peer], x_out.at[:, here], z_send.at[2, k - 1], z_recv.at[2, k - 1], (d, peer)))
    own_a.wait()
    for copy in za:
        copy.wait_recv()
    size = chunk_of(rows)

    @pl.loop(0, rows // size)
    def _(i):
        at = pl.ds(i * size, size)
        total = jnp.zeros((size, width), F32)
        for s in range(n_tp):
            total += jnp.dot(a_z[s, at], lane_place(ch, width, s * ch), preferred_element_type=F32)
        a_nat[at] = total.astype(BF)

    a_nat[rows:] = vec_in[...]
    put = pltpu.make_async_copy(a_nat, a_out.at[d], local.at[2])
    put.start()
    put.wait()
    first, second = bit_orders(n_dp)
    half_z = n_tp // 2
    total_rows = a_nat.shape[0]
    sa = [
        Spread(lambda s: a_out.at[s, pl.ds(0, cut)], first + [1], d, z, s_send.at[0], s_recv.at[0]),
        Spread(lambda s: a_out.at[s, pl.ds(cut, total_rows - cut)], second + [1], d, z, s_send.at[1], s_recv.at[1]),
    ]
    sf = [
        Spread(lambda s: ff_out.at[s, pl.ds(0, half_z)], first + [1], d, z, s_send.at[2], s_recv.at[2]),
        Spread(lambda s: ff_out.at[s, pl.ds(half_z, n_tp - half_z)], second + [1], d, z, s_send.at[3], s_recv.at[3]),
    ]
    for p in sa:
        p.start()
    own_ff.wait()
    for copy in zf:
        copy.wait_recv()
    for p in sf:
        p.start()
    for stage in range(len(first) + 1):
        for group in (sa, sf):
            for p in group:
                p.wait()
            if stage < len(first):
                for p in group:
                    p.start()
    for p in sa + sf:
        p.drain()
    own_x.wait()
    for copy in zx:
        copy.wait_recv()
    for copy in za + zf + zx:
        copy.wait_send()


def gather_weights(ff_in, a_in, vec_in, x_in, n_dp, n_tp):
    rows, ch = a_in.shape
    width = vec_in.shape[1]
    total = rows + vec_in.shape[0]
    cut = total // 2 // 16 * 16
    anyspace = pl.BlockSpec(memory_space=pl.ANY)
    vmem = pl.BlockSpec(memory_space=pltpu.VMEM)
    return pl.pallas_call(
        functools.partial(gather_kernel, n_dp, n_tp, cut),
        out_shape=(
            jax.ShapeDtypeStruct((n_dp, n_tp) + ff_in.shape, BF),
            jax.ShapeDtypeStruct((n_dp, total, width), BF),
            jax.ShapeDtypeStruct((x_in.shape[1], n_tp * x_in.shape[2], width), BF),
        ),
        in_specs=[anyspace, anyspace, vmem, anyspace],
        out_specs=(anyspace, anyspace, anyspace),
        scratch_shapes=[
            pltpu.VMEM((n_tp, rows, ch), BF),
            pltpu.VMEM((total, width), BF),
            pltpu.SemaphoreType.DMA((3, n_tp - 1)),
            pltpu.SemaphoreType.DMA((3, n_tp - 1)),
            pltpu.SemaphoreType.DMA((4, n_dp - 1)),
            pltpu.SemaphoreType.DMA((4, n_dp - 1)),
            pltpu.SemaphoreType.DMA((4,)),
        ],
        compiler_params=pltpu.CompilerParams(
            collective_id=0, has_side_effects=True, vmem_limit_bytes=48 * 1024 * 1024
        ),
        name="gather_weights",
    )(ff_in, a_in, vec_in, x_in)


def scatter_kernel(
    n_dp, n_tp, cut, g0, g1, g2, a0, a1, v_in, x_in, ff_out, a_out, v_out, x_out,
    ff_mine, a_mine, ff_core, a_core, ff_two, a_two, a_cols, ff_z, a_zbuf, ff_sum, v_got,
    load, core_send, core_recv, x_send, x_recv, z_send, z_recv, s_send, s_recv, v_send, v_recv, local,
):
    d, z = lax.axis_index("dp"), lax.axis_index("tp")
    width = a0.shape[2]
    rows = a0.shape[1] + a1.shape[1]
    ch = a_out.shape[1]
    vec = g0.shape[2]
    half = n_dp // 2
    half_z = n_tp // 2
    side = d % 2
    own = d // 2
    greet(d, z, n_dp, n_tp)
    v_out[...] = v_in[...]
    vs = []

    def v_start(i, target, sem):
        vs.append(remote(v_out, v_got.at[i], v_send.at[sem], v_recv.at[sem], target))

    def v_finish(i):
        vs[-1].wait()
        v_out[...] += v_got[i]

    other = (flip(d, 1), z)
    f_core, a_core_copies, f_load, a_load = [], [], [], []
    for i in range(half):
        for g, src in enumerate((g0, g1, g2)):
            f_core.append(
                remote(src.at[2 * i + 1 - side], ff_core.at[i, g], core_send.at[g, i], core_recv.at[g, i], other)
            )
            copy = pltpu.make_async_copy(src.at[2 * i + side], ff_mine.at[i, g], load.at[g, i])
            copy.start()
            f_load.append(copy)
    for i in range(half):
        at = 0
        for g, src in enumerate((a0, a1)):
            part = pl.ds(at, src.shape[1])
            at += src.shape[1]
            a_core_copies.append(
                remote(src.at[2 * i + 1 - side], a_core.at[i, part], core_send.at[3 + g, i], core_recv.at[3 + g, i], other)
            )
            copy = pltpu.make_async_copy(src.at[2 * i + side], a_mine.at[i, part], load.at[3 + g, i])
            copy.start()
            a_load.append(copy)
    v_start(0, other, 0)
    slot = x_out.shape[2]
    own_x = pltpu.make_async_copy(x_in.at[:, pl.ds(z * slot, slot)], x_out.at[z], local.at[1])
    own_x.start()
    zx = []
    for k in range(1, n_tp):
        peer = lax.rem(z + k, n_tp)
        zx.append(
            remote(x_in.at[:, pl.ds(peer * slot, slot)], x_out.at[z], z_send.at[3, k - 1], z_recv.at[3, k - 1], (d, peer))
        )

    first, second = bit_orders(n_dp)
    orders = ([s // 2 for s in first[::-1]], [s // 2 for s in second[::-1]])
    n_stage = len(orders[0])

    def entries(order, t):
        masks = [0]
        for step in order[t:]:
            masks = masks + [m + step for m in masks]
        return masks

    def at(mask):
        index = own
        step = 1
        while step < half:
            if mask & step:
                index = flip(index, step)
            step *= 2
        return index

    flying = {}
    base = {}
    all_x = []

    def begin(name, h, t, mine, two, part):
        step = orders[h][t]
        target = (flip(d, 2 * step), z)
        first_slot = base.get((name, h), 0)
        copies = []
        for j, m in enumerate(entries(orders[h], t + 1)):
            k = first_slot + j
            copies.append(
                (
                    m,
                    k,
                    remote(part(mine, at(m + step)), part(two, k), x_send.at[name, h, k], x_recv.at[name, h, k], target),
                )
            )
        base[name, h] = first_slot + len(copies)
        flying[name, h] = copies

    def finish(name, h, mine, two, part, add):
        for m, k, copy in flying[name, h]:
            copy.wait()
            add(part(mine, at(m)), part(two, k))

    def ff_part(h):
        lo, size = (0, half_z) if h == 0 else (half_z, n_tp - half_z)
        return lambda ref, e: ref.at[e, :, pl.ds(lo, size)]

    def a_part(h):
        lo, size = (0, cut) if h == 0 else (cut, rows - cut)
        return lambda ref, e: ref.at[e, pl.ds(lo, size)]

    def add_deep(dst, src):
        for g in range(dst.shape[0]):
            for s in range(dst.shape[1]):
                add_rows(dst.at[g, s], src.at[g, s])

    for i in range(half):
        for g in range(3):
            f_load[3 * i + g].wait()
            f_core[3 * i + g].wait_recv()
        add_deep(ff_mine.at[i], ff_core.at[i])
    for h in range(2):
        begin(0, h, 0, ff_mine, ff_two, ff_part(h))
    v_finish(0)
    for copy in a_load:
        copy.wait()
    for copy in a_core_copies:
        copy.wait_recv()
    for i in range(half):
        add_rows(a_mine.at[i], a_core.at[i])
    for i, step in enumerate(first):
        v_start(i + 1, (flip(d, step), z), i + 1)
        v_finish(i + 1)
    for t in range(n_stage):
        for h in range(2):
            finish(0, h, ff_mine, ff_two, ff_part(h), add_deep)
            if t + 1 < n_stage:
                begin(0, h, t + 1, ff_mine, ff_two, ff_part(h))
        if t == 0:
            for h in range(2):
                begin(1, h, 0, a_mine, a_two, a_part(h))
    zf, za, zv = [], [], []
    for k in range(1, n_tp):
        peer = lax.rem(z + k, n_tp)
        zf.append(remote(ff_mine.at[own, :, peer], ff_z.at[k - 1], z_send.at[0, k - 1], z_recv.at[0, k - 1], (d, peer)))
        zv.append(
            remote(v_out, v_got.at[n_stage + k], z_send.at[2, k - 1], z_recv.at[2, k - 1], (d, peer))
        )
    for t in range(n_stage):
        for h in range(2):
            finish(1, h, a_mine, a_two, a_part(h), add_rows)
            if t + 1 < n_stage:
                begin(1, h, t + 1, a_mine, a_two, a_part(h))
    size = chunk_of(rows)

    @pl.loop(0, rows // size)
    def _(i):
        here = pl.ds(i * size, size)
        block = a_mine[own, here]
        for s in range(n_tp):
            a_cols[s, here] = mm_nt(block, lane_place(ch, width, s * ch)).astype(BF)

    for k in range(1, n_tp):
        peer = lax.rem(z + k, n_tp)
        za.append(remote(a_cols.at[peer], a_zbuf.at[k - 1], z_send.at[1, k - 1], z_recv.at[1, k - 1], (d, peer)))
    for copy in zf:
        copy.wait_recv()
    f_size = chunk_of(vec)
    for g in range(3):

        @pl.loop(0, vec // f_size)
        def _(i):
            here = pl.ds(i * f_size, f_size)
            total = ff_mine[own, g, z, here].astype(F32)
            for k in range(1, n_tp):
                total += ff_z[k - 1, g, here].astype(F32)
            ff_sum[g, here] = total.astype(BF)

    put = pltpu.make_async_copy(ff_sum, ff_out.at[d], local.at[0])
    put.start()
    put.wait()
    one, two = bit_orders(n_dp)
    pieces = [(0, 0, vec, one), (1, 0, vec, two)]
    if vec % 32 == 0:
        pieces += [(2, 0, vec // 2, one), (2, vec // 2, vec // 2, two)]
    else:
        pieces += [(2, 0, vec, one)]
    sf = [
        Spread(lambda s, g=g, lo=lo, n=n: ff_out.at[s, g, pl.ds(lo, n)], order + [1], d, z, s_send.at[i], s_recv.at[i])
        for i, (g, lo, n, order) in enumerate(pieces)
    ]
    for p in sf:
        p.start()
    for stage in range(len(one) + 1):
        for p in sf:
            p.wait()
            if stage < len(one):
                p.start()
    for copy in zv:
        copy.wait()
    for k in range(1, n_tp):
        v_out[...] += v_got[n_stage + k]
    for copy in za:
        copy.wait_recv()

    @pl.loop(0, rows // size)
    def _(i):
        here = pl.ds(i * size, size)
        total = a_cols[z, here].astype(F32)
        for k in range(1, n_tp):
            total += a_zbuf[k - 1, here].astype(F32)
        a_out[here] = total

    own_x.wait()
    for copy in zx:
        copy.wait_recv()
    for copy in f_core + a_core_copies + zf + za + zx:
        copy.wait_send()
    for p in sf:
        p.drain()


def scatter_grads(ff, a0, a1, vectors, x_in, n_dp, n_tp):
    width = a0.shape[2]
    rows = a0.shape[1] + a1.shape[1]
    vec, hid = ff[0].shape[2:]
    ch = width // n_tp
    cut = rows // 2 // 16 * 16
    half = n_dp // 2
    stages = half.bit_length() - 1
    anyspace = pl.BlockSpec(memory_space=pl.ANY)
    vmem = pl.BlockSpec(memory_space=pltpu.VMEM)
    dma = pltpu.SemaphoreType.DMA
    return pl.pallas_call(
        functools.partial(scatter_kernel, n_dp, n_tp, cut),
        out_shape=(
            jax.ShapeDtypeStruct((n_dp, 3, vec, hid), BF),
            jax.ShapeDtypeStruct((rows, ch), F32),
            jax.ShapeDtypeStruct(vectors.shape, F32),
            jax.ShapeDtypeStruct((n_tp, x_in.shape[0], x_in.shape[1] // n_tp, width), BF),
        ),
        in_specs=[anyspace] * 5 + [vmem, anyspace],
        out_specs=(anyspace, vmem, vmem, anyspace),
        scratch_shapes=[
            pltpu.VMEM((half, 3, n_tp, vec, hid), BF),
            pltpu.VMEM((half, rows, width), BF),
            pltpu.VMEM((half, 3, n_tp, vec, hid), BF),
            pltpu.VMEM((half, rows, width), BF),
            pltpu.VMEM((half - 1, 3, n_tp, vec, hid), BF),
            pltpu.VMEM((half - 1, rows, width), BF),
            pltpu.VMEM((n_tp, rows, ch), BF),
            pltpu.VMEM((n_tp - 1, 3, vec, hid), BF),
            pltpu.VMEM((n_tp - 1, rows, ch), BF),
            pltpu.VMEM((3, vec, hid), BF),
            pltpu.VMEM((stages + n_tp,) + vectors.shape, F32),
            dma((5, half)),
            dma((5, half)),
            dma((5, half)),
            dma((2, 2, half)),
            dma((2, 2, half)),
            dma((4, n_tp - 1)),
            dma((4, n_tp - 1)),
            dma((4, n_dp - 1)),
            dma((4, n_dp - 1)),
            dma((stages + 1,)),
            dma((stages + 1,)),
            dma((2,)),
        ],
        compiler_params=pltpu.CompilerParams(
            collective_id=1, has_side_effects=True, vmem_limit_bytes=60 * 1024 * 1024
        ),
        name="scatter_grads",
    )(*ff, a0, a1, vectors, x_in)


def body(
    tokens,
    lengths,
    cotangent,
    norm1_gain,
    norm1_bias,
    in_weight,
    in_bias,
    filter_base,
    filter_mod,
    out_weight,
    out_bias,
    norm2_gain,
    norm2_bias,
    gate_weight,
    up_weight,
    down_weight,
    down_bias,
):
    micro, local, group, width = tokens.shape
    n_tp = lax.axis_size("tp")
    n_dp = lax.axis_size("dp")
    z = lax.axis_index("tp")
    d = lax.axis_index("dp")
    slot_len = local * n_tp
    own = micro * group // n_tp
    per_micro = min(group, own)
    ch = in_weight.shape[2]
    vec = width // n_dp
    hid = gate_weight.shape[1]
    table = jnp.asarray(packed_table(slot_len))
    table_t = jnp.asarray(np.ascontiguousarray(packed_table(slot_len).T))
    scale = 0.5 / slot_len

    rows = slot_len // n_dp
    last = n_dp - 1
    upper = d > last - d
    filters = jnp.stack([filter_base, filter_mod])
    across = [(i, (n_dp - i) % n_dp) for i in range(n_dp) if i % (n_dp // 2)] + [(0, n_dp // 2), (n_dp // 2, 0)]
    got = lax.ppermute(filters[:, :, rows:], "dp", [(i, last - i) for i in range(n_dp)])
    got_edge = lax.ppermute(filters[:, :, :1], "dp", across)
    direct = jnp.where(upper, got, filters[:, :, :rows]).astype(F32)
    mirror_lower = jnp.concatenate([got[:, :, 1:], got_edge], axis=2)
    mirror_upper = filters[:, :, 1 : rows + 1]
    mirror = jnp.flip(jnp.where(upper, mirror_upper, mirror_lower), 2).astype(F32)
    nyquist = got_edge[:, 0, 0].astype(F32)
    edge = ((jnp.arange(rows) == 0) & (d == 0))[None, :, None]
    half_real = jnp.where(edge, direct[:, 0], direct[:, 0] + mirror[:, 0])
    half_imag = jnp.where(edge, nyquist[:, None], direct[:, 1] - mirror[:, 1])
    half = jnp.stack([half_real, half_imag], 1).astype(BF).reshape(4 * rows, ch)
    slice_of = [2 * i if 2 * i < n_dp else 2 * (last - i) + 1 for i in range(n_dp)]

    a_in = jnp.concatenate([in_weight.transpose(1, 0, 2).reshape(3 * vec, ch), out_weight.T, half])
    vectors = jnp.stack([norm1_gain, norm1_bias, norm2_gain, norm2_bias, out_bias, down_bias])
    vectors = jnp.concatenate([vectors, in_bias])
    vectors = jnp.pad(vectors, ((0, 16 - 9), (0, width - vec)))
    share = hid // n_dp
    ff_in = jnp.concatenate(
        [
            lax.dynamic_slice_in_dim(gate_weight, d * vec, vec, 0),
            lax.dynamic_slice_in_dim(up_weight, d * vec, vec, 0),
            lax.dynamic_slice_in_dim(down_weight, d * share, share, 0).reshape(vec, hid),
        ]
    )
    x_in = tokens.transpose(0, 2, 1, 3).reshape(n_tp, own, local, width)
    ffw, aw, x_own = gather_weights(ff_in, a_in, vectors, x_in, n_dp, n_tp)
    cotangent, _ = lax.optimization_barrier((cotangent, aw))
    vectors = aw[:, 4 * vec + 4 * rows :, :vec].astype(F32).transpose(1, 0, 2).reshape(16, width)
    slots = [slice_of.index(k) for k in range(n_dp)]
    direct = vec % 16 == 0 and hid == width
    if direct:
        ws = [(ffw, (n_dp, n_tp, vec, hid), g) for g in range(3)]
        a_view = aw
    else:
        natural = [
            ffw[:, :, g * vec : (g + 1) * vec].transpose(1, 0, 2, 3).reshape(n_tp, width, hid) for g in range(2)
        ]
        natural.append(
            ffw[:, :, 2 * vec :].reshape(n_dp, n_tp, share, width).transpose(1, 0, 2, 3).reshape(n_tp, hid, width)
        )
        ws = [(w[None], (1,) + w.shape, 0) for w in natural]
        a_view = aw[:, : 4 * vec].reshape(n_dp, 4, vec, width).transpose(1, 0, 2, 3).reshape(1, 4 * width, width)
    feed_weights = (ws[0][0], ws)

    def to_owner(x):
        pieces = x.transpose(0, 2, 1, 3).reshape(n_tp, own, local, width)
        whole = jnp.zeros((own, slot_len, width), x.dtype)
        for source, block in exchange(pieces, z, n_tp):
            whole = lax.dynamic_update_slice(whole, block, (0, source * local, 0))
        return whole

    def to_slots(x):
        pieces = x.reshape(own, n_tp, local, width).transpose(1, 0, 2, 3)
        whole = jnp.zeros((n_tp, own, local, width), x.dtype)
        for source, block in exchange(pieces, z, n_tp):
            whole = lax.dynamic_update_slice(whole, block[None], (source, 0, 0, 0))
        return whole.reshape(micro, group, local, width).transpose(0, 2, 1, 3)

    c_own = to_owner(cotangent)
    flat_len = lax.dynamic_slice_in_dim(lengths.reshape(-1), z * own, own, 0)
    first = 4 * vec // rows
    n1, values, gating, nsum, mixing = project(x_own, flat_len, a_view, vectors)
    spec, conv, gated = spectral(values, gating, mixing, flat_len, table, table_t, aw, first, rows, slots, scale)
    middle, n2, act, side, hidden, out = feed(x_own, gated, flat_len, a_view, feed_weights, vectors)
    layer_out = to_slots(out)
    e, *d_ff = feed_back(c_own, n2, act, side, hidden, flat_len, feed_weights)
    mg, cg, gtg, d_out, sums = branch_back(e, middle, c_own, gated, gating, conv, flat_len, a_view, vectors)
    layer_out, cg = lax.optimization_barrier((layer_out, cg))
    vg, d_filter, cgv = spectral_back(cg, spec, mixing, flat_len, table, table_t, aw, first, rows, slots, scale)
    ig, d_first, sums = input_back(vg, gtg, n1, x_own, mg, nsum, cgv, flat_len, a_view, d_out, sums, vectors)
    if not direct:
        d_ff = [
            g[0].reshape(n_tp, n_dp, vec, hid).transpose(1, 0, 2, 3) for g in d_ff[:2]
        ] + [d_ff[2][0].reshape(n_tp, n_dp, vec, hid).transpose(1, 0, 2, 3)]
        d_first = d_first.reshape(4, n_dp, vec, width).transpose(1, 0, 2, 3).reshape(n_dp, 4 * vec, width)
    ffg, ag, vecs, input_grad = scatter_grads(d_ff, d_first, d_filter, sums, ig, n_dp, n_tp)
    input_grad = input_grad.reshape(micro, group, local, width).transpose(0, 2, 1, 3)
    gate_grad = ffg[:, 0].reshape(width, hid).astype(F32)
    up_grad = ffg[:, 1].reshape(width, hid).astype(F32)
    down_grad = ffg[:, 2].reshape(hid, width).astype(F32)
    in_grad = ag[: 3 * vec].reshape(3, vec, ch).transpose(1, 0, 2)
    out_grad = ag[3 * vec : 4 * vec].T
    fgrad = ag[4 * vec :].astype(BF).reshape(2, 2, rows, ch)
    other = lax.ppermute(fgrad, "dp", [(i, last - i) for i in range(n_dp)])
    low_slice = jnp.where(upper, other, fgrad)
    high_slice = jnp.where(upper, fgrad, other)
    both = jnp.concatenate([low_slice, high_slice], axis=2)
    follow = lax.ppermute(fgrad[:, :, :1], "dp", across)
    zero = jnp.zeros_like(follow[:, 0])
    follow = jnp.where(d == n_dp // 2, jnp.stack([follow[:, 1], zero], 1), follow)
    mirrored = jnp.flip(jnp.concatenate([both[:, :, 1:], follow], axis=2), 2)
    mirrored = jnp.stack([mirrored[:, 0], -mirrored[:, 1]], 1)
    plain = jnp.stack(
        [both[:, 0], jnp.where((d == 0) & (jnp.arange(2 * rows) == 0)[None, :, None], 0.0, both[:, 1].astype(F32)).astype(BF)], 1
    )
    full = jnp.where(upper, mirrored, plain).astype(F32)

    piece = width // (n_dp * n_tp)
    vecs = lax.dynamic_slice_in_dim(vecs, (d * n_tp + z) * piece, piece, 1)
    return (
        layer_out,
        input_grad,
        vecs[0],
        vecs[1],
        in_grad,
        vecs[6:9],
        full[0],
        full[1],
        out_grad,
        vecs[4],
        vecs[2],
        vecs[3],
        gate_grad,
        up_grad,
        down_grad,
        vecs[5],
    )


def solution(mesh):
    in_specs = (
        P(None, "tp", "dp", None),
        P(None, "dp"),
        P(None, "tp", "dp", None),
        P("dp"),
        P("dp"),
        P("dp", None, "tp"),
        P(None, "dp"),
        P(None, "dp", "tp"),
        P(None, "dp", "tp"),
        P("tp", "dp"),
        P("dp"),
        P("dp"),
        P("dp"),
        P(None, "tp"),
        P(None, "tp"),
        P("tp", None),
        P("dp"),
    )
    out_specs = (
        P(None, "tp", "dp", None),
        P(None, "tp", "dp", None),
        P(("dp", "tp")),
        P(("dp", "tp")),
        P("dp", None, "tp"),
        P(None, ("dp", "tp")),
        P(None, "dp", "tp"),
        P(None, "dp", "tp"),
        P("tp", "dp"),
        P(("dp", "tp")),
        P(("dp", "tp")),
        P(("dp", "tp")),
        P(None, "tp"),
        P(None, "tp"),
        P("tp", None),
        P(("dp", "tp")),
    )
    return jax.shard_map(body, mesh=mesh, in_specs=in_specs, out_specs=out_specs, check_vma=False)
```

time: 2400 us -> 760 us (0.32)
  waiting for transfers between devices: 1500 us -> 0.37 us
  Pallas kernels: 0 us -> 651 us
  matrix products: 408 us -> 0 us
  other arithmetic: 279 us -> 9.53 us
  blocking collectives: 105 us -> 0 us
    reduce_scatter x19 -> x0, waiting for transfers between devices: 849 us -> none  [the longest x4 242 us: body(): lax.psum_scatter(jnp.einsum('tbge,dge->tbd', projected_grad, in_back, pre...]
    pallas_call x0 -> x9, Pallas kernels: none -> 651 us  [the longest x7 279 us: call(): pl.pallas_call(kernel, grid_spec=spec, out_shape=tuple(outs), compiler_pa...]
    all_gather x18 -> x0, waiting for transfers between devices: 643 us -> none  [the longest x4 219 us: body(): rows_full = lax.all_gather(rows_low, 'tp', axis=0, tiled=True)]
    dot_general x76 -> x0, matrix products: 408 us -> none  [the longest x4 42.6 us: body(): jnp.einsum('tbd,fd->tbf', grad_full, down_weight, preferred_element_type=...]
    another operation x20 -> x5, other arithmetic: 121 us -> 2.19 us  [the longest x2 2.01 us: body(): filters = jnp.stack([filter_base, filter_mod])]
    reduce_sum x34 -> x0, other arithmetic: 101 us -> none  [the longest x8 31.3 us: layer_norm(): return centred * lax.rsqrt(spread + EPSILON) * weight_gain + weight_shift]
    unnamed x2 -> x0, blocking collectives: 73 us -> none
    unnamed x643 -> x37, local copies, waits for them, and re-layouts: 62.4 us -> 14.7 us
  transfers between devices with their start and end apart: 39 -> 10, of which waited for: 31 -> 1; matrix products, arithmetic and copies ran while one was open for 29% -> 7% of each run, Pallas kernels for 0% -> 29%
where the time goes in v1:
time: 760 us; the launch traced here: 745 us
  Pallas kernels  651 us (86%)
  local copies, waits for them, and re-layouts  60.6 us (8%)
  starting transfers between devices  22.4 us (3%)
  other arithmetic  9.53 us (1%)
    pallas_call x7, Pallas kernels, call(): pl.pallas_call(kernel, grid_spec=spec, out_shape=tuple(outs), compiler_pa...  279 us
    pallas_call x1, Pallas kernels, gather_weights(): pl.pallas_call(functools.partial(gather_kernel, n_dp, n_tp, cut), out_sha...  208 us
    pallas_call x1, Pallas kernels, scatter_grads(): pl.pallas_call(functools.partial(scatter_kernel, n_dp, n_tp, cut), out_sh...  164 us
    ppermute x6, starting transfers between devices, shift(): return lax.ppermute(x, axis, [(i, (i + step) % n) for i in range(n)])  17 us
  transfers between devices with their start and end apart: 10, of which 1 were waited for; matrix products, arithmetic and copies ran while one was open for 7% of the time, Pallas kernels for 29%

profile of v1, /device:TPU:0, one launch (start us, length us, event | category | flops | bytes accessed | tf_op | source)
XLA Modules:
  0.0 745.0 jit_solution(12467511373072775788)
XLA Ops:
  1.7 3.4 collective-permute-start
  8.5 4.0 copy.78
  17.2 208.3 %gather_weights.1 = (bf16[8,4,288,768]{3,2,1,0:T(8,128)(2,1)}, bf16[8,912,768]{2,1,0:T(8,128)(2,1)}, bf16[2,1024,768]{2,1,0:T(8,128)(2,1)S(1)}) custom-call(bf16[288,768]{1,0:T(8,128)(2,1)S(1)} %pad_maximum_fusion.1.ff_in, bf16[896,192]{1,0:T(8,128)(2,1)S(1)} %pad_maximum_fusion.a_in, bf16[16,768]{1,0:T(8,128)(2,1)S(1)} %pad.5.vec_in, ...), custom_call_target="tpu_custom_call" | custom-call | tf_op jit(solution)/shard_map/gather_weights/pallas_call | solution.py:703
  228.6 2.3 copy.63
  234.1 10.0 %collective-permute-start.5 = (bf16[2,256,768]{2,1,0:T(8,128)(2,1)}, bf16[2,256,768]{2,1,0:T(8,128)(2,1)}, u32[]{:S(2)}, u32[]{:S(2)}) collective-permute-start(bf16[2,256,768]{2,1,0:T(8,128)(2,1)} %get-tuple-element.131), channel_id=1, source_target_pairs={{0,1},{1,2},{2,3},{3,0},{4,5},{5,6},{6,7},{7,4},{8,9},{9,10},{10,1... | collective-permute-start | bytes 2359304 | tf_op jit(solution)/shard_map/ppermute | solution.py:31
  244.1 2.2 collective-permute-start.6
  246.5 12.5 %project.1 = (bf16[2,1024,768]{2,1,0:T(8,128)(2,1)}, bf16[2,1024,768]{2,1,0:T(8,128)(2,1)}, bf16[2,1024,768]{2,1,0:T(8,128)(2,1)}, f32[2,8,768]{2,1,0:T(8,128)}, f32[2,8,768]{2,1,0:T(8,128)}) custom-call(s32[2]{0:T(128)} %dynamic_slice.34.lens, bf16[2,1024,768]{2,1,0:T(8,128)(2,1)} %copy-done.2, ...), custom_call_target="tpu_custom_call" | custom-call | flops 4831838208 | bytes 46350336 | tf_op jit(solution)/shard_map/project/pallas_call | solution.py:334
  259.0 33.5 %spectral.1 = (bf16[2,2048,768]{2,1,0:T(8,128)(2,1)}, bf16[2,1024,768]{2,1,0:T(8,128)(2,1)}, bf16[2,1024,768]{2,1,0:T(8,128)(2,1)}) custom-call(s32[2]{0:T(128)} %dynamic_slice.34.lens, bf16[2,1024,768]{2,1,0:T(8,128)(2,1)} %get-tuple-element.57.refs_0_, bf16[2,1024,768]{2,1,0:T(8,128)(2,1)} %get-tuple-element.58.refs_1_.gating, ...), custom_call_target="tpu_custom_call" | custom-call | flops 12884901888 | bytes 72138752 | tf_op jit(solution)/shard_map/spectral/pallas_call | solution.py:334
  292.5 52.2 %feed.1 = (f32[2,1024,768]{2,1,0:T(8,128)}, bf16[2,1024,768]{2,1,0:T(8,128)(2,1)}, bf16[2,4,1024,768]{3,2,1,0:T(8,128)(2,1)}, bf16[2,4,1024,768]{3,2,1,0:T(8,128...) custom-call(s32[2]{0:T(128)} %dynamic_slice.34.lens, bf16[2,1024,768]{2,1,0:T(8,128)(2,1)} %copy-done.2, ...), custom_call_target="tpu_custom_call" | custom-call | flops 31406948352 | bytes 110346240 | tf_op jit(solution)/shard_map/feed/pallas_call | solution.py:334
  344.7 2.1 constant_dynamic-slice_fusion.1
  353.6 1.9 broadcast_in_dim.59
  355.5 2.1 bitcast_dynamic-update-slice_fusion
  357.6 3.3 broadcast_in_dim.53
  362.6 2.0 collective-permute-start.4
  364.6 2.1 constant_dynamic-update-slice_fusion.2
  368.5 97.3 %feed_back.1 = (f32[2,1024,768]{2,1,0:T(8,128)}, bf16[8,4,96,768]{3,2,1,0:T(8,128)(2,1)}, bf16[8,4,96,768]{3,2,1,0:T(8,128)(2,1)}, bf16[8,4,96,768]{3,2,1,0:T(8,128)(2,1)}) custom-call(s32[2]{0:T(128)} %dynamic_slice.34.lens, bf16[2,1024,768]{2,1,0:T(8,128)(2,1)} %constant_dynamic-update-slice_fusion.cot, bf16[2,1024,768]{2,1,0:T(8,128)(2,1)} %get-tuple-element.64.n2, ...), custom_call_target="tpu_custom_call" | custom-call | flops 57982058496 | bytes 106954752 | tf_op jit(solution)/shard_map/feed_back/pallas_call | solution.py:334
  465.8 2.6 bitcast_dynamic-update-slice_fusion.3
  468.4 2.6 bitcast_dynamic-update-slice_fusion.2
  470.9 18.8 %branch_back.1 = (f32[2,1024,768]{2,1,0:T(8,128)}, bf16[2,1024,768]{2,1,0:T(8,128)(2,1)}, bf16[2,1024,768]{2,1,0:T(8,128)(2,1)}, bf16[8,96,768]{2,1,0:T(8,128)(2,1)}, f32[8,768]{1,0:T(8,128)}) custom-call(s32[2]{0:T(128)} %dynamic_slice.34.lens, f32[2,1024,768]{2,1,0:T(8,128)} %get-tuple-element.68.e, f32[2,1024,768]{2,1,0:T(8,128)} %get-tuple-element.69.middle, ...), custom_call_target="tpu_custom_call" | custom-call | flops 4831838208 | bytes 50208768 | tf_op jit(solution)/shard_map/branch_back/pallas_call | solution.py:334
  491.1 40.4 %spectral_back.1 = (bf16[2,1024,768]{2,1,0:T(8,128)(2,1)}, bf16[8,512,768]{2,1,0:T(8,128)(2,1)}, f32[2,8,768]{2,1,0:T(8,128)}) custom-call(s32[2]{0:T(128)} %dynamic_slice.34.lens, bf16[2,1024,768]{2,1,0:T(8,128)(2,1)} %get-tuple-element.76.cg, bf16[2,2048,768]{2,1,0:T(8,128)(2,1)} %get-tuple-element.77.spec, f32[2,8,768]{2,1,0:T(8,128)} %get-tuple-element.59.refs_2_.mixing, ...), custom_call_target="tpu_custom_call" | custom-call | flops 12884901888 | bytes 72187904 | tf_op jit(solution)/shard_map/spectral_back/pallas_call | solution.py:334
  531.6 24.1 %input_back.1 = (bf16[2,1024,768]{2,1,0:T(8,128)(2,1)}, bf16[8,384,768]{2,1,0:T(8,128)(2,1)}, f32[16,768]{1,0:T(8,128)}) custom-call(s32[2]{0:T(128)} %dynamic_slice.34.lens, bf16[2,1024,768]{2,1,0:T(8,128)(2,1)} %get-tuple-element.78.vg, bf16[2,1024,768]{2,1,0:T(8,128)(2,1)} %get-tuple-element.79.gtg, bf16[2,1024,768]{2,1,0:T(8,128)(2,1)} %get-tuple-element.80.n1, ...), custom_call_target="tpu_custom_call" | custom-call | flops 9663676416 | bytes 61759488 | tf_op jit(solution)/shard_map/input_back/pallas_call | solution.py:334
  555.7 163.7 %scatter_grads.1 = (bf16[8,3,96,768]{3,2,1,0:T(8,128)(2,1)}, f32[896,192]{1,0:T(8,128)}, f32[16,768]{1,0:T(8,128)}, bf16[4,2,256,768]{3,2,1,0:T(8,128)(2,1)}) custom-call(bf16[8,4,96,768]{3,2,1,0:T(8,128)(2,1)} %get-tuple-element.73.g0, bf16[8,4,96,768]{3,2,1,0:T(8,128)(2,1)} %get-tuple-element.74.g1, bf16[8,4,96,768]{3,2,1,0:T(8,128)(2,1)} %get-tuple-element.75.g2, ...), custom_call_target="tpu_custom_call" | custom-call | tf_op jit(solution)/shard_map/scatter_grads/pallas_call | solution.py:960
  723.0 2.2 fusion.14
  733.4 4.9 copy.71
  (104 shorter events, 45.2 us)
Async XLA Ops:
  0.6 11.9 %copy-start = (bf16[768,768]{1,0:T(8,128)(2,1)S(1)}, bf16[768,768]{1,0:T(8,128)(2,1)}, u32[]{:S(2)}) copy-start(bf16[768,768]{1,0:T(8,128)(2,1)} %param.32) | copy-start | bytes 3538948
  1.7 13.4 %collective-permute-start = (bf16[2,2,128,192]{2,3,1,0:T(8,128)(2,1)S(1)}, bf16[2,2,128,192]{2,3,1,0:T(8,128)(2,1)S(1)}, u32[]{:S(2)}, u32[]{:S(2)}) collective-permute-start(bf16[2,2,128,192]{2,3,1,0:T(8,128)(2,1)S(1)} %fusion.7), channel_id=1, source_target_pairs={{0,28},{4,24},{8,20},{12,16},{16,12},{20,8},{24,4},{28,0},{1,29},{... | collective-permute-start | bytes 589832 | tf_op jit(solution)/shard_map/ppermute | solution.py:1041
  6.1 8.9 %collective-permute-start.1 = (bf16[2,2,1,192]{2,3,1,0:T(8,128)(2,1)S(1)}, bf16[2,2,1,192]{2,3,1,0:T(8,128)(2,1)S(1)}, u32[]{:S(2)}, u32[]{:S(2)}) collective-permute-start(bf16[2,2,1,192]{2,3,1,0:T(8,128)(2,1)S(1)} %pad_maximum_fusion.4), channel_id=1, source_target_pairs={{4,28},{8,24},{12,20},{20,12},{24,8},{28,4},{0,16},{16,0},{5,29},{... | collective-permute-start | bytes 4616 | tf_op jit(solution)/shard_map/ppermute | solution.py:1042
  8.4 6.4 copy-start.8
  8.4 6.4 copy-start.9
  8.4 6.3 copy-start.10
  8.4 6.3 copy-start.11
  8.5 6.3 copy-start.12
  8.5 6.3 copy-start.13
  8.5 6.3 copy-start.14
  8.5 6.8 copy-start.5
  8.5 6.8 copy-start.6
  12.6 4.5 copy-start.7
  234.1 128.5 %collective-permute-start.5 = (bf16[2,256,768]{2,1,0:T(8,128)(2,1)}, bf16[2,256,768]{2,1,0:T(8,128)(2,1)}, u32[]{:S(2)}, u32[]{:S(2)}) collective-permute-start(bf16[2,256,768]{2,1,0:T(8,128)(2,1)} %get-tuple-element.131), channel_id=1, source_target_pairs={{0,1},{1,2},{2,3},{3,0},{4,5},{5,6},{6,7},{7,4},{8,9},{9,10},{10,1... | collective-permute-start | bytes 2359304 | tf_op jit(solution)/shard_map/ppermute | solution.py:31
  244.1 122.5 %collective-permute-start.6 = (bf16[2,256,768]{2,1,0:T(8,128)(2,1)}, bf16[2,256,768]{2,1,0:T(8,128)(2,1)S(1)}, u32[]{:S(2)}, u32[]{:S(2)}) collective-permute-start(bf16[2,256,768]{2,1,0:T(8,128)(2,1)} %get-tuple-element.130), channel_id=1, source_target_pairs={{0,2},{1,3},{2,0},{3,1},{4,6},{5,7},{6,4},{7,5},{8,10},{9,11},{10,... | collective-permute-start | bytes 2359304 | tf_op jit(solution)/shard_map/ppermute | solution.py:31
  246.3 121.3 %collective-permute-start.7 = (bf16[2,256,768]{2,1,0:T(8,128)(2,1)}, bf16[2,256,768]{2,1,0:T(8,128)(2,1)S(1)}, u32[]{:S(2)}, u32[]{:S(2)}) collective-permute-start(bf16[2,256,768]{2,1,0:T(8,128)(2,1)} %get-tuple-element.129), channel_id=1, source_target_pairs={{0,3},{1,0},{2,1},{3,2},{4,7},{5,4},{6,5},{7,6},{8,11},{9,8},{10,9... | collective-permute-start | bytes 2359304 | tf_op jit(solution)/shard_map/ppermute | solution.py:31
  348.5 117.3 %collective-permute-start.2 = (bf16[2,256,768]{2,0,1:T(2,128)(2,1)}, bf16[2,256,768]{2,0,1:T(2,128)(2,1)}, u32[]{:S(2)}, u32[]{:S(2)}) collective-permute-start(bf16[2,256,768]{2,0,1:T(2,128)(2,1)} %bitcast.84), channel_id=1, source_target_pairs={{0,1},{1,2},{2,3},{3,0},{4,5},{5,6},{6,7},{7,4},{8,9},{9,10},{10,1... | collective-permute-start | bytes 2359304 | tf_op jit(solution)/shard_map/ppermute | solution.py:31
  352.0 116.4 %collective-permute-start.3 = (bf16[2,256,768]{2,0,1:T(2,128)(2,1)}, bf16[2,256,768]{2,0,1:T(2,128)(2,1)}, u32[]{:S(2)}, u32[]{:S(2)}) collective-permute-start(bf16[2,256,768]{2,0,1:T(2,128)(2,1)} %bitcast.83), channel_id=1, source_target_pairs={{0,2},{1,3},{2,0},{3,1},{4,6},{5,7},{6,4},{7,5},{8,10},{9,11},{10,... | collective-permute-start | bytes 2359304 | tf_op jit(solution)/shard_map/ppermute | solution.py:31
  362.6 127.1 %collective-permute-start.4 = (bf16[2,256,768]{2,0,1:T(2,128)(2,1)S(1)}, bf16[2,256,768]{2,0,1:T(2,128)(2,1)S(1)}, u32[]{:S(2)}, u32[]{:S(2)}) collective-permute-start(bf16[2,256,768]{2,0,1:T(2,128)(2,1)S(1)} %bitcast.97), channel_id=1, source_target_pairs={{0,3},{1,0},{2,1},{3,2},{4,7},{5,4},{6,5},{7,6},{8,11},{9,8},{10,9... | collective-permute-start | bytes 2359304 | tf_op jit(solution)/shard_map/ppermute | solution.py:31
  721.6 18.8 %collective-permute-start.9 = (bf16[2,2,1,192]{2,3,1,0:T(8,128)(2,1)S(1)}, bf16[2,2,1,192]{2,3,1,0:T(8,128)(2,1)S(1)}, u32[]{:S(2)}, u32[]{:S(2)}) collective-permute-start(bf16[2,2,1,192]{2,3,1,0:T(8,128)(2,1)S(1)} %bitcast.98), channel_id=1, source_target_pairs={{4,28},{8,24},{12,20},{20,12},{24,8},{28,4},{0,16},{16,0},{5,29},{... | collective-permute-start | bytes 4616 | tf_op jit(solution)/shard_map/ppermute | solution.py:1129
  726.8 6.5 copy-start.4
  733.4 7.4 collective-permute-start.8
  738.3 5.5 copy-start.15
  740.8 4.0 copy-start.1
  (2 other events, 3.3 us)

commit v2 on v1

v2 whole, which is shorter than its diff:
```python
import functools
import math

import jax
import jax.numpy as jnp
import numpy as np
from jax import lax
from jax.experimental import pallas as pl
from jax.experimental.pallas import tpu as pltpu
from jax.sharding import PartitionSpec as P

EPSILON = 1e-05
ONE_TABLE = True
BF = jnp.bfloat16
F32 = jnp.float32
GELU_A = math.sqrt(2.0 / math.pi)
GELU_B = 0.044715


def packed_table(slot_len):
    frequency = np.arange(slot_len, dtype=np.int64)[:, None]
    position = np.arange(slot_len, dtype=np.int64)[None, :]
    angles = (frequency * position % (2 * slot_len)).astype(np.float32) * np.float32(math.pi / slot_len)
    top = np.cos(angles)
    low = -np.sin(angles)
    low[0] = 1.0 - 2.0 * (np.arange(slot_len) % 2)
    return np.concatenate([top, low]).astype(np.float32).astype(jnp.bfloat16)


def shift(x, axis, step):
    n = lax.axis_size(axis)
    return lax.ppermute(x, axis, [(i, (i + step) % n) for i in range(n)])


def exchange(pieces, place, n):
    out = [(place, lax.dynamic_index_in_dim(pieces, place, 0, keepdims=False))]
    for step in range(1, n):
        block = lax.dynamic_index_in_dim(pieces, (place + step) % n, 0, keepdims=False)
        out.append(((place + n - step) % n, shift(block, "tp", step)))
    return out


def mm(a, b):
    return lax.dot_general(a, b, (((1,), (0,)), ((), ())), preferred_element_type=F32)


def mm_nt(a, b):
    return lax.dot_general(a, b, (((1,), (1,)), ((), ())), preferred_element_type=F32)


def mm_tn(a, b):
    return lax.dot_general(a, b, (((0,), (0,)), ((), ())), preferred_element_type=F32)


def mean_of(v):
    return jnp.sum(v, axis=-1, keepdims=True) * (1.0 / v.shape[-1])


def standardize(v):
    centred = v - mean_of(v)
    inverse = lax.rsqrt(mean_of(centred * centred) + EPSILON)
    return centred * inverse, inverse


def norm_back(e, gain, s, q):
    eg = e * gain
    return q * (eg - mean_of(eg) - s * mean_of(eg * s))


def gelu_parts(v):
    square = v * v
    th = jnp.tanh(v * (GELU_A + (GELU_A * GELU_B) * square))
    rise = 0.5 + 0.5 * th
    act = v * rise
    slope = rise + act * (1.0 - th) * (GELU_A + (3.0 * GELU_A * GELU_B) * square)
    return act, slope


def live(rows, first, count):
    at = lax.broadcasted_iota(jnp.int32, (rows, 1), 0) + first
    return jnp.where(at < count, 1.0, 0.0)


def joined(ref):
    v = ref[...]
    return v.reshape(-1, v.shape[-1])


def two_part_dot(a, b, dims):
    high = a.astype(BF)
    low = (a - high.astype(F32)).astype(BF)
    return lax.dot_general(high, b, (dims, ((), ())), preferred_element_type=F32) + lax.dot_general(
        low, b, (dims, ((), ())), preferred_element_type=F32
    )


def top_row(v, rows=8):
    r = lax.broadcasted_iota(jnp.int32, (rows, v.shape[1]), 0)
    return jnp.where(r == 0, jnp.broadcast_to(v, (rows, v.shape[1])), 0.0)


def project_kernel(tile, lens, x, wv, wg, wc, vec, n1, values, gating, nsum, mixing):
    s, t = pl.program_id(0), pl.program_id(1)
    count = lens[s]
    valid = live(tile, t * tile, count)
    std, _ = standardize(x[0].astype(F32))
    normed = (std * vec[0:1] + vec[1:2]).astype(BF)
    n1[0] = normed
    values[0] = ((mm(normed, joined(wv)) + vec[6:7]) * valid).astype(BF)
    gating[0] = (mm(normed, joined(wg)) + vec[7:8]).astype(BF)
    part = top_row(jnp.sum(normed.astype(F32) * valid, axis=0, keepdims=True))

    @pl.when(t == 0)
    def _():
        nsum[0] = part

    @pl.when(t > 0)
    def _():
        nsum[0] += part

    @pl.when(t == pl.num_programs(1) - 1)
    def _():
        length = count.astype(F32)
        cond = two_part_dot(nsum[0], joined(wc), ((1,), (0,))) + length * vec[8:9]
        mixing[0] = jnp.tanh(cond / length)


def filters_of(refs, slots, mix):
    base_r, base_i, mod_r, mod_i = [jnp.concatenate([ref[j] for j in slots]).astype(F32) for ref in refs]
    return base_r + mix * mod_r, base_i + mix * mod_i, mod_r, mod_i


def spectral_kernel(slots, scale, values, gating, mixing, table, f0, f1, f2, f3, spec, conv, gated):
    own = values.shape[0]
    n = values.shape[1]
    raw = [mm(table[...], values[s]) for s in range(own)]
    edge = lax.broadcasted_iota(jnp.int32, (n, 1), 0) == 0
    outs = []
    for s in range(own):
        v = raw[s]
        spec[s] = v.astype(BF)
        sr, si = v[:n], v[n:]
        fr, fi, _, _ = filters_of((f0, f1, f2, f3), slots, mixing[s, 0:1])
        fr2 = jnp.where(edge, fi, fr)
        fi = jnp.where(edge, 0.0, fi)
        prod = jnp.concatenate([(fr * sr - fi * si).astype(BF), (fr2 * si + fi * sr).astype(BF)])
        outs.append(mm_tn(table[...], prod))
    for s in range(own):
        out = outs[s] * scale
        conv[s] = out.astype(BF)
        gated[s] = (out * gating[s].astype(F32)).astype(BF)


def feed_kernel(tile, n_tp, lens, x, gated, w_out, wg, wu, wd, vec, middle, n2, act, side, hidden, out):
    s, t = pl.program_id(0), pl.program_id(1)
    valid = live(tile, t * tile, lens[s])
    mid = x[0].astype(F32) + valid * (mm_nt(gated[0], joined(w_out)) + vec[4:5])
    middle[0] = mid
    std, _ = standardize(mid)
    normed = (std * vec[2:3] + vec[3:4]).astype(BF)
    n2[0] = normed
    feed = jnp.zeros(mid.shape, F32)
    for p in range(n_tp):
        gate = mm(normed, joined(wg.at[:, p]))
        up = mm(normed, joined(wu.at[:, p]))
        a, slope = gelu_parts(gate)
        act[0, p] = a.astype(BF)
        side[0, p] = (up * slope).astype(BF)
        h = (a * up).astype(BF)
        hidden[0, p] = h
        feed += mm(h, joined(wd.at[:, p]))
    out[0] = (mid + valid * (feed + vec[5:6])).astype(BF)


def feed_back_kernel(tile, lens, cot, n2, act, side, hidden, wg, wu, wd, e_out, d_gate, d_up, d_down, acc_g, acc_u, acc_d, fgs, ggs, ugs):
    p, s = pl.program_id(0), pl.program_id(1)
    n = cot.shape[1]

    @pl.when(p == 0)
    def _():
        e_out[s] = jnp.zeros(e_out.shape[1:], F32)

    @pl.when(s == 0)
    def _():
        for acc in (acc_g, acc_u, acc_d):
            acc[...] = jnp.zeros(acc.shape, F32)

    down, gate, up = joined(wd.at[:, 0]), joined(wg.at[:, 0]), joined(wu.at[:, 0])
    for i in range(n // tile):
        here = pl.ds(i * tile, tile)
        fg = (cot[0, here].astype(F32) * live(tile, i * tile, lens[s])).astype(BF)
        fgs[here] = fg
        hg = mm_nt(fg, down)
        ggs[here] = (hg * side[0, 0, here].astype(F32)).astype(BF)
        ugs[here] = (hg * act[0, 0, here].astype(F32)).astype(BF)
    for i in range(n // tile):
        here = pl.ds(i * tile, tile)
        e_out[s, here] += mm_nt(ggs[here], gate) + mm_nt(ugs[here], up)
    normed = n2[0]
    acc_g[...] += mm_tn(normed, ggs[...])
    acc_u[...] += mm_tn(normed, ugs[...])
    acc_d[...] += mm_tn(hidden[0, 0], fgs[...])

    @pl.when(s == pl.num_programs(1) - 1)
    def _():
        for acc, out in zip((acc_g, acc_u, acc_d), (d_gate, d_up, d_down)):
            out[:, 0] = acc[...].astype(BF).reshape(out.shape[0], out.shape[2], out.shape[3])


def branch_back_kernel(tile, lens, e, middle, cot, gated, gating, conv, w_out, vec, mg_out, cg, gtg, d_out, sums, acc):
    s, t = pl.program_id(0), pl.program_id(1)
    begin = (s == 0) & (t == 0)
    end = (s == pl.num_programs(0) - 1) & (t == pl.num_programs(1) - 1)

    @pl.when(begin)
    def _():
        acc[...] = jnp.zeros(acc.shape, F32)
        sums[...] = jnp.zeros(sums.shape, F32)

    valid = live(tile, t * tile, lens[s])
    up = cot[0].astype(F32)
    fg = (up * valid).astype(BF).astype(F32)
    std, inverse = standardize(middle[0])
    grad = e[0]
    mg = up + norm_back(grad, vec[2:3], std, inverse)
    mg_out[0] = mg
    bgr = (mg * valid).astype(BF)
    ggr = mm(bgr, joined(w_out))
    cg[0] = (ggr * gating[0].astype(F32)).astype(BF)
    gtg[0] = (ggr * conv[0].astype(F32)).astype(BF)
    part = mm_tn(bgr, gated[0])
    rows = [grad * std, grad, bgr.astype(F32), fg]
    rows = [jnp.sum(r, axis=0, keepdims=True) for r in rows]

    acc[...] += part
    for i, r in enumerate(rows):
        sums[i : i + 1] += r

    @pl.when(end)
    def _():
        d_out[...] = acc[...].astype(BF).reshape(d_out.shape)


def spectral_back_kernel(slots, scale, lens, cg, spec, mixing, table, f0, f1, f2, f3, vg, fgrad, cgv):
    own = cg.shape[0]
    n = cg.shape[1]
    size = n // len(slots)
    raw = [mm(table[...], cg[s]) for s in range(own)]
    edge = lax.broadcasted_iota(jnp.int32, (n, 1), 0) == 0
    outs, total = [], None
    for s in range(own):
        v = raw[s] * scale
        pr, pi = v[:n], v[n:]
        mix = mixing[s, 0:1]
        fr, fi, mod_r, mod_i = filters_of((f0, f1, f2, f3), slots, mix)
        fr2 = jnp.where(edge, fi, fr)
        fi = jnp.where(edge, 0.0, fi)
        sg = jnp.concatenate([(fr * pr + fi * pi).astype(BF), (fr2 * pi - fi * pr).astype(BF)])
        outs.append(mm_tn(table[...], sg))
        sr, si = spec[s, :n].astype(F32), spec[s, n:].astype(F32)
        both = pi * si
        dr = pr * sr + jnp.where(edge, 0.0, both)
        di = jnp.where(edge, both, pi * sr - pr * si)
        mixg = jnp.sum(mod_r * dr + mod_i * di, axis=0, keepdims=True)
        step = mixg * (1.0 - mix * mix) / lens[s].astype(F32)
        cgv[s] = top_row(step.astype(BF).astype(F32))
        parts = (dr, di, mix * dr, mix * di)
        total = parts if total is None else tuple(t + p for t, p in zip(total, parts))
    for s in range(own):
        vg[s] = (outs[s] * live(n, 0, lens[s])).astype(BF)
    for j in range(len(slots)):
        k = slots.index(j)
        for i in range(4):
            fgrad[j, pl.ds(i * size, size)] = total[i][k * size : (k + 1) * size].astype(BF)


def input_back_kernel(tile, lens, vg, gtg, n1, x, mg, nsum, cgv, wv, wg, wc, d_out, sums_in, vec, ig, d_in, sums, acc_v, acc_g, acc_c):
    s, t = pl.program_id(0), pl.program_id(1)
    begin = (s == 0) & (t == 0)
    end = (s == pl.num_programs(0) - 1) & (t == pl.num_programs(1) - 1)
    count = lens[s]

    @pl.when(begin)
    def _():
        for acc in (acc_v, acc_g, acc_c):
            acc[...] = jnp.zeros(acc.shape, F32)
        sums[...] = jnp.zeros(sums.shape, F32)
        sums[2:6] = sums_in[0:4]

    valid = live(tile, t * tile, count)
    cvec = mm_nt(cgv[0].astype(BF), joined(wc))[0:1]
    vgb, gtb = vg[0], gtg[0]
    e = mm_nt(vgb, joined(wv)) + mm_nt(gtb, joined(wg)) + valid * cvec
    std, inverse = standardize(x[0].astype(F32))
    ig[0] = (mg[0] + norm_back(e, vec[0:1], std, inverse)).astype(BF)
    normed = n1[0]
    part_v, part_g = mm_tn(normed, vgb), mm_tn(normed, gtb)
    rows = [e * std, e, vgb.astype(F32), gtb.astype(F32)]
    rows = [jnp.sum(r, axis=0, keepdims=True) for r in rows]

    acc_v[...] += part_v
    acc_g[...] += part_g
    for i, r in zip((0, 1, 6, 7), rows):
        sums[i : i + 1] += r

    @pl.when(t == 0)
    def _():
        acc_c[...] += two_part_dot(nsum[0], cgv[0].astype(BF), ((0,), (0,)))
        sums[8:9] += cgv[0, 0:1] * count.astype(F32)

    @pl.when(end)
    def _():
        r = d_out.shape[1]
        shape = (d_in.shape[0], r, d_in.shape[2])
        for i, acc in enumerate((acc_v, acc_g, acc_c)):
            d_in[:, i * r : (i + 1) * r] = acc[...].astype(BF).reshape(shape)
        d_in[:, 3 * r :] = d_out[...]


def call(kernel, grid, lens, ins, in_specs, outs, out_specs, scratch, flops, name, limit=56):
    spec = pltpu.PrefetchScalarGridSpec(
        num_scalar_prefetch=1, grid=grid, in_specs=in_specs, out_specs=out_specs, scratch_shapes=scratch
    )
    moved = sum(math.prod(v.shape) * v.dtype.itemsize for v in list(ins) + list(outs))
    return pl.pallas_call(
        kernel,
        grid_spec=spec,
        out_shape=tuple(outs),
        compiler_params=pltpu.CompilerParams(
            dimension_semantics=("arbitrary",) * len(grid), vmem_limit_bytes=limit * 1024 * 1024
        ),
        cost_estimate=pl.CostEstimate(flops=int(flops), bytes_accessed=int(moved), transcendentals=0),
        name=name,
    )(lens, *ins)


def once(block, index):
    return pl.BlockSpec(block, lambda *_: index, pipeline_mode=pl.Buffered(1))


def shape_of(shape, dtype):
    return jax.ShapeDtypeStruct(shape, dtype)


def project(x, lens, aw, vec):
    own, n, width = x.shape
    tile = min(512, n)
    nd, r = aw.shape[0], width // aw.shape[0]
    tok = pl.BlockSpec((1, tile, width), lambda s, t, *_: (s, t, 0))
    one = pl.BlockSpec((1, 8, width), lambda s, t, *_: (s, 0, 0))
    weights = [once((nd, r, width), (0, g, 0)) for g in range(3)]
    sd = shape_of(x.shape, BF)
    row = shape_of((own, 8, width), F32)
    return call(
        functools.partial(project_kernel, tile),
        (own, n // tile),
        lens,
        [x, aw, aw, aw, vec],
        [tok] + weights + [once(vec.shape, (0, 0))],
        [sd, sd, sd, row, row],
        (tok, tok, tok, one, one),
        [],
        4 * own * n * width * width,
        "project",
    )


def filter_specs(fw, n_dp, rows, cb, first):
    return [
        pl.BlockSpec((n_dp, rows, cb), lambda *g, i=i: (0, first + i, g[0])) for i in range(4)
    ]


def spectral(values, gating, mixing, lens, table, fw, first, rows, slots, scale):
    own, n, width = values.shape
    cb = min(256, width)
    n_dp = fw.shape[0]
    tok = pl.BlockSpec((own, n, cb), lambda c, *_: (0, 0, c))
    both = pl.BlockSpec((own, 2 * n, cb), lambda c, *_: (0, 0, c))
    one = pl.BlockSpec((own, 8, cb), lambda c, *_: (0, 0, c))

    def kernel(lens, *refs):
        spectral_kernel(slots, scale, *refs)

    return call(
        kernel,
        (width // cb,),
        lens,
        [values, gating, mixing, table] + [fw] * 4,
        [tok, tok, one, once(table.shape, (0, 0))] + filter_specs(fw, n_dp, rows, cb, first),
        [shape_of((own, 2 * n, width), BF), shape_of(values.shape, BF), shape_of(values.shape, BF)],
        (both, tok, tok),
        [],
        8 * own * n * n * width,
        "spectral",
    )


def feed(x, gated, lens, aw, ffw, vec):
    own, n, width = x.shape
    tile = min(512, n)
    nd, n_tp, _, hid = ffw[0].shape
    r = width // aw.shape[0]
    tok = pl.BlockSpec((1, tile, width), lambda s, t, *_: (s, t, 0))
    wide = pl.BlockSpec((1, n_tp, tile, hid), lambda s, t, *_: (s, 0, t, 0))
    ws = [once(shape, (0, 0, at, 0)) for _, shape, at in ffw[1]]
    big = shape_of((own, n_tp, n, hid), BF)
    return call(
        functools.partial(feed_kernel, tile, n_tp),
        (own, n // tile),
        lens,
        [x, gated, aw] + [w for w, _, _ in ffw[1]] + [vec],
        [tok, tok, once((aw.shape[0], r, width), (0, 3, 0))] + ws + [once(vec.shape, (0, 0))],
        [shape_of(x.shape, F32), shape_of(x.shape, BF), big, big, big, shape_of(x.shape, BF)],
        (tok, tok, wide, wide, wide, tok),
        [],
        2 * own * n * width * (width + 3 * n_tp * hid),
        "feed",
        limit=60,
    )


def feed_back(cot, n2, act, side, hidden, lens, ffw):
    own, n, width = cot.shape
    n_tp, hid = act.shape[1], act.shape[3]
    tile = min(512, n)
    tok = pl.BlockSpec((1, n, width), lambda p, s, *_: (s, 0, 0))
    wide = pl.BlockSpec((1, 1, n, hid), lambda p, s, *_: (s, p, 0, 0))
    ws = [
        pl.BlockSpec((shape[0], 1) + shape[2:], lambda p, s, *_, at=at: (0, p, at, 0)) for _, shape, at in ffw[1]
    ]
    d_specs = [pl.BlockSpec((shape[0], 1) + shape[2:], lambda p, s, *_: (0, p, 0, 0)) for _, shape, _ in ffw[1]]
    d_shapes = [shape_of(shape, BF) for _, shape, _ in ffw[1]]
    return call(
        functools.partial(feed_back_kernel, tile),
        (n_tp, own),
        lens,
        [cot, n2, act, side, hidden] + [w for w, _, _ in ffw[1]],
        [tok, tok, wide, wide, wide] + ws,
        [shape_of(cot.shape, F32)] + d_shapes,
        (pl.BlockSpec(cot.shape, lambda *_: (0, 0, 0), pipeline_mode=pl.Buffered(1)), *d_specs),
        [
            pltpu.VMEM((width, hid), F32),
            pltpu.VMEM((width, hid), F32),
            pltpu.VMEM((hid, width), F32),
            pltpu.VMEM((n, width), BF),
            pltpu.VMEM((n, hid), BF),
            pltpu.VMEM((n, hid), BF),
        ],
        12 * own * n * width * n_tp * hid,
        "feed_back",
        limit=60,
    )


def branch_back(e, middle, cot, gated, gating, conv, lens, aw, vec):
    own, n, width = cot.shape
    tile = min(512, n)
    nd, r = aw.shape[0], width // aw.shape[0]
    tok = pl.BlockSpec((1, tile, width), lambda s, t, *_: (s, t, 0))
    return call(
        functools.partial(branch_back_kernel, tile),
        (own, n // tile),
        lens,
        [e, middle, cot, gated, gating, conv, aw, vec],
        [tok] * 6 + [once((nd, r, width), (0, 3, 0)), once(vec.shape, (0, 0))],
        [
            shape_of(cot.shape, F32),
            shape_of(cot.shape, BF),
            shape_of(cot.shape, BF),
            shape_of((nd, r, width), BF),
            shape_of((8, width), F32),
        ],
        (tok, tok, tok, pl.BlockSpec((nd, r, width), lambda *_: (0, 0, 0)), pl.BlockSpec((8, width), lambda *_: (0, 0))),
        [pltpu.VMEM((width, width), F32)],
        4 * own * n * width * width,
        "branch_back",
    )


def spectral_back(cg, spec, mixing, lens, table, fw, first, rows, slots, scale):
    own, n, width = cg.shape
    cb = min(256, width)
    n_dp = fw.shape[0]
    tok = pl.BlockSpec((own, n, cb), lambda c, *_: (0, 0, c))
    both = pl.BlockSpec((own, 2 * n, cb), lambda c, *_: (0, 0, c))
    one = pl.BlockSpec((own, 8, cb), lambda c, *_: (0, 0, c))
    return call(
        functools.partial(spectral_back_kernel, slots, scale),
        (width // cb,),
        lens,
        [cg, spec, mixing, table] + [fw] * 4,
        [tok, both, one, once(table.shape, (0, 0))] + filter_specs(fw, n_dp, rows, cb, first),
        [shape_of(cg.shape, BF), shape_of((n_dp, 4 * rows, width), BF), shape_of((own, 8, width), F32)],
        (tok, pl.BlockSpec((n_dp, 4 * rows, cb), lambda c, *_: (0, 0, c)), one),
        [],
        8 * own * n * n * width,
        "spectral_back",
    )


def input_back(vg, gtg, n1, x, mg, nsum, cgv, lens, aw, d_out, sums, vec):
    own, n, width = x.shape
    tile = min(512, n)
    nd, r = aw.shape[0], width // aw.shape[0]
    tok = pl.BlockSpec((1, tile, width), lambda s, t, *_: (s, t, 0))
    one = pl.BlockSpec((1, 8, width), lambda s, t, *_: (s, 0, 0))
    weights = [once((nd, r, width), (0, g, 0)) for g in range(3)]
    return call(
        functools.partial(input_back_kernel, tile),
        (own, n // tile),
        lens,
        [vg, gtg, n1, x, mg, nsum, cgv, aw, aw, aw, d_out, sums, vec],
        [tok] * 5 + [one] * 2 + weights + [once((nd, r, width), (0, 0, 0)), once((8, width), (0, 0)), once(vec.shape, (0, 0))],
        [shape_of(x.shape, BF), shape_of((nd, 4 * r, width), BF), shape_of((16, width), F32)],
        (tok, pl.BlockSpec((nd, 4 * r, width), lambda *_: (0, 0, 0)), pl.BlockSpec((16, width), lambda *_: (0, 0))),
        [pltpu.VMEM((width, width), F32)] * 3,
        8 * own * n * width * width,
        "input_back",
    )


MESH = pl.DeviceIdType.MESH


def flip(index, step):
    return index + step - 2 * step * ((index // step) % 2)


def bit_orders(n_dp):
    bits = [1 << b for b in range(1, (n_dp - 1).bit_length())]
    return bits, bits[::-1]


def greet(d, z, n_dp, n_tp):
    barrier = pltpu.get_barrier_semaphore()
    count = 0
    step = 1
    while step < n_dp:
        pl.semaphore_signal(barrier, inc=1, device_id=(flip(d, step), z), device_id_type=MESH)
        step *= 2
        count += 1
    for k in range(1, n_tp):
        pl.semaphore_signal(barrier, inc=1, device_id=(d, lax.rem(z + k, n_tp)), device_id_type=MESH)
        count += 1
    pl.semaphore_wait(barrier, count)


def remote(src, dst, send, recv, target):
    copy = pltpu.make_async_remote_copy(
        src_ref=src, dst_ref=dst, send_sem=send, recv_sem=recv, device_id=target, device_id_type=MESH
    )
    copy.start()
    return copy


class Pack:
    def __init__(self, rows, ch):
        self.rows, self.ch = rows, ch
        self.main = ch // 128
        self.rest = ch % 128
        self.dense = self.rest == 64 and rows % 32 == 0
        self.tail = 0 if not self.rest else rows // 2 if self.dense else rows
        self.total = self.main * rows + self.tail

    def pack(self, v):
        parts = [v[:, i * 128 : (i + 1) * 128] for i in range(self.main)]
        if self.rest:
            left = v[:, self.main * 128 :]
            if self.dense:
                parts.append(jnp.concatenate([left[: self.tail], left[self.tail :]], axis=1))
            else:
                parts.append(jnp.pad(left, ((0, 0), (0, 128 - self.rest))))
        return jnp.concatenate(parts)

    def unpack(self, v):
        parts = [v[i * self.rows : (i + 1) * self.rows] for i in range(self.main)]
        if self.rest:
            left = v[self.main * self.rows :]
            if self.dense:
                parts.append(jnp.concatenate([left[:, :64], left[:, 64:]]))
            else:
                parts.append(left[:, : self.rest])
        return jnp.concatenate(parts, axis=1)

    def pieces(self):
        out = [(i * self.rows, 0, self.rows, 0, 128, i * 128) for i in range(self.main)]
        at = self.main * self.rows
        if self.dense:
            out += [(at, 0, self.tail, 0, 64, self.main * 128), (at, self.tail, self.tail, 64, 64, self.main * 128)]
        elif self.rest:
            out += [(at, 0, self.rows, 0, self.rest, self.main * 128)]
        return out


def lanes_to(width, lane, lanes, column):
    r = lax.broadcasted_iota(jnp.int32, (128, width), 0)
    c = lax.broadcasted_iota(jnp.int32, (128, width), 1)
    inside = (r >= lane) & (r < lane + lanes)
    return jnp.where(inside & (c - r == column - lane), 1.0, 0.0).astype(BF)


def fill_places(ones, layout, width, n_tp):
    pieces = layout.pieces()
    for s in range(n_tp):
        for i, (_, _, _, lane, lanes, column) in enumerate(pieces):
            ones[s * len(pieces) + i] = lanes_to(width, lane, lanes, s * layout.ch + column)


class Line:
    def __init__(self, part, d, z, n, send, recv):
        self.part, self.d, self.z, self.n, self.send, self.recv = part, d, z, n, send, recv

    def _copy(self, way, t, block):
        target = (self.d, self.z + 1 if way == 0 else self.z - 1)
        return pltpu.make_async_remote_copy(
            src_ref=self.part(block),
            dst_ref=self.part(block),
            send_sem=self.send.at[way, t],
            recv_sem=self.recv.at[way, t],
            device_id=target,
            device_id_type=MESH,
        )

    def start(self, t):
        z, n = self.z, self.n

        @pl.when((z >= t) & (z < n - 1))
        def _():
            self._copy(0, t, z - t).start()

        @pl.when((z + t < n) & (z > 0))
        def _():
            self._copy(1, t, z + t).start()

    def wait(self, t):
        z, n = self.z, self.n

        @pl.when(z >= t + 1)
        def _():
            self._copy(0, t, z - 1 - t).wait_recv()

        @pl.when(z + t + 1 < n)
        def _():
            self._copy(1, t, z + 1 + t).wait_recv()

    def drain(self):
        z, n = self.z, self.n
        for t in range(n - 1):

            @pl.when((z >= t) & (z < n - 1))
            def _(t=t):
                self._copy(0, t, z - t).wait_send()

            @pl.when((z + t < n) & (z > 0))
            def _(t=t):
                self._copy(1, t, z + t).wait_send()


class Spread:
    def __init__(self, part, order, d, z, send, recv):
        self.part, self.z, self.send, self.recv = part, z, send, recv
        held, self.steps, used = [d], [], 0
        for step in order:
            self.steps.append((flip(d, step), [(slot, used + i) for i, slot in enumerate(held)]))
            used += len(held)
            held = held + [flip(slot, step) for slot in held]
        self.stage = 0

    def copies(self, stage):
        target, sent = self.steps[stage]
        return [
            pltpu.make_async_remote_copy(
                src_ref=self.part(slot),
                dst_ref=self.part(slot),
                send_sem=self.send.at[i],
                recv_sem=self.recv.at[i],
                device_id=(target, self.z),
                device_id_type=MESH,
            )
            for slot, i in sent
        ]

    def start(self):
        for copy in self.copies(self.stage):
            copy.start()

    def wait(self):
        for copy in self.copies(self.stage):
            copy.wait_recv()
        self.stage += 1

    def drain(self):
        for stage in range(len(self.steps)):
            for copy in self.copies(stage):
                copy.wait_send()


def chunk_of(rows):
    return next((c for c in (128, 96, 64, 48, 32, 16) if rows % c == 0), rows)


def add_rows(dst, src):
    rows = dst.shape[0]
    size = chunk_of(rows)

    @pl.loop(0, rows // size)
    def _(i):
        at = pl.ds(i * size, size)
        dst[at] = (dst[at].astype(F32) + src[at].astype(F32)).astype(BF)


def lane_place(rows, cols, offset):
    r = lax.broadcasted_iota(jnp.int32, (rows, cols), 0)
    c = lax.broadcasted_iota(jnp.int32, (rows, cols), 1)
    return jnp.where(c - r == offset, 1.0, 0.0).astype(BF)


def gather_kernel(
    n_dp, n_tp, cut, ff_in, a_in, vec_in, x_in, ff_out, a_out, x_out, a_z, a_nat, ones,
    la_send, la_recv, lf_send, lf_recv, x_send, x_recv, s_send, s_recv, local,
):
    d, z = lax.axis_index("dp"), lax.axis_index("tp")
    width = a_nat.shape[1]
    ch = width // n_tp
    rows = a_nat.shape[0] - vec_in.shape[0]
    layout = Pack(rows, ch)
    own_ff = pltpu.make_async_copy(ff_in, ff_out.at[d, z], local.at[0])
    own_ff.start()
    own_a = pltpu.make_async_copy(a_in, a_z.at[z], local.at[1])
    own_a.start()
    greet(d, z, n_dp, n_tp)
    line_a = Line(lambda s: a_z.at[s], d, z, n_tp, la_send, la_recv)
    line_f = Line(lambda s: ff_out.at[d, s], d, z, n_tp, lf_send, lf_recv)
    first, second = bit_orders(n_dp)
    ff_rows = ff_in.shape[0]
    ff_cut = ff_rows // 2 // 16 * 16

    def block_spreads(block):
        out = []
        for h, (lo, count, order) in enumerate(((0, ff_cut, first), (ff_cut, ff_rows - ff_cut, second))):
            at = 2 + 2 * block + h
            out.append(
                Spread(
                    lambda s, lo=lo, count=count: ff_out.at[s, block, pl.ds(lo, count)],
                    order + [1], d, z, s_send.at[at], s_recv.at[at],
                )
            )
        return out

    own_a.wait()
    line_a.start(0)
    own_ff.wait()
    f_own = block_spreads(z)
    for p in f_own:
        p.start()
    fill_places(ones, layout, width, n_tp)
    for t in range(n_tp - 1):
        line_a.wait(t)
        if t + 1 < n_tp - 1:
            line_a.start(t + 1)
    line_f.start(0)
    half_rows = rows // 2
    n_pieces = len(layout.pieces())
    size = chunk_of(half_rows)
    for side in range(2):
        found = []
        for j, (packed, low, count, _, _, _) in enumerate(layout.pieces()):
            if low <= side * half_rows < low + count:
                found.append((packed + side * half_rows - low, j))

        @pl.loop(0, half_rows // size)
        def _(i, found=found, side=side):
            total = jnp.zeros((size, width), F32)
            for s in range(n_tp):
                for packed, j in found:
                    total += mm(a_z[s, pl.ds(packed + i * size, size)], ones[s * n_pieces + j])
            a_nat[pl.ds(side * half_rows + i * size, size)] = total.astype(BF)

    a_nat[rows:] = vec_in[...]
    put = pltpu.make_async_copy(a_nat, a_out.at[d], local.at[2])
    put.start()
    put.wait()
    total_rows = a_nat.shape[0]
    sa = [
        Spread(lambda s: a_out.at[s, pl.ds(0, cut)], first + [1], d, z, s_send.at[0], s_recv.at[0]),
        Spread(lambda s: a_out.at[s, pl.ds(cut, total_rows - cut)], second + [1], d, z, s_send.at[1], s_recv.at[1]),
    ]
    for p in sa:
        p.start()
    stages = len(first) + 1

    def advance(group):
        for p in group:
            p.wait()
            if p.stage < stages:
                p.start()

    advance(f_own)
    blocks = []
    for t in range(n_tp - 1):
        line_f.wait(t)
        if t + 1 < n_tp - 1:
            line_f.start(t + 1)
        for exists, block in ((z >= t + 1, z - 1 - t), (z + t + 1 < n_tp, z + 1 + t)):
            group = block_spreads(block)
            blocks.append((exists, group))

            @pl.when(exists)
            def _(group=group):
                for p in group:
                    p.start()

        if t == 0:
            advance(sa)
            advance(f_own)
    size = x_in.shape[2]
    here = pl.ds(z * size, size)
    own_x = pltpu.make_async_copy(x_in.at[z], x_out.at[:, here], local.at[3])
    own_x.start()
    zx = []
    for k in range(1, n_tp):
        peer = lax.rem(z + k, n_tp)
        zx.append(remote(x_in.at[peer], x_out.at[:, here], x_send.at[k - 1], x_recv.at[k - 1], (d, peer)))
    for stage in range(stages):
        for exists, group in blocks:

            @pl.when(exists)
            def _(group=group):
                advance(group)

        if stage + 1 < stages:
            advance(sa)
        if stage == 0:
            for p in f_own:
                p.wait()
    for p in sa + f_own:
        p.drain()
    for exists, group in blocks:

        @pl.when(exists)
        def _(group=group):
            for p in group:
                p.drain()

    own_x.wait()
    for copy in zx:
        copy.wait_recv()
    for copy in zx:
        copy.wait_send()
    line_a.drain()
    line_f.drain()


def gather_weights(ff_in, a_in, a_rows, vec_in, x_in, n_dp, n_tp):
    width = vec_in.shape[1]
    rows = a_rows
    total = rows + vec_in.shape[0]
    cut = total // 2 // 16 * 16
    anyspace = pl.BlockSpec(memory_space=pl.ANY)
    vmem = pl.BlockSpec(memory_space=pltpu.VMEM)
    return pl.pallas_call(
        functools.partial(gather_kernel, n_dp, n_tp, cut),
        out_shape=(
            jax.ShapeDtypeStruct((n_dp, n_tp) + ff_in.shape, BF),
            jax.ShapeDtypeStruct((n_dp, total, width), BF),
            jax.ShapeDtypeStruct((x_in.shape[1], n_tp * x_in.shape[2], width), BF),
        ),
        in_specs=[anyspace, anyspace, vmem, anyspace],
        out_specs=(anyspace, anyspace, anyspace),
        scratch_shapes=[
            pltpu.VMEM((n_tp,) + a_in.shape, BF),
            pltpu.VMEM((total, width), BF),
            pltpu.VMEM((n_tp * len(Pack(rows, width // n_tp).pieces()), 128, width), BF),
            pltpu.SemaphoreType.DMA((2, n_tp - 1)),
            pltpu.SemaphoreType.DMA((2, n_tp - 1)),
            pltpu.SemaphoreType.DMA((2, n_tp - 1)),
            pltpu.SemaphoreType.DMA((2, n_tp - 1)),
            pltpu.SemaphoreType.DMA((n_tp - 1,)),
            pltpu.SemaphoreType.DMA((n_tp - 1,)),
            pltpu.SemaphoreType.DMA((2 + 2 * n_tp, n_dp - 1)),
            pltpu.SemaphoreType.DMA((2 + 2 * n_tp, n_dp - 1)),
            pltpu.SemaphoreType.DMA((4,)),
        ],
        compiler_params=pltpu.CompilerParams(
            collective_id=0, has_side_effects=True, vmem_limit_bytes=48 * 1024 * 1024
        ),
        name="gather_weights",
    )(ff_in, a_in, vec_in, x_in)


class Fold:
    def __init__(self, part, mine, two, order, own, d, z, send, recv):
        self.part, self.mine, self.two, self.z, self.send, self.recv = part, mine, two, z, send, recv
        self.steps, used = [], 0

        def at(mask):
            index, step = own, 1
            while step <= mask:
                if mask & step:
                    index = flip(index, step)
                step *= 2
            return index

        for t, step in enumerate(order):
            masks = [0]
            for later in order[t + 1 :]:
                masks = masks + [m + later for m in masks]
            moves = [(at(m + step), at(m), used + j) for j, m in enumerate(masks)]
            used += len(moves)
            self.steps.append((flip(d, 2 * step), moves))
        self.stage = 0

    def copies(self, stage):
        target, moves = self.steps[stage]
        return [
            pltpu.make_async_remote_copy(
                src_ref=self.part(self.mine, away),
                dst_ref=self.part(self.two, k),
                send_sem=self.send.at[k],
                recv_sem=self.recv.at[k],
                device_id=(target, self.z),
                device_id_type=MESH,
            )
            for away, _, k in moves
        ]

    def start(self):
        for copy in self.copies(self.stage):
            copy.start()

    def finish(self, add):
        for copy, (_, keep, k) in zip(self.copies(self.stage), self.steps[self.stage][1]):
            copy.wait()
            add(self.part(self.mine, keep), self.part(self.two, k))
        self.stage += 1


class LineSum:
    def __init__(self, mine, got, d, z, n, send, recv):
        self.mine, self.got, self.d, self.z, self.n, self.send, self.recv = mine, got, d, z, n, send, recv

    def _copy(self, way, block):
        return pltpu.make_async_remote_copy(
            src_ref=self.mine(block),
            dst_ref=self.got.at[way, block],
            send_sem=self.send.at[way, block],
            recv_sem=self.recv.at[way, block],
            device_id=(self.d, self.z - 1 if way == 0 else self.z + 1),
            device_id_type=MESH,
        )

    def take(self, block, add):
        z, n = self.z, self.n

        @pl.when((block <= z) & (z < n - 1))
        def _():
            self._copy(0, block).wait_recv()
            add(self.mine(block), self.got.at[0, block])

        @pl.when((block >= z) & (z > 0))
        def _():
            self._copy(1, block).wait_recv()
            add(self.mine(block), self.got.at[1, block])

    def give(self, block):
        @pl.when(block < self.z)
        def _():
            self._copy(0, block).start()

        @pl.when(block > self.z)
        def _():
            self._copy(1, block).start()

    def drain(self, block):
        @pl.when(block < self.z)
        def _():
            self._copy(0, block).wait_send()

        @pl.when(block > self.z)
        def _():
            self._copy(1, block).wait_send()


def scatter_kernel(
    n_dp, n_tp, cut, g0, g1, g2, a0, a1, v_in, x_in, ff_out, a_out, v_out, x_out,
    ff_mine, a_mine, ff_core, a_core, ff_two, a_two, a_cols, ff_got, a_got, v_got, ones,
    load, core_send, core_recv, f_send, f_recv, h_send, h_recv, lf_send, lf_recv, la_send, la_recv,
    z_send, z_recv, s_send, s_recv, v_send, v_recv, local,
):
    d, z = lax.axis_index("dp"), lax.axis_index("tp")
    width = a0.shape[3]
    rows = a0.shape[2] + a1.shape[2]
    layout = Pack(rows, width // n_tp)
    vec = g0.shape[3]
    half = n_dp // 2
    side = d % 2
    own = d // 2
    other = (flip(d, 1), z)
    late = z // (n_tp // 2)
    order = [n_tp - 1 - j + late * (2 * j - n_tp + 1) for j in range(n_tp)]
    greet(d, z, n_dp, n_tp)
    f_core, f_load = [], []
    for j, b in enumerate(order):
        for g, src in enumerate((g0, g1, g2)):
            f_core.append(
                remote(src.at[:, 1 - side, b], ff_core.at[b, :, g], core_send.at[g, j], core_recv.at[g, j], other)
            )
            copy = pltpu.make_async_copy(src.at[:, side, b], ff_mine.at[b, :, g], load.at[g, j])
            copy.start()
            f_load.append(copy)
    a_swap, a_load = [], []
    at = 0
    for g, src in enumerate((a0, a1)):
        part = pl.ds(at, src.shape[2])
        at += src.shape[2]
        a_swap.append(remote(src.at[:, 1 - side], a_core.at[:, part], core_send.at[3, g], core_recv.at[3, g], other))
        copy = pltpu.make_async_copy(src.at[:, side], a_mine.at[:, part], load.at[3, g])
        copy.start()
        a_load.append(copy)
    slot = x_out.shape[2]
    own_x = pltpu.make_async_copy(x_in.at[:, pl.ds(z * slot, slot)], x_out.at[z], local.at[1])
    own_x.start()
    zx = []
    for k in range(1, n_tp):
        peer = lax.rem(z + k, n_tp)
        zx.append(
            remote(x_in.at[:, pl.ds(peer * slot, slot)], x_out.at[z], z_send.at[1, k - 1], z_recv.at[1, k - 1], (d, peer))
        )
    v_out[...] = v_in[...]
    first, second = bit_orders(n_dp)
    for i, step in enumerate([1] + first):
        copy = remote(v_out, v_got.at[i], v_send.at[i], v_recv.at[i], (flip(d, step), z))
        copy.wait()
        v_out[...] += v_got[i]
    v_base = len(first) + 1
    zv = []
    for k in range(1, n_tp):
        peer = lax.rem(z + k, n_tp)
        zv.append(remote(v_out, v_got.at[v_base + k - 1], z_send.at[0, k - 1], z_recv.at[0, k - 1], (d, peer)))
    fill_places(ones, layout, width, n_tp)

    def add_three(dst, src):
        for g in range(3):
            add_rows(dst.at[g], src.at[g])

    ways = ([s // 2 for s in first[::-1]], [s // 2 for s in second[::-1]])
    folds = []
    for j, b in enumerate(order):
        for g in range(3):
            f_load[3 * j + g].wait()
            f_core[3 * j + g].wait_recv()
        for i in range(half):
            add_three(ff_mine.at[b, i], ff_core.at[b, i])
        fold = Fold(
            lambda ref, e, b=b: ref.at[b, e], ff_mine, ff_two, ways[j % 2], own, d, z, f_send.at[j], f_recv.at[j]
        )
        fold.start()
        folds.append(fold)
    for copy in a_load:
        copy.wait()
    for copy in a_swap:
        copy.wait_recv()
    for i in range(half):
        add_rows(a_mine.at[i], a_core.at[i])
    a_folds = [
        Fold(
            lambda ref, e, lo=lo, count=count: ref.at[e, pl.ds(lo, count)],
            a_mine, a_two, ways[h], own, d, z, h_send.at[h], h_recv.at[h],
        )
        for h, (lo, count) in enumerate(((0, cut), (cut, rows - cut)))
    ]
    n_stage = len(ways[0])
    line_f = LineSum(lambda b: ff_mine.at[b, own], ff_got, d, z, n_tp, lf_send, lf_recv)
    line_a = LineSum(lambda b: a_cols.at[b], a_got, d, z, n_tp, la_send, la_recv)
    for t in range(n_stage - 1):
        for fold in folds:
            fold.finish(add_three)
            fold.start()
        if t == 0:
            for fold in a_folds:
                fold.start()
    for j, (fold, b) in enumerate(zip(folds, order)):
        fold.finish(add_three)

        @pl.when(b != z)
        def _(b=b):
            line_f.take(b, add_three)
            line_f.give(b)

    for t in range(1, n_stage):
        for fold in a_folds:
            fold.finish(add_rows)
            fold.start()
    line_f.take(z, add_three)
    put = pltpu.make_async_copy(ff_mine.at[z, own], ff_out.at[d], local.at[0])
    put.start()
    put.wait()
    pieces = [(0, 0, vec, first), (1, 0, vec, second)]
    if vec % 32 == 0:
        pieces += [(2, 0, vec // 2, first), (2, vec // 2, vec // 2, second)]
    else:
        pieces += [(2, 0, vec, first)]
    sf = [
        Spread(lambda s, g=g, lo=lo, n=n: ff_out.at[s, g, pl.ds(lo, n)], way + [1], d, z, s_send.at[i], s_recv.at[i])
        for i, (g, lo, n, way) in enumerate(pieces)
    ]
    for p in sf:
        p.start()
    for fold in a_folds:
        fold.finish(add_rows)
    n_pieces = len(layout.pieces())
    groups = {}
    for i, (packed, low, count, _, _, _) in enumerate(layout.pieces()):
        groups.setdefault((packed, count), []).append((low, i))
    for (packed, count), found in groups.items():
        size = chunk_of(count)

        @pl.loop(0, count // size)
        def _(i, packed=packed, found=found, size=size):
            for s in range(n_tp):
                total = jnp.zeros((size, 128), F32)
                for low, j in found:
                    block = a_mine[own, pl.ds(low + i * size, size)]
                    total += mm_nt(block, ones[s * n_pieces + j])
                a_cols[s, pl.ds(packed + i * size, size)] = total.astype(BF)

    for stage in range(len(first) + 1):
        for p in sf:
            p.wait()
            if stage < len(first):
                p.start()
        if stage == 0:
            for b in order:

                @pl.when(b != z)
                def _(b=b):
                    line_a.take(b, add_rows)
                    line_a.give(b)

    line_a.take(z, add_rows)
    a_out[...] = a_cols[z].astype(F32)
    for copy in zv:
        copy.wait()
    for k in range(1, n_tp):
        v_out[...] += v_got[v_base + k - 1]
    own_x.wait()
    for copy in zx:
        copy.wait_recv()
    for copy in f_core + a_swap + zx:
        copy.wait_send()
    for b in range(n_tp):
        line_f.drain(b)
        line_a.drain(b)
    for p in sf:
        p.drain()


def scatter_grads(ff, a0, a1, vectors, x_in, n_dp, n_tp):
    width = a0.shape[2]
    rows = a0.shape[1] + a1.shape[1]
    vec, hid = ff[0].shape[2:]
    packed = Pack(rows, width // n_tp).total
    cut = rows // 2 // 16 * 16
    half = n_dp // 2
    anyspace = pl.BlockSpec(memory_space=pl.ANY)
    vmem = pl.BlockSpec(memory_space=pltpu.VMEM)
    dma = pltpu.SemaphoreType.DMA
    pairs = lambda v: v.reshape((half, 2) + v.shape[1:])
    most = max(4, n_tp, 2)
    return pl.pallas_call(
        functools.partial(scatter_kernel, n_dp, n_tp, cut),
        out_shape=(
            jax.ShapeDtypeStruct((n_dp, 3, vec, hid), BF),
            jax.ShapeDtypeStruct((packed, 128), F32),
            jax.ShapeDtypeStruct(vectors.shape, F32),
            jax.ShapeDtypeStruct((n_tp, x_in.shape[0], x_in.shape[1] // n_tp, width), BF),
        ),
        in_specs=[anyspace] * 5 + [vmem, anyspace],
        out_specs=(anyspace, vmem, vmem, anyspace),
        scratch_shapes=[
            pltpu.VMEM((n_tp, half, 3, vec, hid), BF),
            pltpu.VMEM((half, rows, width), BF),
            pltpu.VMEM((n_tp, half, 3, vec, hid), BF),
            pltpu.VMEM((half, rows, width), BF),
            pltpu.VMEM((n_tp, half - 1, 3, vec, hid), BF),
            pltpu.VMEM((half - 1, rows, width), BF),
            pltpu.VMEM((n_tp, packed, 128), BF),
            pltpu.VMEM((2, n_tp, 3, vec, hid), BF),
            pltpu.VMEM((2, n_tp, packed, 128), BF),
            pltpu.VMEM(((half - 1).bit_length() + n_tp,) + vectors.shape, F32),
            pltpu.VMEM((n_tp * len(Pack(rows, width // n_tp).pieces()), 128, width), BF),
            dma((4, most)),
            dma((4, most)),
            dma((4, most)),
            dma((n_tp, half - 1)),
            dma((n_tp, half - 1)),
            dma((2, half - 1)),
            dma((2, half - 1)),
            dma((2, n_tp)),
            dma((2, n_tp)),
            dma((2, n_tp)),
            dma((2, n_tp)),
            dma((2, n_tp - 1)),
            dma((2, n_tp - 1)),
            dma((4, n_dp - 1)),
            dma((4, n_dp - 1)),
            dma(((half - 1).bit_length() + 1,)),
            dma(((half - 1).bit_length() + 1,)),
            dma((2,)),
        ],
        compiler_params=pltpu.CompilerParams(
            collective_id=1, has_side_effects=True, vmem_limit_bytes=60 * 1024 * 1024
        ),
        name="scatter_grads",
    )(*[pairs(g) for g in ff], pairs(a0), pairs(a1), vectors, x_in)


def body(
    tokens,
    lengths,
    cotangent,
    norm1_gain,
    norm1_bias,
    in_weight,
    in_bias,
    filter_base,
    filter_mod,
    out_weight,
    out_bias,
    norm2_gain,
    norm2_bias,
    gate_weight,
    up_weight,
    down_weight,
    down_bias,
):
    micro, local, group, width = tokens.shape
    n_tp = lax.axis_size("tp")
    n_dp = lax.axis_size("dp")
    z = lax.axis_index("tp")
    d = lax.axis_index("dp")
    slot_len = local * n_tp
    own = micro * group // n_tp
    per_micro = min(group, own)
    ch = in_weight.shape[2]
    vec = width // n_dp
    hid = gate_weight.shape[1]
    table = jnp.asarray(packed_table(slot_len))
    scale = 0.5 / slot_len

    rows = slot_len // n_dp
    last = n_dp - 1
    upper = d > last - d
    filters = jnp.stack([filter_base, filter_mod])
    across = [(i, (n_dp - i) % n_dp) for i in range(n_dp) if i % (n_dp // 2)] + [(0, n_dp // 2), (n_dp // 2, 0)]
    got = lax.ppermute(filters[:, :, rows:], "dp", [(i, last - i) for i in range(n_dp)])
    got_edge = lax.ppermute(filters[:, :, :1], "dp", across)
    direct = jnp.where(upper, got, filters[:, :, :rows]).astype(F32)
    mirror_lower = jnp.concatenate([got[:, :, 1:], got_edge], axis=2)
    mirror_upper = filters[:, :, 1 : rows + 1]
    mirror = jnp.flip(jnp.where(upper, mirror_upper, mirror_lower), 2).astype(F32)
    nyquist = got_edge[:, 0, 0].astype(F32)
    edge = ((jnp.arange(rows) == 0) & (d == 0))[None, :, None]
    half_real = jnp.where(edge, direct[:, 0], direct[:, 0] + mirror[:, 0])
    half_imag = jnp.where(edge, nyquist[:, None], direct[:, 1] - mirror[:, 1])
    half = jnp.stack([half_real, half_imag], 1).astype(BF).reshape(4 * rows, ch)
    slice_of = [2 * i if 2 * i < n_dp else 2 * (last - i) + 1 for i in range(n_dp)]

    a_in = jnp.concatenate([in_weight.transpose(1, 0, 2).reshape(3 * vec, ch), out_weight.T, half])
    vectors = jnp.stack([norm1_gain, norm1_bias, norm2_gain, norm2_bias, out_bias, down_bias])
    vectors = jnp.concatenate([vectors, in_bias])
    vectors = jnp.pad(vectors, ((0, 16 - 9), (0, width - vec)))
    share = hid // n_dp
    ff_in = jnp.concatenate(
        [
            lax.dynamic_slice_in_dim(gate_weight, d * vec, vec, 0),
            lax.dynamic_slice_in_dim(up_weight, d * vec, vec, 0),
            lax.dynamic_slice_in_dim(down_weight, d * share, share, 0).reshape(vec, hid),
        ]
    )
    x_in = tokens.transpose(0, 2, 1, 3).reshape(n_tp, own, local, width)
    layout = Pack(a_in.shape[0], ch)
    ffw, aw, x_own = gather_weights(ff_in, layout.pack(a_in), a_in.shape[0], vectors, x_in, n_dp, n_tp)
    cotangent, _ = lax.optimization_barrier((cotangent, aw))
    vectors = aw[:, 4 * vec + 4 * rows :, :vec].astype(F32).transpose(1, 0, 2).reshape(16, width)
    slots = [slice_of.index(k) for k in range(n_dp)]
    direct = vec % 16 == 0 and hid == width
    if direct:
        ws = [(ffw, (n_dp, n_tp, vec, hid), g) for g in range(3)]
        a_view = aw
    else:
        natural = [
            ffw[:, :, g * vec : (g + 1) * vec].transpose(1, 0, 2, 3).reshape(n_tp, width, hid) for g in range(2)
        ]
        natural.append(
            ffw[:, :, 2 * vec :].reshape(n_dp, n_tp, share, width).transpose(1, 0, 2, 3).reshape(n_tp, hid, width)
        )
        ws = [(w[None], (1,) + w.shape, 0) for w in natural]
        a_view = aw[:, : 4 * vec].reshape(n_dp, 4, vec, width).transpose(1, 0, 2, 3).reshape(1, 4 * width, width)
    feed_weights = (ws[0][0], ws)

    def to_owner(x):
        pieces = x.transpose(0, 2, 1, 3).reshape(n_tp, own, local, width)
        return lax.all_to_all(pieces, "tp", 0, 1, tiled=False).reshape(own, slot_len, width)

    def to_slots(x):
        pieces = x.reshape(own, n_tp, local, width)
        whole = lax.all_to_all(pieces, "tp", 1, 0, tiled=False)
        return whole.reshape(micro, group, local, width).transpose(0, 2, 1, 3)

    c_own = to_owner(cotangent)
    flat_len = lax.dynamic_slice_in_dim(lengths.reshape(-1), z * own, own, 0)
    first = 4 * vec // rows
    n1, values, gating, nsum, mixing = project(x_own, flat_len, a_view, vectors)
    spec, conv, gated = spectral(values, gating, mixing, flat_len, table, aw, first, rows, slots, scale)
    middle, n2, act, side, hidden, out = feed(x_own, gated, flat_len, a_view, feed_weights, vectors)
    layer_out = to_slots(out)
    e, *d_ff = feed_back(c_own, n2, act, side, hidden, flat_len, feed_weights)
    mg, cg, gtg, d_out, sums = branch_back(e, middle, c_own, gated, gating, conv, flat_len, a_view, vectors)
    layer_out, cg = lax.optimization_barrier((layer_out, cg))
    vg, d_filter, cgv = spectral_back(cg, spec, mixing, flat_len, table, aw, first, rows, slots, scale)
    ig, d_first, sums = input_back(vg, gtg, n1, x_own, mg, nsum, cgv, flat_len, a_view, d_out, sums, vectors)
    if not direct:
        d_ff = [
            g[0].reshape(n_tp, n_dp, vec, hid).transpose(1, 0, 2, 3) for g in d_ff[:2]
        ] + [d_ff[2][0].reshape(n_tp, n_dp, vec, hid).transpose(1, 0, 2, 3)]
        d_first = d_first.reshape(4, n_dp, vec, width).transpose(1, 0, 2, 3).reshape(n_dp, 4 * vec, width)
    ffg, ag, vecs, input_grad = scatter_grads(d_ff, d_first, d_filter, sums, ig, n_dp, n_tp)
    input_grad = input_grad.reshape(micro, group, local, width).transpose(0, 2, 1, 3)
    ag = layout.unpack(ag)
    gate_grad = ffg[:, 0].reshape(width, hid).astype(F32)
    up_grad = ffg[:, 1].reshape(width, hid).astype(F32)
    down_grad = ffg[:, 2].reshape(hid, width).astype(F32)
    in_grad = ag[: 3 * vec].reshape(3, vec, ch).transpose(1, 0, 2)
    out_grad = ag[3 * vec : 4 * vec].T
    fgrad = ag[4 * vec :].astype(BF).reshape(2, 2, rows, ch)
    other = lax.ppermute(fgrad, "dp", [(i, last - i) for i in range(n_dp)])
    low_slice = jnp.where(upper, other, fgrad)
    high_slice = jnp.where(upper, fgrad, other)
    both = jnp.concatenate([low_slice, high_slice], axis=2)
    follow = lax.ppermute(fgrad[:, :, :1], "dp", across)
    zero = jnp.zeros_like(follow[:, 0])
    follow = jnp.where(d == n_dp // 2, jnp.stack([follow[:, 1], zero], 1), follow)
    mirrored = jnp.flip(jnp.concatenate([both[:, :, 1:], follow], axis=2), 2)
    mirrored = jnp.stack([mirrored[:, 0], -mirrored[:, 1]], 1)
    plain = jnp.stack(
        [both[:, 0], jnp.where((d == 0) & (jnp.arange(2 * rows) == 0)[None, :, None], 0.0, both[:, 1].astype(F32)).astype(BF)], 1
    )
    full = jnp.where(upper, mirrored, plain).astype(F32)

    piece = width // (n_dp * n_tp)
    vecs = lax.dynamic_slice_in_dim(vecs, (d * n_tp + z) * piece, piece, 1)
    return (
        layer_out,
        input_grad,
        vecs[0],
        vecs[1],
        in_grad,
        vecs[6:9],
        full[0],
        full[1],
        out_grad,
        vecs[4],
        vecs[2],
        vecs[3],
        gate_grad,
        up_grad,
        down_grad,
        vecs[5],
    )


def solution(mesh):
    in_specs = (
        P(None, "tp", "dp", None),
        P(None, "dp"),
        P(None, "tp", "dp", None),
        P("dp"),
        P("dp"),
        P("dp", None, "tp"),
        P(None, "dp"),
        P(None, "dp", "tp"),
        P(None, "dp", "tp"),
        P("tp", "dp"),
        P("dp"),
        P("dp"),
        P("dp"),
        P(None, "tp"),
        P(None, "tp"),
        P("tp", None),
        P("dp"),
    )
    out_specs = (
        P(None, "tp", "dp", None),
        P(None, "tp", "dp", None),
        P(("dp", "tp")),
        P(("dp", "tp")),
        P("dp", None, "tp"),
        P(None, ("dp", "tp")),
        P(None, "dp", "tp"),
        P(None, "dp", "tp"),
        P("tp", "dp"),
        P(("dp", "tp")),
        P(("dp", "tp")),
        P(("dp", "tp")),
        P(None, "tp"),
        P(None, "tp"),
        P("tp", None),
        P(("dp", "tp")),
    )
    return jax.shard_map(body, mesh=mesh, in_specs=in_specs, out_specs=out_specs, check_vma=False)
```

time: 760 us -> 604 us (0.79)
  Pallas kernels: 651 us -> 520 us
  local copies, waits for them, and re-layouts: 60.6 us -> 46.6 us
    pallas_call x1, Pallas kernels: 208 us -> 136 us  [gather_weights(): pl.pallas_call(functools.partial(gather_kernel, n_dp, n_tp, cut), out_sha...]
    pallas_call x7, Pallas kernels: 279 us -> 229 us  [call(): pl.pallas_call(kernel, grid_spec=spec, out_shape=tuple(outs), compiler_pa...]
    ppermute x6 -> x0, starting transfers between devices: 17 us -> none  [shift(): return lax.ppermute(x, axis, [(i, (i + step) % n) for i in range(n)])]
    dynamic_update_slice x8 -> x0, local copies, waits for them, and re-layouts: 14.3 us -> none  [the longest x4 8.23 us: to_slots(): whole = lax.dynamic_update_slice(whole, block[None], (source, 0, 0, 0))]
    all_to_all x0 -> x2, starting transfers between devices: none -> 10 us  [the longest x1 5.4 us: to_slots(): whole = lax.all_to_all(pieces, 'tp', 1, 0, tiled=False)]
    pallas_call x1, Pallas kernels: 164 us -> 155 us  [scatter_grads(): pl.pallas_call(functools.partial(scatter_kernel, n_dp, n_tp, cut), out_sh...]
    unnamed x37 -> x36, local copies, waits for them, and re-layouts: 14.7 us -> 20.1 us
  transfers between devices with their start and end apart: 10 -> 6, of which waited for: 1 -> 1; matrix products, arithmetic and copies ran while one was open for 7% -> 7% of each run, Pallas kernels for 29% -> 30%
where the time goes in v2:
time: 604 us; the launch traced here: 595 us
  Pallas kernels  520 us (86%)
  local copies, waits for them, and re-layouts  46.6 us (8%)
  starting transfers between devices  16.2 us (3%)
  other arithmetic  9.79 us (2%)
    pallas_call x7, Pallas kernels, call(): pl.pallas_call(kernel, grid_spec=spec, out_shape=tuple(outs), compiler_pa...  229 us
    pallas_call x1, Pallas kernels, scatter_grads(): pl.pallas_call(functools.partial(scatter_kernel, n_dp, n_tp, cut), out_sh...  155 us
    pallas_call x1, Pallas kernels, gather_weights(): pl.pallas_call(functools.partial(gather_kernel, n_dp, n_tp, cut), out_sha...  136 us
    unnamed x36, local copies, waits for them, and re-layouts  20.1 us
  transfers between devices with their start and end apart: 6, of which 1 were waited for; matrix products, arithmetic and copies ran while one was open for 7% of the time, Pallas kernels for 30%

profile of v2, /device:TPU:0, one launch (start us, length us, event | category | flops | bytes accessed | tf_op | source)
XLA Modules:
  0.0 594.7 jit_solution(8043059215953902125)
XLA Ops:
  1.7 3.4 collective-permute-start
  7.7 4.0 copy.74
  17.1 136.3 %gather_weights.1 = (bf16[8,4,288,768]{3,2,1,0:T(8,128)(2,1)}, bf16[8,912,768]{2,1,0:T(8,128)(2,1)}, bf16[2,1024,768]{2,1,0:T(8,128)(2,1)S(1)}) custom-call(bf16[288,768]{1,0:T(8,128)(2,1)S(1)} %pad_maximum_fusion.1.ff_in, bf16[1344,128]{1,0:T(8,128)(2,1)S(1)} %fusion.3.a_in, bf16[16,768]{1,0:T(8,128)(2,1)S(1)} %pad.5.vec_in, bf16[4,2,256,768]{3,2,1,0:T(8,128)(2,1)} %bitcast.71), custom_call_target="tpu_custom_call" | custom-call | tf_op jit(solution)/shard_map/gather_weights/pallas_call | solution.py:862
  153.4 1.7 copy-done.2
  155.1 4.7 all-to-all-start.1
  161.2 12.5 %project.1 = (bf16[2,1024,768]{2,1,0:T(8,128)(2,1)}, bf16[2,1024,768]{2,1,0:T(8,128)(2,1)}, bf16[2,1024,768]{2,1,0:T(8,128)(2,1)}, f32[2,8,768]{2,1,0:T(8,128)}, f32[2,8,768]{2,1,0:T(8,128)}) custom-call(s32[2]{0:T(128)} %dynamic_slice.15.lens, bf16[2,1024,768]{2,1,0:T(8,128)(2,1)} %copy-done.2, ...), custom_call_target="tpu_custom_call" | custom-call | flops 4831838208 | bytes 46350336 | tf_op jit(solution)/shard_map/project/pallas_call | solution.py:325
  173.8 21.8 %spectral.1 = (bf16[2,2048,768]{2,1,0:T(8,128)(2,1)}, bf16[2,1024,768]{2,1,0:T(8,128)(2,1)}, bf16[2,1024,768]{2,1,0:T(8,128)(2,1)}) custom-call(s32[2]{0:T(128)} %dynamic_slice.15.lens, bf16[2,1024,768]{2,1,0:T(8,128)(2,1)} %get-tuple-element.57.refs_0_, bf16[2,1024,768]{2,1,0:T(8,128)(2,1)} %get-tuple-element.58.refs_1_.gating, ...), custom_call_target="tpu_custom_call" | custom-call | flops 12884901888 | bytes 67944448 | tf_op jit(solution)/shard_map/spectral/pallas_call | solution.py:325
  195.6 52.1 %feed.1 = (f32[2,1024,768]{2,1,0:T(8,128)}, bf16[2,1024,768]{2,1,0:T(8,128)(2,1)}, bf16[2,4,1024,768]{3,2,1,0:T(8,128)(2,1)}, bf16[2,4,1024,768]{3,2,1,0:T(8,128...) custom-call(s32[2]{0:T(128)} %dynamic_slice.15.lens, bf16[2,1024,768]{2,1,0:T(8,128)(2,1)} %copy-done.2, ...), custom_call_target="tpu_custom_call" | custom-call | flops 31406948352 | bytes 110346240 | tf_op jit(solution)/shard_map/feed/pallas_call | solution.py:325
  247.7 6.7 %copy.65 = bf16[1,2,4,256,768]{4,1,3,0,2:T(2,128)(2,1)} copy(bf16[1,2,4,256,768]{4,3,2,1,0:T(8,128)(2,1)} %bitcast.81) | data formatting | bytes 6291456 | tf_op jit(solution)/shard_map/broadcast_in_dim;reshape | solution.py:1309
  254.4 5.4 all-to-all-start
  259.8 4.1 copy.66
  263.9 73.9 %feed_back.1 = (f32[2,1024,768]{2,1,0:T(8,128)}, bf16[8,4,96,768]{3,2,1,0:T(8,128)(2,1)}, bf16[8,4,96,768]{3,2,1,0:T(8,128)(2,1)}, bf16[8,4,96,768]{3,2,1,0:T(8,128)(2,1)}) custom-call(s32[2]{0:T(128)} %dynamic_slice.15.lens, bf16[2,1024,768]{2,1,0:T(8,128)(2,1)} %bitcast.72, bf16[2,1024,768]{2,1,0:T(8,128)(2,1)} %get-tuple-element.64.n2, ...), custom_call_target="tpu_custom_call" | custom-call | flops 57982058496 | bytes 106954752 | tf_op jit(solution)/shard_map/feed_back/pallas_call | solution.py:325
  337.8 18.9 %branch_back.1 = (f32[2,1024,768]{2,1,0:T(8,128)}, bf16[2,1024,768]{2,1,0:T(8,128)(2,1)}, bf16[2,1024,768]{2,1,0:T(8,128)(2,1)}, bf16[8,96,768]{2,1,0:T(8,128)(2,1)}, f32[8,768]{1,0:T(8,128)}) custom-call(s32[2]{0:T(128)} %dynamic_slice.15.lens, f32[2,1024,768]{2,1,0:T(8,128)} %get-tuple-element.68.e, f32[2,1024,768]{2,1,0:T(8,128)} %get-tuple-element.69.middle, ...), custom_call_target="tpu_custom_call" | custom-call | flops 4831838208 | bytes 50208768 | tf_op jit(solution)/shard_map/branch_back/pallas_call | solution.py:325
  356.6 25.9 %spectral_back.1 = (bf16[2,1024,768]{2,1,0:T(8,128)(2,1)}, bf16[8,512,768]{2,1,0:T(8,128)(2,1)}, f32[2,8,768]{2,1,0:T(8,128)}) custom-call(s32[2]{0:T(128)} %dynamic_slice.15.lens, bf16[2,1024,768]{2,1,0:T(8,128)(2,1)} %get-tuple-element.76.cg, bf16[2,2048,768]{2,1,0:T(8,128)(2,1)} %get-tuple-element.77.spec, f32[2,8,768]{2,1,0:T(8,128)} %get-tuple-element.59.refs_2_.mixing, ...), custom_call_target="tpu_custom_call" | custom-call | flops 12884901888 | bytes 67993600 | tf_op jit(solution)/shard_map/spectral_back/pallas_call | solution.py:325
  382.5 23.5 %input_back.1 = (bf16[2,1024,768]{2,1,0:T(8,128)(2,1)}, bf16[8,384,768]{2,1,0:T(8,128)(2,1)}, f32[16,768]{1,0:T(8,128)}) custom-call(s32[2]{0:T(128)} %dynamic_slice.15.lens, bf16[2,1024,768]{2,1,0:T(8,128)(2,1)} %get-tuple-element.78.vg, bf16[2,1024,768]{2,1,0:T(8,128)(2,1)} %get-tuple-element.79.gtg, bf16[2,1024,768]{2,1,0:T(8,128)(2,1)} %get-tuple-element.80.n1, ...), custom_call_target="tpu_custom_call" | custom-call | flops 9663676416 | bytes 61759488 | tf_op jit(solution)/shard_map/input_back/pallas_call | solution.py:325
  406.0 155.2 %scatter_grads.1 = (bf16[8,3,96,768]{3,2,1,0:T(8,128)(2,1)}, f32[1344,128]{1,0:T(8,128)}, f32[16,768]{1,0:T(8,128)}, bf16[4,2,256,768]{3,2,1,0:T(8,128)(2,1)}) custom-call(bf16[4,2,4,96,768]{4,3,2,1,0:T(8,128)(2,1)} %bitcast.75, bf16[4,2,4,96,768]{4,3,2,1,0:T(8,128)(2,1)} %bitcast.76, bf16[4,2,4,96,768]{4,3,2,1,0:T(8,128)(2,1)} %bitcast.77, ...), custom_call_target="tpu_custom_call" | custom-call | tf_op jit(solution)/shard_map/scatter_grads/pallas_call | solution.py:1171
  563.8 2.1 collective-permute-start.3
  566.0 2.2 fusion.16
  568.2 1.7 bitcast_convert_fusion
  569.9 1.7 bitcast_convert_fusion.1
  571.5 1.7 bitcast_convert_fusion.2
  573.2 1.5 dynamic-slice_bitcast_fusion
  576.2 6.8 %copy.71 = bf16[4,256,2,768]{3,2,1,0:T(2,128)(2,1)} copy(bf16[4,256,2,768]{3,1,2,0:T(8,128)(2,1)} %bitcast.80) | data formatting | bytes 6291456
  588.4 5.8 copy.76
  (87 shorter events, 19.7 us)
Async XLA Ops:
  0.6 11.2 %copy-start = (bf16[768,768]{1,0:T(8,128)(2,1)S(1)}, bf16[768,768]{1,0:T(8,128)(2,1)}, u32[]{:S(2)}) copy-start(bf16[768,768]{1,0:T(8,128)(2,1)} %param.31) | copy-start | bytes 3538948
  1.7 13.2 %collective-permute-start = (bf16[2,2,128,192]{2,3,1,0:T(8,128)(2,1)S(1)}, bf16[2,2,128,192]{2,3,1,0:T(8,128)(2,1)S(1)}, u32[]{:S(2)}, u32[]{:S(2)}) collective-permute-start(bf16[2,2,128,192]{2,3,1,0:T(8,128)(2,1)S(1)} %fusion.9), channel_id=1, source_target_pairs={{0,28},{4,24},{8,20},{12,16},{16,12},{20,8},{24,4},{28,0},{1,29},{... | collective-permute-start | bytes 589832 | tf_op jit(solution)/shard_map/ppermute | solution.py:1257
  6.1 8.7 %collective-permute-start.1 = (bf16[2,2,1,192]{2,3,1,0:T(8,128)(2,1)S(1)}, bf16[2,2,1,192]{2,3,1,0:T(8,128)(2,1)S(1)}, u32[]{:S(2)}, u32[]{:S(2)}) collective-permute-start(bf16[2,2,1,192]{2,3,1,0:T(8,128)(2,1)S(1)} %pad_maximum_fusion.6), channel_id=1, source_target_pairs={{4,28},{8,24},{12,20},{20,12},{24,8},{28,4},{0,16},{16,0},{5,29},{... | collective-permute-start | bytes 4616 | tf_op jit(solution)/shard_map/ppermute | solution.py:1258
  7.6 4.2 copy-start.6
  7.6 6.0 %copy-start.7 = (bf16[3,96]{1,0:T(4,128)(2,1)S(1)}, bf16[3,96]{1,0:T(4,128)(2,1)}, u32[]{:S(2)}) copy-start(bf16[3,96]{1,0:T(4,128)(2,1)} %param.24) | copy-start | bytes 1732
  7.6 6.0 %copy-start.8 = (bf16[96]{0:T(256)(128)(2,1)S(1)}, bf16[96]{0:T(256)(128)(2,1)}, u32[]{:S(2)}) copy-start(bf16[96]{0:T(256)(128)(2,1)} %param.21) | copy-start | bytes 580
  7.6 6.0 %copy-start.9 = (bf16[96]{0:T(256)(128)(2,1)S(1)}, bf16[96]{0:T(256)(128)(2,1)}, u32[]{:S(2)}) copy-start(bf16[96]{0:T(256)(128)(2,1)} %param.22) | copy-start | bytes 580
  7.6 6.0 %copy-start.10 = (bf16[96]{0:T(256)(128)(2,1)S(1)}, bf16[96]{0:T(256)(128)(2,1)}, u32[]{:S(2)}) copy-start(bf16[96]{0:T(256)(128)(2,1)} %param.29) | copy-start | bytes 580
  7.6 6.0 %copy-start.11 = (bf16[96]{0:T(256)(128)(2,1)S(1)}, bf16[96]{0:T(256)(128)(2,1)}, u32[]{:S(2)}) copy-start(bf16[96]{0:T(256)(128)(2,1)} %param.30) | copy-start | bytes 580
  7.6 6.0 %copy-start.12 = (bf16[96]{0:T(256)(128)(2,1)S(1)}, bf16[96]{0:T(256)(128)(2,1)}, u32[]{:S(2)}) copy-start(bf16[96]{0:T(256)(128)(2,1)} %param.28) | copy-start | bytes 580
  7.6 6.0 %copy-start.13 = (bf16[96]{0:T(256)(128)(2,1)S(1)}, bf16[96]{0:T(256)(128)(2,1)}, u32[]{:S(2)}) copy-start(bf16[96]{0:T(256)(128)(2,1)} %param.34) | copy-start | bytes 580
  7.6 7.4 %copy-start.3 = (bf16[2,256,192]{1,2,0:T(8,128)(2,1)S(1)}, bf16[2,256,192]{1,2,0:T(8,128)(2,1)}, u32[]{:S(2)}) copy-start(bf16[2,256,192]{1,2,0:T(8,128)(2,1)} %param.25) | copy-start | bytes 589828
  7.7 7.4 %copy-start.4 = (bf16[2,256,192]{1,2,0:T(8,128)(2,1)S(1)}, bf16[2,256,192]{1,2,0:T(8,128)(2,1)}, u32[]{:S(2)}) copy-start(bf16[2,256,192]{1,2,0:T(8,128)(2,1)} %param.26) | copy-start | bytes 589828
  12.9 4.0 copy-start.5
  153.4 1.7 copy-start.2
  155.1 99.4 %all-to-all-start.1 = ((bf16[4,2,1,256,768]{4,1,3,2,0:T(2,128)(2,1)}), bf16[4,2,1,256,768]{4,1,3,2,0:T(2,128)(2,1)}, u32[]{:S(2)}, u32[]{:S(2)}) async-start(bf16[4,2,1,256,768]{4,1,3,2,0:T(2,128)(2,1)} %bitcast.79), calls=%async_computation.1 | async-start | bytes 6291456 | tf_op jit(solution)/shard_map/all_to_all | solution.py:1305
  254.4 102.2 %all-to-all-start = ((bf16[1,2,4,256,768]{4,1,3,0,2:T(2,128)(2,1)}), bf16[1,2,4,256,768]{4,1,3,0,2:T(2,128)(2,1)}, u32[]{:S(2)}, u32[]{:S(2)}) async-start(bf16[1,2,4,256,768]{4,1,3,0,2:T(2,128)(2,1)} %copy.65), calls=%async_computation | async-start | bytes 6291456 | tf_op jit(solution)/shard_map/all_to_all | solution.py:1309
  563.8 20.6 %collective-permute-start.2 = (bf16[2,2,128,192]{2,3,1,0:T(8,128)(2,1)S(1)}, bf16[2,2,128,192]{2,3,1,0:T(8,128)(2,1)S(1)}, u32[]{:S(2)}, u32[]{:S(2)}) collective-permute-start(bf16[2,2,128,192]{2,3,1,0:T(8,128)(2,1)S(1)} %copy.67), channel_id=1, source_target_pairs={{0,28},{4,24},{8,20},{12,16},{16,12},{20,8},{24,4},{28,0},{1,29},{... | collective-permute-start | bytes 589832 | tf_op jit(solution)/shard_map/ppermute | solution.py:1338
  563.8 20.5 %collective-permute-start.3 = (bf16[2,2,1,192]{2,3,1,0:T(8,128)(2,1)S(1)}, bf16[2,2,1,192]{2,3,1,0:T(8,128)(2,1)S(1)}, u32[]{:S(2)}, u32[]{:S(2)}) collective-permute-start(bf16[2,2,1,192]{2,3,1,0:T(8,128)(2,1)S(1)} %bitcast.92), channel_id=1, source_target_pairs={{4,28},{8,24},{12,20},{20,12},{24,8},{28,4},{0,16},{16,0},{5,29},{... | collective-permute-start | bytes 4616 | tf_op jit(solution)/shard_map/ppermute | solution.py:1342
  576.2 8.5 %copy-start.14 = (pred[256]{0:T(512)(128)(4,1)S(1)}, pred[256]{0:T(512)(128)(4,1)}, u32[]{:S(2)}) copy-start(pred[256]{0:T(512)(128)(4,1)} %compare_and_fusion) | copy-start | bytes 772
  588.4 5.8 copy-start.1

commit v3 on v2

--- a/solution.py
+++ b/solution.py
@@ -10,7 +10,7 @@
 from jax.sharding import PartitionSpec as P
 
 EPSILON = 1e-05
-ONE_TABLE = True
+ROWS = 64
 BF = jnp.bfloat16
 F32 = jnp.float32
 GELU_A = math.sqrt(2.0 / math.pi)
@@ -99,13 +99,12 @@
     return jnp.where(r == 0, jnp.broadcast_to(v, (rows, v.shape[1])), 0.0)
 
 
-def project_kernel(tile, lens, x, wv, wg, wc, vec, n1, values, gating, nsum, mixing):
+def project_kernel(tile, lens, x, wv, wg, wc, vec, values, gating, nsum, mixing):
     s, t = pl.program_id(0), pl.program_id(1)
     count = lens[s]
     valid = live(tile, t * tile, count)
     std, _ = standardize(x[0].astype(F32))
     normed = (std * vec[0:1] + vec[1:2]).astype(BF)
-    n1[0] = normed
     values[0] = ((mm(normed, joined(wv)) + vec[6:7]) * valid).astype(BF)
     gating[0] = (mm(normed, joined(wg)) + vec[7:8]).astype(BF)
     part = top_row(jnp.sum(normed.astype(F32) * valid, axis=0, keepdims=True))
@@ -155,7 +154,7 @@
     s, t = pl.program_id(0), pl.program_id(1)
     valid = live(tile, t * tile, lens[s])
     mid = x[0].astype(F32) + valid * (mm_nt(gated[0], joined(w_out)) + vec[4:5])
-    middle[0] = mid
+    middle[0] = mid.astype(BF)
     std, _ = standardize(mid)
     normed = (std * vec[2:3] + vec[3:4]).astype(BF)
     n2[0] = normed
@@ -169,16 +168,16 @@
         h = (a * up).astype(BF)
         hidden[0, p] = h
         feed += mm(h, joined(wd.at[:, p]))
-    out[0] = (mid + valid * (feed + vec[5:6])).astype(BF)
-
-
-def feed_back_kernel(tile, lens, cot, n2, act, side, hidden, wg, wu, wd, e_out, d_gate, d_up, d_down, acc_g, acc_u, acc_d, fgs, ggs, ugs):
+    out[:, 0] = (mid + valid * (feed + vec[5:6])).astype(BF).reshape(out.shape[0], out.shape[2], out.shape[3])
+
+
+def feed_back_kernel(tile, lens, cot, n2, act, side, hidden, wg, wu, wd, e_out, d_gate, d_up, d_down, e_acc, acc_g, acc_u, acc_d, fgs, ggs, ugs):
     p, s = pl.program_id(0), pl.program_id(1)
     n = cot.shape[1]
 
     @pl.when(p == 0)
     def _():
-        e_out[s] = jnp.zeros(e_out.shape[1:], F32)
+        e_acc[s] = jnp.zeros(e_acc.shape[1:], F32)
 
     @pl.when(s == 0)
     def _():
@@ -195,19 +194,27 @@
         ugs[here] = (hg * act[0, 0, here].astype(F32)).astype(BF)
     for i in range(n // tile):
         here = pl.ds(i * tile, tile)
-        e_out[s, here] += mm_nt(ggs[here], gate) + mm_nt(ugs[here], up)
+        e_acc[s, here] += mm_nt(ggs[here], gate) + mm_nt(ugs[here], up)
     normed = n2[0]
     acc_g[...] += mm_tn(normed, ggs[...])
     acc_u[...] += mm_tn(normed, ugs[...])
     acc_d[...] += mm_tn(hidden[0, 0], fgs[...])
 
+    @pl.when(p == pl.num_programs(0) - 1)
+    def _():
+        e_out[0] = e_acc[s].astype(BF)
+
     @pl.when(s == pl.num_programs(1) - 1)
     def _():
         for acc, out in zip((acc_g, acc_u, acc_d), (d_gate, d_up, d_down)):
             out[:, 0] = acc[...].astype(BF).reshape(out.shape[0], out.shape[2], out.shape[3])
 
 
-def branch_back_kernel(tile, lens, e, middle, cot, gated, gating, conv, w_out, vec, mg_out, cg, gtg, d_out, sums, acc):
+def eights(v):
+    return jnp.sum(v.reshape(-1, 8, v.shape[-1]), axis=0)
+
+
+def branch_back_kernel(tile, lens, e, middle, cot, gating, conv, w_out, vec, mg_out, cg, gtg, d_out, sums, acc, bgs, gts, part_sums):
     s, t = pl.program_id(0), pl.program_id(1)
     begin = (s == 0) & (t == 0)
     end = (s == pl.num_programs(0) - 1) & (t == pl.num_programs(1) - 1)
@@ -215,30 +222,40 @@
     @pl.when(begin)
     def _():
         acc[...] = jnp.zeros(acc.shape, F32)
-        sums[...] = jnp.zeros(sums.shape, F32)
-
-    valid = live(tile, t * tile, lens[s])
-    up = cot[0].astype(F32)
-    fg = (up * valid).astype(BF).astype(F32)
-    std, inverse = standardize(middle[0])
-    grad = e[0]
-    mg = up + norm_back(grad, vec[2:3], std, inverse)
-    mg_out[0] = mg
-    bgr = (mg * valid).astype(BF)
-    ggr = mm(bgr, joined(w_out))
-    cg[0] = (ggr * gating[0].astype(F32)).astype(BF)
-    gtg[0] = (ggr * conv[0].astype(F32)).astype(BF)
-    part = mm_tn(bgr, gated[0])
-    rows = [grad * std, grad, bgr.astype(F32), fg]
-    rows = [jnp.sum(r, axis=0, keepdims=True) for r in rows]
-
-    acc[...] += part
-    for i, r in enumerate(rows):
-        sums[i : i + 1] += r
+        part_sums[...] = jnp.zeros(part_sums.shape, F32)
+
+    count = lens[s]
+    gain = vec[2:3]
+    step = min(ROWS, tile)
+    for i in range(tile // step):
+        here = pl.ds(i * step, step)
+        valid = live(step, t * tile + i * step, count)
+        up = cot[0, here].astype(F32)
+        std, inverse = standardize(middle[0, here].astype(F32))
+        grad = e[0, here].astype(F32)
+        mg = up + norm_back(grad, gain, std, inverse)
+        mg_out[0, here] = mg.astype(BF)
+        bgr = (mg * valid).astype(BF)
+        bgs[here] = bgr
+        fg = (up * valid).astype(BF).astype(F32)
+        for j, v in enumerate((grad * std, grad, bgr.astype(F32), fg)):
+            part_sums[j] += eights(v)
+    ggr = mm(bgs[...], joined(w_out))
+    for i in range(tile // step):
+        here = pl.ds(i * step, step)
+        gate, out = gating[0, here].astype(F32), conv[0, here].astype(F32)
+        g = ggr[i * step : (i + 1) * step]
+        cg[0, here] = (g * gate).astype(BF)
+        gtg[0, here] = (g * out).astype(BF)
+        gts[here] = (out * gate).astype(BF)
+    acc[...] += mm_tn(bgs[...], gts[...])
 
     @pl.when(end)
     def _():
         d_out[...] = acc[...].astype(BF).reshape(d_out.shape)
+        sums[...] = jnp.zeros(sums.shape, F32)
+        for j in range(4):
+            sums[j : j + 1] = jnp.sum(part_sums[j], axis=0, keepdims=True)
 
 
 def spectral_back_kernel(slots, scale, lens, cg, spec, mixing, table, f0, f1, f2, f3, vg, fgrad, cgv):
@@ -274,7 +291,7 @@
             fgrad[j, pl.ds(i * size, size)] = total[i][k * size : (k + 1) * size].astype(BF)
 
 
-def input_back_kernel(tile, lens, vg, gtg, n1, x, mg, nsum, cgv, wv, wg, wc, d_out, sums_in, vec, ig, d_in, sums, acc_v, acc_g, acc_c):
+def input_back_kernel(tile, lens, vg, gtg, x, mg, nsum, cgv, wv, wg, wc, d_out, sums_in, vec, ig, d_in, sums, acc_v, acc_g, acc_c):
     s, t = pl.program_id(0), pl.program_id(1)
     begin = (s == 0) & (t == 0)
     end = (s == pl.num_programs(0) - 1) & (t == pl.num_programs(1) - 1)
@@ -292,8 +309,8 @@
     vgb, gtb = vg[0], gtg[0]
     e = mm_nt(vgb, joined(wv)) + mm_nt(gtb, joined(wg)) + valid * cvec
     std, inverse = standardize(x[0].astype(F32))
-    ig[0] = (mg[0] + norm_back(e, vec[0:1], std, inverse)).astype(BF)
-    normed = n1[0]
+    ig[0] = (mg[0].astype(F32) + norm_back(e, vec[0:1], std, inverse)).astype(BF)
+    normed = (std * vec[0:1] + vec[1:2]).astype(BF)
     part_v, part_g = mm_tn(normed, vgb), mm_tn(normed, gtb)
     rows = [e * std, e, vgb.astype(F32), gtb.astype(F32)]
     rows = [jnp.sum(r, axis=0, keepdims=True) for r in rows]
@@ -357,8 +374,8 @@
         lens,
         [x, aw, aw, aw, vec],
         [tok] + weights + [once(vec.shape, (0, 0))],
-        [sd, sd, sd, row, row],
-        (tok, tok, tok, one, one),
+        [sd, sd, row, row],
+        (tok, tok, one, one),
         [],
         4 * own * n * width * width,
         "project",
@@ -396,23 +413,23 @@
     )
 
 
-def feed(x, gated, lens, aw, ffw, vec):
+def feed(x, gated, lens, aw, ws, n_tp, hid, vec):
     own, n, width = x.shape
     tile = min(512, n)
-    nd, n_tp, _, hid = ffw[0].shape
+    local = n // n_tp
     r = width // aw.shape[0]
     tok = pl.BlockSpec((1, tile, width), lambda s, t, *_: (s, t, 0))
     wide = pl.BlockSpec((1, n_tp, tile, hid), lambda s, t, *_: (s, 0, t, 0))
-    ws = [once(shape, (0, 0, at, 0)) for _, shape, at in ffw[1]]
+    parts = pl.BlockSpec((tile // local, 1, local, width), lambda s, t, *_: (t, s, 0, 0))
     big = shape_of((own, n_tp, n, hid), BF)
     return call(
         functools.partial(feed_kernel, tile, n_tp),
         (own, n // tile),
         lens,
-        [x, gated, aw] + [w for w, _, _ in ffw[1]] + [vec],
-        [tok, tok, once((aw.shape[0], r, width), (0, 3, 0))] + ws + [once(vec.shape, (0, 0))],
-        [shape_of(x.shape, F32), shape_of(x.shape, BF), big, big, big, shape_of(x.shape, BF)],
-        (tok, tok, wide, wide, wide, tok),
+        [x, gated, aw] + [w[0] for w in ws] + [vec],
+        [tok, tok, once((aw.shape[0], r, width), (0, 3, 0))] + [once(w[1], w[2]) for w in ws] + [once(vec.shape, (0, 0))],
+        [shape_of(x.shape, BF), shape_of(x.shape, BF), big, big, big, shape_of((n_tp, own, local, width), BF)],
+        (tok, tok, wide, wide, wide, parts),
         [],
         2 * own * n * width * (width + 3 * n_tp * hid),
         "feed",
@@ -426,20 +443,22 @@
     tile = min(512, n)
     tok = pl.BlockSpec((1, n, width), lambda p, s, *_: (s, 0, 0))
     wide = pl.BlockSpec((1, 1, n, hid), lambda p, s, *_: (s, p, 0, 0))
-    ws = [
-        pl.BlockSpec((shape[0], 1) + shape[2:], lambda p, s, *_, at=at: (0, p, at, 0)) for _, shape, at in ffw[1]
-    ]
-    d_specs = [pl.BlockSpec((shape[0], 1) + shape[2:], lambda p, s, *_: (0, p, 0, 0)) for _, shape, _ in ffw[1]]
-    d_shapes = [shape_of(shape, BF) for _, shape, _ in ffw[1]]
+    w_specs = [pl.BlockSpec(w[3], lambda p, s, *_, f=w[4]: f(p)) for w in ffw]
+    nd = [next(v for v in w[3]) for w in ffw]
+    sides = [(width, hid), (width, hid), (hid, width)]
+    shapes = [(k, n_tp, a // k, b) for k, (a, b) in zip(nd, sides)]
+    d_specs = [pl.BlockSpec((shape[0], 1) + shape[2:], lambda p, s, *_: (0, p, 0, 0)) for shape in shapes]
+    d_shapes = [shape_of(shape, BF) for shape in shapes]
     return call(
         functools.partial(feed_back_kernel, tile),
         (n_tp, own),
         lens,
-        [cot, n2, act, side, hidden] + [w for w, _, _ in ffw[1]],
-        [tok, tok, wide, wide, wide] + ws,
-        [shape_of(cot.shape, F32)] + d_shapes,
-        (pl.BlockSpec(cot.shape, lambda *_: (0, 0, 0), pipeline_mode=pl.Buffered(1)), *d_specs),
+        [cot, n2, act, side, hidden] + [w[0] for w in ffw],
+        [tok, tok, wide, wide, wide] + w_specs,
+        [shape_of(cot.shape, BF)] + d_shapes,
+        (pl.BlockSpec((1, n, width), lambda p, s, *_: (jnp.where(p == n_tp - 1, s, 0), 0, 0)), *d_specs),
         [
+            pltpu.VMEM(cot.shape, F32),
             pltpu.VMEM((width, hid), F32),
             pltpu.VMEM((width, hid), F32),
             pltpu.VMEM((hid, width), F32),
@@ -453,7 +472,7 @@
     )
 
 
-def branch_back(e, middle, cot, gated, gating, conv, lens, aw, vec):
+def branch_back(e, middle, cot, gating, conv, lens, aw, vec):
     own, n, width = cot.shape
     tile = min(512, n)
     nd, r = aw.shape[0], width // aw.shape[0]
@@ -462,17 +481,22 @@
         functools.partial(branch_back_kernel, tile),
         (own, n // tile),
         lens,
-        [e, middle, cot, gated, gating, conv, aw, vec],
-        [tok] * 6 + [once((nd, r, width), (0, 3, 0)), once(vec.shape, (0, 0))],
+        [e, middle, cot, gating, conv, aw, vec],
+        [tok] * 5 + [once((nd, r, width), (0, 3, 0)), once(vec.shape, (0, 0))],
         [
-            shape_of(cot.shape, F32),
+            shape_of(cot.shape, BF),
             shape_of(cot.shape, BF),
             shape_of(cot.shape, BF),
             shape_of((nd, r, width), BF),
             shape_of((8, width), F32),
         ],
         (tok, tok, tok, pl.BlockSpec((nd, r, width), lambda *_: (0, 0, 0)), pl.BlockSpec((8, width), lambda *_: (0, 0))),
-        [pltpu.VMEM((width, width), F32)],
+        [
+            pltpu.VMEM((width, width), F32),
+            pltpu.VMEM((tile, width), BF),
+            pltpu.VMEM((tile, width), BF),
+            pltpu.VMEM((4, 8, width), F32),
+        ],
         4 * own * n * width * width,
         "branch_back",
     )
@@ -499,7 +523,7 @@
     )
 
 
-def input_back(vg, gtg, n1, x, mg, nsum, cgv, lens, aw, d_out, sums, vec):
+def input_back(vg, gtg, x, mg, nsum, cgv, lens, aw, d_out, sums, vec):
     own, n, width = x.shape
     tile = min(512, n)
     nd, r = aw.shape[0], width // aw.shape[0]
@@ -510,8 +534,8 @@
         functools.partial(input_back_kernel, tile),
         (own, n // tile),
         lens,
-        [vg, gtg, n1, x, mg, nsum, cgv, aw, aw, aw, d_out, sums, vec],
-        [tok] * 5 + [one] * 2 + weights + [once((nd, r, width), (0, 0, 0)), once((8, width), (0, 0)), once(vec.shape, (0, 0))],
+        [vg, gtg, x, mg, nsum, cgv, aw, aw, aw, d_out, sums, vec],
+        [tok] * 4 + [one] * 2 + weights + [once((nd, r, width), (0, 0, 0)), once((8, width), (0, 0)), once(vec.shape, (0, 0))],
         [shape_of(x.shape, BF), shape_of((nd, 4 * r, width), BF), shape_of((16, width), F32)],
         (tok, pl.BlockSpec((nd, 4 * r, width), lambda *_: (0, 0, 0)), pl.BlockSpec((16, width), lambda *_: (0, 0))),
         [pltpu.VMEM((width, width), F32)] * 3,
@@ -532,9 +556,9 @@
     return bits, bits[::-1]
 
 
-def greet(d, z, n_dp, n_tp):
+def greet(d, z, n_dp, n_tp, pairs=False):
     barrier = pltpu.get_barrier_semaphore()
-    count = 0
+    count = greet_pairs(d, z, n_dp) if pairs else 0
     step = 1
     while step < n_dp:
         pl.semaphore_signal(barrier, inc=1, device_id=(flip(d, step), z), device_id_type=MESH)
@@ -544,6 +568,23 @@
         pl.semaphore_signal(barrier, inc=1, device_id=(d, lax.rem(z + k, n_tp)), device_id_type=MESH)
         count += 1
     pl.semaphore_wait(barrier, count)
+
+
+def across_of(d, n):
+    return lax.rem(n - d, n) + (n // 2) * (1 - (d % (n // 2) + n // 2 - 1) // (n // 2)) * (1 - 2 * (d // (n // 2)))
+
+
+def one_hot(rows, cols, test):
+    r = lax.broadcasted_iota(jnp.int32, (rows, cols), 0)
+    c = lax.broadcasted_iota(jnp.int32, (rows, cols), 1)
+    return jnp.where(test(r, c), 1.0, 0.0).astype(BF)
+
+
+def greet_pairs(d, z, n_dp):
+    barrier = pltpu.get_barrier_semaphore()
+    for peer in (n_dp - 1 - d, across_of(d, n_dp)):
+        pl.semaphore_signal(barrier, inc=1, device_id=(peer, z), device_id_type=MESH)
+    return 2
 
 
 def remote(src, dst, send, recv, target):
@@ -717,50 +758,71 @@
 
 
 def gather_kernel(
-    n_dp, n_tp, cut, ff_in, a_in, vec_in, x_in, ff_out, a_out, x_out, a_z, a_nat, ones,
-    la_send, la_recv, lf_send, lf_recv, x_send, x_recv, s_send, s_recv, local,
+    n_dp, n_tp, cut, a_rows, mirror, w0, w1, w2, a_in, f_in, vec_in, x_in, ff_out, a_out, x_out, a_z, a_nat, ones, f_got, f_edge,
+    la_send, la_recv, lf_send, lf_recv, x_send, x_recv, s_send, s_recv, f_send, f_recv, local,
 ):
     d, z = lax.axis_index("dp"), lax.axis_index("tp")
     width = a_nat.shape[1]
     ch = width // n_tp
     rows = a_nat.shape[0] - vec_in.shape[0]
-    layout = Pack(rows, ch)
-    own_ff = pltpu.make_async_copy(ff_in, ff_out.at[d, z], local.at[0])
-    own_ff.start()
-    own_a = pltpu.make_async_copy(a_in, a_z.at[z], local.at[1])
+    layout = Pack(a_rows, ch)
+    own_ff = [pltpu.make_async_copy(w, ff_out.at[:, z, g], local.at[3 + g]) for g, w in enumerate((w0, w1, w2))]
+    for copy in own_ff:
+        copy.start()
+    own_a = pltpu.make_async_copy(a_in, a_z.at[z, pl.ds(0, layout.total)], local.at[1])
     own_a.start()
-    greet(d, z, n_dp, n_tp)
+    greet(d, z, n_dp, n_tp, mirror)
+    if mirror:
+        k = f_in.shape[2] // 2
+        swaps = [
+            remote(f_in.at[:, :, pl.ds(k, k)], f_got, f_send.at[0], f_recv.at[0], (n_dp - 1 - d, z)),
+            remote(f_in.at[:, :, pl.ds(0, k)], f_edge, f_send.at[1], f_recv.at[1], (across_of(d, n_dp), z)),
+        ]
+        turn = one_hot(k, k, lambda r, c: r + c == k)
+        corner = one_hot(k, k, lambda r, c: r + c == 0)
+        upper = d > n_dp - 1 - d
+        lane = lax.broadcasted_iota(jnp.int32, (1, k), 1)
+        special = jnp.logical_and(lane == 0, d == 0)
+        for copy in swaps:
+            copy.wait()
+        sums = []
+        for c in range(4):
+            low, high = f_in[c, :, :k], f_in[c, :, k:]
+            direct = jnp.where(upper, f_got[c], low).astype(F32)
+            image = mm(jnp.where(upper, low, f_got[c]), turn) + mm(jnp.where(upper, high, f_edge[c]), corner)
+            if c % 2 == 0:
+                nyquist = image
+                folded = jnp.where(special, direct, direct + image)
+            else:
+                folded = jnp.where(special, nyquist, direct - image)
+            a_z[z, pl.ds(layout.total + c * ch, ch)] = folded.astype(BF)
     line_a = Line(lambda s: a_z.at[s], d, z, n_tp, la_send, la_recv)
     line_f = Line(lambda s: ff_out.at[d, s], d, z, n_tp, lf_send, lf_recv)
     first, second = bit_orders(n_dp)
-    ff_rows = ff_in.shape[0]
-    ff_cut = ff_rows // 2 // 16 * 16
+    vec = w0.shape[1]
 
     def block_spreads(block):
         out = []
-        for h, (lo, count, order) in enumerate(((0, ff_cut, first), (ff_cut, ff_rows - ff_cut, second))):
+        for h, order in enumerate((first, second)):
             at = 2 + 2 * block + h
-            out.append(
-                Spread(
-                    lambda s, lo=lo, count=count: ff_out.at[s, block, pl.ds(lo, count)],
-                    order + [1], d, z, s_send.at[at], s_recv.at[at],
-                )
-            )
+            if vec % 32 == 0:
+                part = lambda s, h=h: ff_out.at[s, block, :, pl.ds(h * (vec // 2), vec // 2)]
+            else:
+                part = lambda s, h=h: ff_out.at[s, block, pl.ds(h, 1 + h)]
+            out.append(Spread(part, order + [1], d, z, s_send.at[at], s_recv.at[at]))
         return out
 
     own_a.wait()
     line_a.start(0)
-    own_ff.wait()
-    f_own = block_spreads(z)
-    for p in f_own:
-        p.start()
     fill_places(ones, layout, width, n_tp)
     for t in range(n_tp - 1):
         line_a.wait(t)
         if t + 1 < n_tp - 1:
             line_a.start(t + 1)
+    for copy in own_ff:
+        copy.wait()
     line_f.start(0)
-    half_rows = rows // 2
+    half_rows = a_rows // 2
     n_pieces = len(layout.pieces())
     size = chunk_of(half_rows)
     for side in range(2):
@@ -777,6 +839,13 @@
                     total += mm(a_z[s, pl.ds(packed + i * size, size)], ones[s * n_pieces + j])
             a_nat[pl.ds(side * half_rows + i * size, size)] = total.astype(BF)
 
+    if mirror:
+        for c in range(4):
+            total = jnp.zeros((k, width), F32)
+            for s in range(n_tp):
+                place = one_hot(ch, width, lambda r, col, s=s: col - r == s * ch)
+                total += mm_tn(a_z[s, pl.ds(layout.total + c * ch, ch)], place)
+            a_nat[pl.ds(a_rows + c * k, k)] = total.astype(BF)
     a_nat[rows:] = vec_in[...]
     put = pltpu.make_async_copy(a_nat, a_out.at[d], local.at[2])
     put.start()
@@ -796,7 +865,6 @@
             if p.stage < stages:
                 p.start()
 
-    advance(f_own)
     blocks = []
     for t in range(n_tp - 1):
         line_f.wait(t)
@@ -813,10 +881,9 @@
 
         if t == 0:
             advance(sa)
-            advance(f_own)
     size = x_in.shape[2]
     here = pl.ds(z * size, size)
-    own_x = pltpu.make_async_copy(x_in.at[z], x_out.at[:, here], local.at[3])
+    own_x = pltpu.make_async_copy(x_in.at[z], x_out.at[:, here], local.at[0])
     own_x.start()
     zx = []
     for k in range(1, n_tp):
@@ -831,10 +898,7 @@
 
         if stage + 1 < stages:
             advance(sa)
-        if stage == 0:
-            for p in f_own:
-                p.wait()
-    for p in sa + f_own:
+    for p in sa:
         p.drain()
     for exists, group in blocks:
 
@@ -852,26 +916,31 @@
     line_f.drain()
 
 
-def gather_weights(ff_in, a_in, a_rows, vec_in, x_in, n_dp, n_tp):
+def gather_weights(ff, a_in, a_rows, f_in, vec_in, x_in, n_dp, n_tp):
     width = vec_in.shape[1]
-    rows = a_rows
+    mirror = f_in.shape[2] % 256 == 0
+    ch = width // n_tp
+    rows = a_rows + (2 * f_in.shape[2] if mirror else 0)
+    k = f_in.shape[2] // 2
     total = rows + vec_in.shape[0]
     cut = total // 2 // 16 * 16
     anyspace = pl.BlockSpec(memory_space=pl.ANY)
     vmem = pl.BlockSpec(memory_space=pltpu.VMEM)
     return pl.pallas_call(
-        functools.partial(gather_kernel, n_dp, n_tp, cut),
+        functools.partial(gather_kernel, n_dp, n_tp, cut, a_rows, mirror),
         out_shape=(
-            jax.ShapeDtypeStruct((n_dp, n_tp) + ff_in.shape, BF),
+            jax.ShapeDtypeStruct((n_dp, n_tp, 3) + ff[0].shape[1:], BF),
             jax.ShapeDtypeStruct((n_dp, total, width), BF),
             jax.ShapeDtypeStruct((x_in.shape[1], n_tp * x_in.shape[2], width), BF),
         ),
-        in_specs=[anyspace, anyspace, vmem, anyspace],
+        in_specs=[anyspace] * 4 + [vmem, vmem, anyspace],
         out_specs=(anyspace, anyspace, anyspace),
         scratch_shapes=[
-            pltpu.VMEM((n_tp,) + a_in.shape, BF),
+            pltpu.VMEM((n_tp, a_in.shape[0] + (4 * ch if mirror else 0), 128), BF),
             pltpu.VMEM((total, width), BF),
-            pltpu.VMEM((n_tp * len(Pack(rows, width // n_tp).pieces()), 128, width), BF),
+            pltpu.VMEM((n_tp * len(Pack(a_rows, ch).pieces()), 128, width), BF),
+            pltpu.VMEM((4, ch, k), BF),
+            pltpu.VMEM((4, ch, k), BF),
             pltpu.SemaphoreType.DMA((2, n_tp - 1)),
             pltpu.SemaphoreType.DMA((2, n_tp - 1)),
             pltpu.SemaphoreType.DMA((2, n_tp - 1)),
@@ -880,13 +949,15 @@
             pltpu.SemaphoreType.DMA((n_tp - 1,)),
             pltpu.SemaphoreType.DMA((2 + 2 * n_tp, n_dp - 1)),
             pltpu.SemaphoreType.DMA((2 + 2 * n_tp, n_dp - 1)),
-            pltpu.SemaphoreType.DMA((4,)),
+            pltpu.SemaphoreType.DMA((2,)),
+            pltpu.SemaphoreType.DMA((2,)),
+            pltpu.SemaphoreType.DMA((6,)),
         ],
         compiler_params=pltpu.CompilerParams(
             collective_id=0, has_side_effects=True, vmem_limit_bytes=48 * 1024 * 1024
         ),
         name="gather_weights",
-    )(ff_in, a_in, vec_in, x_in)
+    )(*ff, a_in, f_in, vec_in, x_in)
 
 
 class Fold:
@@ -943,7 +1014,7 @@
     def _copy(self, way, block):
         return pltpu.make_async_remote_copy(
             src_ref=self.mine(block),
-            dst_ref=self.got.at[way, block],
+            dst_ref=self.got(way, block),
             send_sem=self.send.at[way, block],
             recv_sem=self.recv.at[way, block],
             device_id=(self.d, self.z - 1 if way == 0 else self.z + 1),
@@ -956,12 +1027,12 @@
         @pl.when((block <= z) & (z < n - 1))
         def _():
             self._copy(0, block).wait_recv()
-            add(self.mine(block), self.got.at[0, block])
+            add(self.mine(block), self.got(0, block))
 
         @pl.when((block >= z) & (z > 0))
         def _():
             self._copy(1, block).wait_recv()
-            add(self.mine(block), self.got.at[1, block])
+            add(self.mine(block), self.got(1, block))
 
     def give(self, block):
         @pl.when(block < self.z)
@@ -983,15 +1054,17 @@
 
 
 def scatter_kernel(
-    n_dp, n_tp, cut, g0, g1, g2, a0, a1, v_in, x_in, ff_out, a_out, v_out, x_out,
-    ff_mine, a_mine, ff_core, a_core, ff_two, a_two, a_cols, ff_got, a_got, v_got, ones,
-    load, core_send, core_recv, f_send, f_recv, h_send, h_recv, lf_send, lf_recv, la_send, la_recv,
-    z_send, z_recv, s_send, s_recv, v_send, v_recv, local,
+    n_dp, n_tp, cut, mirror, g0, g1, g2, a0, a1, v_in, x_in, ff_out, a_out, f_out, v_out, x_out,
+    ff_mine, a_mine, ff_core, a_core, ff_two, a_two, a_cols, ff_got, a_got, v_got, ones, f_own, f_got, f_edge,
+    load, core_send, core_recv, f_send, f_recv, h_send, h_recv, lf_send, lf_recv, la_send, la_recv, lb_send, lb_recv,
+    z_send, z_recv, s_send, s_recv, v_send, v_recv, f_swap_send, f_swap_recv, local,
 ):
     d, z = lax.axis_index("dp"), lax.axis_index("tp")
     width = a0.shape[3]
     rows = a0.shape[2] + a1.shape[2]
-    layout = Pack(rows, width // n_tp)
+    ch = width // n_tp
+    a_rows = a0.shape[2] if mirror else rows
+    layout = Pack(a_rows, ch)
     vec = g0.shape[3]
     half = n_dp // 2
     side = d % 2
@@ -999,8 +1072,17 @@
     other = (flip(d, 1), z)
     late = z // (n_tp // 2)
     order = [n_tp - 1 - j + late * (2 * j - n_tp + 1) for j in range(n_tp)]
-    greet(d, z, n_dp, n_tp)
-    f_core, f_load = [], []
+    greet(d, z, n_dp, n_tp, mirror)
+    f_core, f_load, a_swap, a_load = [], [], [], []
+
+    def swap_a(g, src, at):
+        part = pl.ds(at, src.shape[2])
+        a_swap.append(remote(src.at[:, 1 - side], a_core.at[:, part], core_send.at[3, g], core_recv.at[3, g], other))
+        copy = pltpu.make_async_copy(src.at[:, side], a_mine.at[:, part], load.at[3, g])
+        copy.start()
+        a_load.append(copy)
+
+    swap_a(1, a1, a0.shape[2])
     for j, b in enumerate(order):
         for g, src in enumerate((g0, g1, g2)):
             f_core.append(
@@ -1009,15 +1091,7 @@
             copy = pltpu.make_async_copy(src.at[:, side, b], ff_mine.at[b, :, g], load.at[g, j])
             copy.start()
             f_load.append(copy)
-    a_swap, a_load = [], []
-    at = 0
-    for g, src in enumerate((a0, a1)):
-        part = pl.ds(at, src.shape[2])
-        at += src.shape[2]
-        a_swap.append(remote(src.at[:, 1 - side], a_core.at[:, part], core_send.at[3, g], core_recv.at[3, g], other))
-        copy = pltpu.make_async_copy(src.at[:, side], a_mine.at[:, part], load.at[3, g])
-        copy.start()
-        a_load.append(copy)
+    swap_a(0, a0, 0)
     slot = x_out.shape[2]
     own_x = pltpu.make_async_copy(x_in.at[:, pl.ds(z * slot, slot)], x_out.at[z], local.at[1])
     own_x.start()
@@ -1045,6 +1119,40 @@
             add_rows(dst.at[g], src.at[g])
 
     ways = ([s // 2 for s in first[::-1]], [s // 2 for s in second[::-1]])
+    n_stage = len(ways[0])
+    held = layout.total
+
+    def a_ready(i):
+        a_load[i].wait()
+        a_swap[i].wait_recv()
+        src = (a1, a0)[i]
+        part = pl.ds(0 if i else a0.shape[2], src.shape[2])
+        for e in range(half):
+            add_rows(a_mine.at[e, part], a_core.at[e, part])
+
+    def a_group(base, count, at):
+        cut = count // 2 // 16 * 16
+        return [
+            Fold(
+                lambda ref, e, lo=lo, size=size: ref.at[e, pl.ds(lo, size)],
+                a_mine, a_two, ways[h], own, d, z, h_send.at[at + h], h_recv.at[at + h],
+            )
+            for h, (lo, size) in enumerate(((base, cut), (base + cut, count - cut)))
+        ]
+
+    def start(group):
+        for p in group:
+            p.start()
+
+    def step(group, add):
+        for fold in group:
+            fold.finish(add)
+            if fold.stage < n_stage:
+                fold.start()
+
+    a_ready(0)
+    side_folds = a_group(a_rows, rows - a_rows, 2) if mirror else []
+    start(side_folds)
     folds = []
     for j, b in enumerate(order):
         for g in range(3):
@@ -1057,41 +1165,51 @@
         )
         fold.start()
         folds.append(fold)
-    for copy in a_load:
-        copy.wait()
-    for copy in a_swap:
-        copy.wait_recv()
-    for i in range(half):
-        add_rows(a_mine.at[i], a_core.at[i])
-    a_folds = [
-        Fold(
-            lambda ref, e, lo=lo, count=count: ref.at[e, pl.ds(lo, count)],
-            a_mine, a_two, ways[h], own, d, z, h_send.at[h], h_recv.at[h],
-        )
-        for h, (lo, count) in enumerate(((0, cut), (cut, rows - cut)))
-    ]
-    n_stage = len(ways[0])
-    line_f = LineSum(lambda b: ff_mine.at[b, own], ff_got, d, z, n_tp, lf_send, lf_recv)
-    line_a = LineSum(lambda b: a_cols.at[b], a_got, d, z, n_tp, la_send, la_recv)
+    a_ready(1)
+    main_folds = a_group(0, a_rows, 0)
+    line_f = LineSum(lambda b: ff_mine.at[b, own], lambda w, b: ff_got.at[w, b], d, z, n_tp, lf_send, lf_recv)
+    line_a = LineSum(
+        lambda b: a_cols.at[b, pl.ds(0, held)], lambda w, b: a_got.at[w, b, pl.ds(0, held)], d, z, n_tp, la_send, la_recv
+    )
+    line_b = LineSum(
+        lambda b: a_cols.at[b, pl.ds(held, 4 * ch)],
+        lambda w, b: a_got.at[w, b, pl.ds(held, 4 * ch)],
+        d, z, n_tp, lb_send, lb_recv,
+    )
+
+    def pass_on(line, b, add):
+        @pl.when(b != z)
+        def _():
+            line.take(b, add)
+            line.give(b)
+
     for t in range(n_stage - 1):
-        for fold in folds:
-            fold.finish(add_three)
-            fold.start()
+        step(side_folds, add_rows)
+        step(folds, add_three)
         if t == 0:
-            for fold in a_folds:
-                fold.start()
-    for j, (fold, b) in enumerate(zip(folds, order)):
+            start(main_folds)
+    if mirror:
+        step(side_folds, add_rows)
+        k = a1.shape[2] // 4
+        for s in range(n_tp):
+            place = one_hot(ch, width, lambda r, col, s=s: col - r == s * ch)
+            for c in range(4):
+                block = a_mine[own, pl.ds(a_rows + c * k, k)]
+                a_cols[s, pl.ds(held + c * ch, ch)] = mm_nt(place, block).astype(BF)
+        for b in order:
+            pass_on(line_b, b, add_rows)
+    for fold, b in zip(folds, order):
         fold.finish(add_three)
-
-        @pl.when(b != z)
-        def _(b=b):
-            line_f.take(b, add_three)
-            line_f.give(b)
-
+        pass_on(line_f, b, add_three)
+    swaps = []
+    if mirror:
+        line_b.take(z, add_rows)
+        for c in range(4):
+            f_own[c] = a_cols[z, pl.ds(held + c * ch, ch)]
+        swaps.append(remote(f_own, f_got, f_swap_send.at[0], f_swap_recv.at[0], (n_dp - 1 - d, z)))
+        swaps.append(remote(f_own, f_edge, f_swap_send.at[1], f_swap_recv.at[1], (across_of(d, n_dp), z)))
     for t in range(1, n_stage):
-        for fold in a_folds:
-            fold.finish(add_rows)
-            fold.start()
+        step(main_folds, add_rows)
     line_f.take(z, add_three)
     put = pltpu.make_async_copy(ff_mine.at[z, own], ff_out.at[d], local.at[0])
     put.start()
@@ -1105,10 +1223,8 @@
         Spread(lambda s, g=g, lo=lo, n=n: ff_out.at[s, g, pl.ds(lo, n)], way + [1], d, z, s_send.at[i], s_recv.at[i])
         for i, (g, lo, n, way) in enumerate(pieces)
     ]
-    for p in sf:
-        p.start()
-    for fold in a_folds:
-        fold.finish(add_rows)
+    start(sf)
+    step(main_folds, add_rows)
     n_pieces = len(layout.pieces())
     groups = {}
     for i, (packed, low, count, _, _, _) in enumerate(layout.pieces()):
@@ -1132,14 +1248,32 @@
                 p.start()
         if stage == 0:
             for b in order:
-
-                @pl.when(b != z)
-                def _(b=b):
-                    line_a.take(b, add_rows)
-                    line_a.give(b)
+                pass_on(line_a, b, add_rows)
 
     line_a.take(z, add_rows)
-    a_out[...] = a_cols[z].astype(F32)
+    if mirror:
+        upper = d > n_dp - 1 - d
+        turn_low = one_hot(k, 2 * k, lambda r, col: r + col == 2 * k)
+        turn_high = one_hot(k, 2 * k, lambda r, col: r + k + col == 2 * k)
+        corner = one_hot(k, 2 * k, lambda r, col: r + col == 0)
+        stay_low = one_hot(k, 2 * k, lambda r, col: r == col)
+        stay_high = one_hot(k, 2 * k, lambda r, col: r + k == col)
+        lane = lax.broadcasted_iota(jnp.int32, (1, 2 * k), 1)
+        zero_at = jnp.logical_and(lane == 0, d == 0)
+        for copy in swaps:
+            copy.wait()
+        for c in range(4):
+            low, high = jnp.where(upper, f_got[c], f_own[c]), jnp.where(upper, f_own[c], f_got[c])
+            plain = mm(low, stay_low) + mm(high, stay_high)
+            if c % 2 == 0:
+                edge = jnp.where(d == n_dp // 2, f_edge[c + 1], f_edge[c])
+                turned = mm(low, turn_low) + mm(high, turn_high) + mm(edge, corner)
+            else:
+                plain = jnp.where(zero_at, 0.0, plain)
+                edge = jnp.where(d == n_dp // 2, 0.0, f_edge[c].astype(F32)).astype(BF)
+                turned = -(mm(low, turn_low) + mm(high, turn_high) + mm(edge, corner))
+            f_out[c] = jnp.where(upper, turned, plain)
+    a_out[...] = a_cols[z, pl.ds(0, layout.total)].astype(F32)
     for copy in zv:
         copy.wait()
     for k in range(1, n_tp):
@@ -1152,6 +1286,8 @@
     for b in range(n_tp):
         line_f.drain(b)
         line_a.drain(b)
+        if mirror:
+            line_b.drain(b)
     for p in sf:
         p.drain()
 
@@ -1160,7 +1296,12 @@
     width = a0.shape[2]
     rows = a0.shape[1] + a1.shape[1]
     vec, hid = ff[0].shape[2:]
-    packed = Pack(rows, width // n_tp).total
+    ch = width // n_tp
+    k = a1.shape[1] // 4
+    mirror = k % 128 == 0
+    a_rows = a0.shape[1] if mirror else rows
+    held = Pack(a_rows, ch).total
+    packed = held + (4 * ch if mirror else 0)
     cut = rows // 2 // 16 * 16
     half = n_dp // 2
     anyspace = pl.BlockSpec(memory_space=pl.ANY)
@@ -1169,15 +1310,16 @@
     pairs = lambda v: v.reshape((half, 2) + v.shape[1:])
     most = max(4, n_tp, 2)
     return pl.pallas_call(
-        functools.partial(scatter_kernel, n_dp, n_tp, cut),
+        functools.partial(scatter_kernel, n_dp, n_tp, cut, mirror),
         out_shape=(
             jax.ShapeDtypeStruct((n_dp, 3, vec, hid), BF),
-            jax.ShapeDtypeStruct((packed, 128), F32),
+            jax.ShapeDtypeStruct((held, 128), F32),
+            jax.ShapeDtypeStruct((4, ch, 2 * k), F32),
             jax.ShapeDtypeStruct(vectors.shape, F32),
             jax.ShapeDtypeStruct((n_tp, x_in.shape[0], x_in.shape[1] // n_tp, width), BF),
         ),
         in_specs=[anyspace] * 5 + [vmem, anyspace],
-        out_specs=(anyspace, vmem, vmem, anyspace),
+        out_specs=(anyspace, vmem, vmem, vmem, anyspace),
         scratch_shapes=[
             pltpu.VMEM((n_tp, half, 3, vec, hid), BF),
             pltpu.VMEM((half, rows, width), BF),
@@ -1189,14 +1331,19 @@
             pltpu.VMEM((2, n_tp, 3, vec, hid), BF),
             pltpu.VMEM((2, n_tp, packed, 128), BF),
             pltpu.VMEM(((half - 1).bit_length() + n_tp,) + vectors.shape, F32),
-            pltpu.VMEM((n_tp * len(Pack(rows, width // n_tp).pieces()), 128, width), BF),
+            pltpu.VMEM((n_tp * len(Pack(a_rows, ch).pieces()), 128, width), BF),
+            pltpu.VMEM((4, ch, k), BF),
+            pltpu.VMEM((4, ch, k), BF),
+            pltpu.VMEM((4, ch, k), BF),
             dma((4, most)),
             dma((4, most)),
             dma((4, most)),
             dma((n_tp, half - 1)),
             dma((n_tp, half - 1)),
-            dma((2, half - 1)),
-            dma((2, half - 1)),
+            dma((4, half - 1)),
+            dma((4, half - 1)),
+            dma((2, n_tp)),
+            dma((2, n_tp)),
             dma((2, n_tp)),
             dma((2, n_tp)),
             dma((2, n_tp)),
@@ -1207,6 +1354,8 @@
             dma((4, n_dp - 1)),
             dma(((half - 1).bit_length() + 1,)),
             dma(((half - 1).bit_length() + 1,)),
+            dma((2,)),
+            dma((2,)),
             dma((2,)),
         ],
         compiler_params=pltpu.CompilerParams(
@@ -1252,81 +1401,79 @@
     rows = slot_len // n_dp
     last = n_dp - 1
     upper = d > last - d
+    mirror = rows % 128 == 0
     filters = jnp.stack([filter_base, filter_mod])
     across = [(i, (n_dp - i) % n_dp) for i in range(n_dp) if i % (n_dp // 2)] + [(0, n_dp // 2), (n_dp // 2, 0)]
-    got = lax.ppermute(filters[:, :, rows:], "dp", [(i, last - i) for i in range(n_dp)])
-    got_edge = lax.ppermute(filters[:, :, :1], "dp", across)
-    direct = jnp.where(upper, got, filters[:, :, :rows]).astype(F32)
-    mirror_lower = jnp.concatenate([got[:, :, 1:], got_edge], axis=2)
-    mirror_upper = filters[:, :, 1 : rows + 1]
-    mirror = jnp.flip(jnp.where(upper, mirror_upper, mirror_lower), 2).astype(F32)
-    nyquist = got_edge[:, 0, 0].astype(F32)
-    edge = ((jnp.arange(rows) == 0) & (d == 0))[None, :, None]
-    half_real = jnp.where(edge, direct[:, 0], direct[:, 0] + mirror[:, 0])
-    half_imag = jnp.where(edge, nyquist[:, None], direct[:, 1] - mirror[:, 1])
-    half = jnp.stack([half_real, half_imag], 1).astype(BF).reshape(4 * rows, ch)
+    if not mirror:
+        got = lax.ppermute(filters[:, :, rows:], "dp", [(i, last - i) for i in range(n_dp)])
+        got_edge = lax.ppermute(filters[:, :, :1], "dp", across)
+        direct = jnp.where(upper, got, filters[:, :, :rows]).astype(F32)
+        mirror_lower = jnp.concatenate([got[:, :, 1:], got_edge], axis=2)
+        mirror_upper = filters[:, :, 1 : rows + 1]
+        image = jnp.flip(jnp.where(upper, mirror_upper, mirror_lower), 2).astype(F32)
+        nyquist = got_edge[:, 0, 0].astype(F32)
+        edge = ((jnp.arange(rows) == 0) & (d == 0))[None, :, None]
+        half_real = jnp.where(edge, direct[:, 0], direct[:, 0] + image[:, 0])
+        half_imag = jnp.where(edge, nyquist[:, None], direct[:, 1] - image[:, 1])
+        half = jnp.stack([half_real, half_imag], 1).astype(BF).reshape(4 * rows, ch)
+
     slice_of = [2 * i if 2 * i < n_dp else 2 * (last - i) + 1 for i in range(n_dp)]
 
-    a_in = jnp.concatenate([in_weight.transpose(1, 0, 2).reshape(3 * vec, ch), out_weight.T, half])
+    a_in = [in_weight.transpose(1, 0, 2).reshape(3 * vec, ch), out_weight.T] + ([] if mirror else [half])
+    a_in = jnp.concatenate(a_in)
+    f_in = filters.transpose(0, 1, 3, 2).reshape(4, ch, 2 * rows)
     vectors = jnp.stack([norm1_gain, norm1_bias, norm2_gain, norm2_bias, out_bias, down_bias])
     vectors = jnp.concatenate([vectors, in_bias])
     vectors = jnp.pad(vectors, ((0, 16 - 9), (0, width - vec)))
     share = hid // n_dp
-    ff_in = jnp.concatenate(
-        [
-            lax.dynamic_slice_in_dim(gate_weight, d * vec, vec, 0),
-            lax.dynamic_slice_in_dim(up_weight, d * vec, vec, 0),
-            lax.dynamic_slice_in_dim(down_weight, d * share, share, 0).reshape(vec, hid),
-        ]
-    )
+    ff = [w.reshape(n_dp, vec, hid) for w in (gate_weight, up_weight, down_weight)]
     x_in = tokens.transpose(0, 2, 1, 3).reshape(n_tp, own, local, width)
     layout = Pack(a_in.shape[0], ch)
-    ffw, aw, x_own = gather_weights(ff_in, layout.pack(a_in), a_in.shape[0], vectors, x_in, n_dp, n_tp)
+    ffw, aw, x_own = gather_weights(ff, layout.pack(a_in), a_in.shape[0], f_in, vectors, x_in, n_dp, n_tp)
     cotangent, _ = lax.optimization_barrier((cotangent, aw))
     vectors = aw[:, 4 * vec + 4 * rows :, :vec].astype(F32).transpose(1, 0, 2).reshape(16, width)
     slots = [slice_of.index(k) for k in range(n_dp)]
     direct = vec % 16 == 0 and hid == width
     if direct:
-        ws = [(ffw, (n_dp, n_tp, vec, hid), g) for g in range(3)]
+        ws = [
+            (ffw, (n_dp, n_tp, None, vec, hid), (0, 0, g, 0, 0), (n_dp, 1, None, vec, hid), lambda p, g=g: (0, p, g, 0, 0))
+            for g in range(3)
+        ]
         a_view = aw
     else:
-        natural = [
-            ffw[:, :, g * vec : (g + 1) * vec].transpose(1, 0, 2, 3).reshape(n_tp, width, hid) for g in range(2)
+        natural = [ffw[:, :, g].transpose(1, 0, 2, 3).reshape(n_tp, width, hid) for g in range(2)]
+        natural.append(ffw[:, :, 2].reshape(n_dp, n_tp, share, width).transpose(1, 0, 2, 3).reshape(n_tp, hid, width))
+        ws = [
+            (w[None], (1,) + w.shape, (0, 0, 0, 0), (1, 1) + w.shape[1:], lambda p: (0, p, 0, 0)) for w in natural
         ]
-        natural.append(
-            ffw[:, :, 2 * vec :].reshape(n_dp, n_tp, share, width).transpose(1, 0, 2, 3).reshape(n_tp, hid, width)
-        )
-        ws = [(w[None], (1,) + w.shape, 0) for w in natural]
         a_view = aw[:, : 4 * vec].reshape(n_dp, 4, vec, width).transpose(1, 0, 2, 3).reshape(1, 4 * width, width)
-    feed_weights = (ws[0][0], ws)
 
     def to_owner(x):
         pieces = x.transpose(0, 2, 1, 3).reshape(n_tp, own, local, width)
         return lax.all_to_all(pieces, "tp", 0, 1, tiled=False).reshape(own, slot_len, width)
 
     def to_slots(x):
-        pieces = x.reshape(own, n_tp, local, width)
-        whole = lax.all_to_all(pieces, "tp", 1, 0, tiled=False)
+        whole = lax.all_to_all(x.reshape(n_tp, own * local, width), "tp", 0, 0, tiled=False)
         return whole.reshape(micro, group, local, width).transpose(0, 2, 1, 3)
 
     c_own = to_owner(cotangent)
     flat_len = lax.dynamic_slice_in_dim(lengths.reshape(-1), z * own, own, 0)
     first = 4 * vec // rows
-    n1, values, gating, nsum, mixing = project(x_own, flat_len, a_view, vectors)
+    values, gating, nsum, mixing = project(x_own, flat_len, a_view, vectors)
     spec, conv, gated = spectral(values, gating, mixing, flat_len, table, aw, first, rows, slots, scale)
-    middle, n2, act, side, hidden, out = feed(x_own, gated, flat_len, a_view, feed_weights, vectors)
+    middle, n2, act, side, hidden, out = feed(x_own, gated, flat_len, a_view, ws, n_tp, hid, vectors)
     layer_out = to_slots(out)
-    e, *d_ff = feed_back(c_own, n2, act, side, hidden, flat_len, feed_weights)
-    mg, cg, gtg, d_out, sums = branch_back(e, middle, c_own, gated, gating, conv, flat_len, a_view, vectors)
+    e, *d_ff = feed_back(c_own, n2, act, side, hidden, flat_len, ws)
+    mg, cg, gtg, d_out, sums = branch_back(e, middle, c_own, gating, conv, flat_len, a_view, vectors)
     layer_out, cg = lax.optimization_barrier((layer_out, cg))
     vg, d_filter, cgv = spectral_back(cg, spec, mixing, flat_len, table, aw, first, rows, slots, scale)
-    ig, d_first, sums = input_back(vg, gtg, n1, x_own, mg, nsum, cgv, flat_len, a_view, d_out, sums, vectors)
+    ig, d_first, sums = input_back(vg, gtg, x_own, mg, nsum, cgv, flat_len, a_view, d_out, sums, vectors)
     if not direct:
         d_ff = [
             g[0].reshape(n_tp, n_dp, vec, hid).transpose(1, 0, 2, 3) for g in d_ff[:2]
         ] + [d_ff[2][0].reshape(n_tp, n_dp, vec, hid).transpose(1, 0, 2, 3)]
         d_first = d_first.reshape(4, n_dp, vec, width).transpose(1, 0, 2, 3).reshape(n_dp, 4 * vec, width)
-    ffg, ag, vecs, input_grad = scatter_grads(d_ff, d_first, d_filter, sums, ig, n_dp, n_tp)
+    ffg, ag, full, vecs, input_grad = scatter_grads(d_ff, d_first, d_filter, sums, ig, n_dp, n_tp)
     input_grad = input_grad.reshape(micro, group, local, width).transpose(0, 2, 1, 3)
     ag = layout.unpack(ag)
     gate_grad = ffg[:, 0].reshape(width, hid).astype(F32)
@@ -1334,21 +1481,23 @@
     down_grad = ffg[:, 2].reshape(hid, width).astype(F32)
     in_grad = ag[: 3 * vec].reshape(3, vec, ch).transpose(1, 0, 2)
     out_grad = ag[3 * vec : 4 * vec].T
-    fgrad = ag[4 * vec :].astype(BF).reshape(2, 2, rows, ch)
-    other = lax.ppermute(fgrad, "dp", [(i, last - i) for i in range(n_dp)])
-    low_slice = jnp.where(upper, other, fgrad)
-    high_slice = jnp.where(upper, fgrad, other)
-    both = jnp.concatenate([low_slice, high_slice], axis=2)
-    follow = lax.ppermute(fgrad[:, :, :1], "dp", across)
-    zero = jnp.zeros_like(follow[:, 0])
-    follow = jnp.where(d == n_dp // 2, jnp.stack([follow[:, 1], zero], 1), follow)
-    mirrored = jnp.flip(jnp.concatenate([both[:, :, 1:], follow], axis=2), 2)
-    mirrored = jnp.stack([mirrored[:, 0], -mirrored[:, 1]], 1)
-    plain = jnp.stack(
-        [both[:, 0], jnp.where((d == 0) & (jnp.arange(2 * rows) == 0)[None, :, None], 0.0, both[:, 1].astype(F32)).astype(BF)], 1
-    )
-    full = jnp.where(upper, mirrored, plain).astype(F32)
-
+    if mirror:
+        full = full.reshape(2, 2, ch, 2 * rows).transpose(0, 1, 3, 2)
+    else:
+        fgrad = ag[4 * vec :].astype(BF).reshape(2, 2, rows, ch)
+        other = lax.ppermute(fgrad, "dp", [(i, last - i) for i in range(n_dp)])
+        low_slice = jnp.where(upper, other, fgrad)
+        high_slice = jnp.where(upper, fgrad, other)
+        both = jnp.concatenate([low_slice, high_slice], axis=2)
+        follow = lax.ppermute(fgrad[:, :, :1], "dp", across)
+        zero = jnp.zeros_like(follow[:, 0])
+        follow = jnp.where(d == n_dp // 2, jnp.stack([follow[:, 1], zero], 1), follow)
+        mirrored = jnp.flip(jnp.concatenate([both[:, :, 1:], follow], axis=2), 2)
+        mirrored = jnp.stack([mirrored[:, 0], -mirrored[:, 1]], 1)
+        plain = jnp.stack(
+            [both[:, 0], jnp.where((d == 0) & (jnp.arange(2 * rows) == 0)[None, :, None], 0.0, both[:, 1].astype(F32)).astype(BF)], 1
+        )
+        full = jnp.where(upper, mirrored, plain).astype(F32)
     piece = width // (n_dp * n_tp)
     vecs = lax.dynamic_slice_in_dim(vecs, (d * n_tp + z) * piece, piece, 1)
     return (

time: 604 us -> 570 us (0.944)
  Pallas kernels: 520 us -> 506 us
  local copies, waits for them, and re-layouts: 46.6 us -> 38.2 us
  starting transfers between devices: 16.2 us -> 9.17 us
    pallas_call x2, Pallas kernels: 291 us -> 282 us  [the longest x1 149 us: scatter_grads(): pl.pallas_call(functools.partial(scatter_kernel, n_dp, n_tp, cut, mirror)...]
    another operation x2 -> x0, local copies, waits for them, and re-layouts: 6.89 us -> none  [the longest x1 6.75 us: to_slots(): whole = lax.all_to_all(pieces, 'tp', 1, 0, tiled=False)]
    ppermute x4 -> x0, starting transfers between devices: 6.18 us -> none  [the longest x1 3.4 us: body(): lax.ppermute(filters[:, :, rows:], 'dp', [(i, last - i) for i in range(n_...]
    unnamed x36 -> x42, local copies, waits for them, and re-layouts: 20.1 us -> 21.7 us
  transfers between devices with their start and end apart: 6 -> 2, of which waited for: 1 -> 0; matrix products, arithmetic and copies ran while one was open for 7% -> 1% of each run, Pallas kernels for 30% -> 31%
where the time goes in v3:
time: 570 us; the launch traced here: 561 us
  Pallas kernels  506 us (89%)
  local copies, waits for them, and re-layouts  38.2 us (7%)
  starting transfers between devices  9.17 us (2%)
  other arithmetic  6.82 us (1%)
    pallas_call x7, Pallas kernels, call(): pl.pallas_call(kernel, grid_spec=spec, out_shape=tuple(outs), compiler_pa...  224 us
    pallas_call x1, Pallas kernels, scatter_grads(): pl.pallas_call(functools.partial(scatter_kernel, n_dp, n_tp, cut, mirror)...  149 us
    pallas_call x1, Pallas kernels, gather_weights(): pl.pallas_call(functools.partial(gather_kernel, n_dp, n_tp, cut, a_rows,...  133 us
    unnamed x42, local copies, waits for them, and re-layouts  21.7 us
  transfers between devices with their start and end apart: 2, of which 0 were waited for; matrix products, arithmetic and copies ran while one was open for 1% of the time, Pallas kernels for 31%

profile of v3, /device:TPU:0, one launch (start us, length us, event | category | flops | bytes accessed | tf_op | source)
XLA Modules:
  0.0 561.4 jit_solution(6529664613130284923)
XLA Ops:
  3.4 4.2 copy.58
  8.0 1.3 copy-done.2
  9.3 133.4 %gather_weights.1 = (bf16[8,4,3,96,768]{4,3,2,1,0:T(8,128)(2,1)}, bf16[8,912,768]{2,1,0:T(8,128)(2,1)}, bf16[2,1024,768]{2,1,0:T(8,128)(2,1)}) custom-call(bf16[8,96,768]{2,1,0:T(8,128)(2,1)S(1)} %bitcast.74, bf16[8,96,768]{2,1,0:T(8,128)(2,1)S(1)} %bitcast.75, bf16[8,96,768]{2,1,0:T(8,128)(2,1)S(1)} %bitcast.76, bf16[576,128]{1,0:T(8,128)(2,1)S(1)} %fusion.7.a_in, ...), custom_call_target="tpu_custom_call" | custom-call | tf_op jit(solution)/shard_map/gather_weights/pallas_call | solution.py:929
  142.7 3.7 all-to-all-start.1
  148.7 12.2 %project.1 = (bf16[2,1024,768]{2,1,0:T(8,128)(2,1)}, bf16[2,1024,768]{2,1,0:T(8,128)(2,1)}, f32[2,8,768]{2,1,0:T(8,128)}, f32[2,8,768]{2,1,0:T(8,128)}) custom-call(s32[2]{0:T(128)} %dynamic_slice.6.lens, bf16[2,1024,768]{2,1,0:T(8,128)(2,1)} %get-tuple-element.55.x, ...), custom_call_target="tpu_custom_call" | custom-call | flops 4831838208 | bytes 43204608 | tf_op jit(solution)/shard_map/project/pallas_call | solution.py:342
  160.9 21.8 %spectral.1 = (bf16[2,2048,768]{2,1,0:T(8,128)(2,1)}, bf16[2,1024,768]{2,1,0:T(8,128)(2,1)}, bf16[2,1024,768]{2,1,0:T(8,128)(2,1)}) custom-call(s32[2]{0:T(128)} %dynamic_slice.6.lens, bf16[2,1024,768]{2,1,0:T(8,128)(2,1)} %get-tuple-element.57.refs_0_, bf16[2,1024,768]{2,1,0:T(8,128)(2,1)} %get-tuple-element.58.refs_1_.gating, ...), custom_call_target="tpu_custom_call" | custom-call | flops 12884901888 | bytes 67944448 | tf_op jit(solution)/shard_map/spectral/pallas_call | solution.py:342
  182.7 52.0 %feed.1 = (bf16[2,1024,768]{2,1,0:T(8,128)(2,1)}, bf16[2,1024,768]{2,1,0:T(8,128)(2,1)}, bf16[2,4,1024,768]{3,2,1,0:T(8,128)(2,1)}, bf16[2,4,1024,768]{3,2,1,0:T...) custom-call(s32[2]{0:T(128)} %dynamic_slice.6.lens, ...), custom_call_target="tpu_custom_call" | custom-call | flops 31406948352 | bytes 107200512 | tf_op jit(solution)/shard_map/feed/pallas_call | solution.py:342
  234.7 1.7 copy-done.3
  236.4 5.5 all-to-all-start
  241.9 4.0 copy.53
  245.9 72.7 %feed_back.1 = (bf16[2,1024,768]{2,1,0:T(8,128)(2,1)}, bf16[8,4,96,768]{3,2,1,0:T(8,128)(2,1)}, bf16[8,4,96,768]{3,2,1,0:T(8,128)(2,1)}, bf16[8,4,96,768]{3,2,1,0:T(8,128)(2,1)}) custom-call(s32[2]{0:T(128)} %dynamic_slice.6.lens, bf16[2,1024,768]{2,1,0:T(8,128)(2,1)} %bitcast.80, bf16[2,1024,768]{2,1,0:T(8,128)(2,1)} %get-tuple-element.64.n2, ...), custom_call_target="tpu_custom_call" | custom-call | flops 57982058496 | bytes 103809024 | tf_op jit(solution)/shard_map/feed_back/pallas_call | solution.py:342
  318.6 16.5 %branch_back.1 = (bf16[2,1024,768]{2,1,0:T(8,128)(2,1)}, bf16[2,1024,768]{2,1,0:T(8,128)(2,1)}, bf16[2,1024,768]{2,1,0:T(8,128)(2,1)}, bf16[8,96,768]{2,1,0:T(8,128)(2,1)}, f32[8,768]{1,0:T(8,128)}) custom-call(s32[2]{0:T(128)} %dynamic_slice.6.lens, bf16[2,1024,768]{2,1,0:T(8,128)(2,1)} %get-tuple-element.68.e, ...), custom_call_target="tpu_custom_call" | custom-call | flops 4831838208 | bytes 37625856 | tf_op jit(solution)/shard_map/branch_back/pallas_call | solution.py:342
  335.1 25.7 %spectral_back.1 = (bf16[2,1024,768]{2,1,0:T(8,128)(2,1)}, bf16[8,512,768]{2,1,0:T(8,128)(2,1)}, f32[2,8,768]{2,1,0:T(8,128)}) custom-call(s32[2]{0:T(128)} %dynamic_slice.6.lens, bf16[2,1024,768]{2,1,0:T(8,128)(2,1)} %get-tuple-element.76.cg, bf16[2,2048,768]{2,1,0:T(8,128)(2,1)} %get-tuple-element.77.spec, f32[2,8,768]{2,1,0:T(8,128)} %get-tuple-element.59.refs_2_.mixing, ...), custom_call_target="tpu_custom_call" | custom-call | flops 12884901888 | bytes 67993600 | tf_op jit(solution)/shard_map/spectral_back/pallas_call | solution.py:342
  360.8 22.8 %input_back.1 = (bf16[2,1024,768]{2,1,0:T(8,128)(2,1)}, bf16[8,384,768]{2,1,0:T(8,128)(2,1)}, f32[16,768]{1,0:T(8,128)}) custom-call(s32[2]{0:T(128)} %dynamic_slice.6.lens, bf16[2,1024,768]{2,1,0:T(8,128)(2,1)} %get-tuple-element.78.vg, bf16[2,1024,768]{2,1,0:T(8,128)(2,1)} %get-tuple-element.79.gtg, bf16[2,1024,768]{2,1,0:T(8,128)(2,1)} %get-tuple-element.55.x, ...), custom_call_target="tpu_custom_call" | custom-call | flops 9663676416 | bytes 55468032 | tf_op jit(solution)/shard_map/input_back/pallas_call | solution.py:342
  383.7 148.7 %scatter_grads.1 = (bf16[8,3,96,768]{3,2,1,0:T(8,128)(2,1)}, f32[576,128]{1,0:T(8,128)}, f32[4,192,256]{2,1,0:T(8,128)}, f32[16,768]{1,0:T(8,128)}, bf16[4,2,256,768]{3,2,1,0:T(8,128)(2,1)}) custom-call(bf16[4,2,4,96,768]{4,3,2,1,0:T(8,128)(2,1)} %bitcast.83, bf16[4,2,4,96,768]{4,3,2,1,0:T(8,128)(2,1)} %bitcast.84, bf16[4,2,4,96,768]{4,3,2,1,0:T(8,128)(2,1)} %bitcast.85, ...), custom_call_target="tpu_custom_call" | custom-call | tf_op jit(solution)/shard_map/scatter_grads/pallas_call | solution.py:1312
  532.4 1.1 fusion.10
  535.1 3.6 fusion.9
  538.7 1.7 bitcast_convert_fusion.2
  540.4 1.6 copy.56
  542.7 6.9 %copy.55 = bf16[4,256,2,768]{3,2,1,0:T(2,128)(2,1)} copy(bf16[4,256,2,768]{3,1,2,0:T(8,128)(2,1)} %bitcast.89) | data formatting | bytes 6291456
  550.5 4.9 copy.54
  555.4 2.7 bitcast_convert_fusion
  558.1 1.4 dynamic-slice.2
  559.5 1.5 dynamic-slice_bitcast_fusion
  (54 shorter events, 8.5 us)
Async XLA Ops:
  3.2 4.4 copy-start.6
  3.2 4.5 copy-start.8
  3.3 4.5 copy-start.9
  3.3 4.5 copy-start.11
  3.3 4.5 copy-start.12
  3.3 4.5 copy-start.13
  3.3 4.5 copy-start.14
  3.3 4.5 copy-start.15
  3.3 4.5 copy-start.16
  3.3 4.5 copy-start.17
  3.4 4.6 copy-start
  3.4 4.6 copy-start.1
  8.0 1.3 copy-start.2
  142.7 5.2 copy-start.10
  142.7 92.0 %all-to-all-start.1 = ((bf16[4,2,1,256,768]{4,1,3,2,0:T(2,128)(2,1)}), bf16[4,2,1,256,768]{4,1,3,2,0:T(2,128)(2,1)S(1)}, u32[]{:S(2)}, u32[]{:S(2)}) async-start(bf16[4,2,1,256,768]{4,1,3,2,0:T(2,128)(2,1)} %bitcast.87), calls=%async_computation.1 | async-start | bytes 6291456 | tf_op jit(solution)/shard_map/all_to_all | solution.py:1453
  234.7 1.7 copy-start.3
  236.4 98.6 %all-to-all-start = ((bf16[4,512,768]{2,1,0:T(8,128)(2,1)}), bf16[4,512,768]{2,1,0:T(8,128)(2,1)S(1)}, u32[]{:S(2)}, u32[]{:S(2)}) async-start(bf16[4,512,768]{2,1,0:T(8,128)(2,1)} %bitcast.88), calls=%async_computation | async-start | bytes 6291456 | tf_op jit(solution)/shard_map/all_to_all | solution.py:1456
  542.7 6.9 %copy-start.7 = (f32[4,192,256]{2,1,0:T(8,128)S(1)}, f32[4,192,256]{2,1,0:T(8,128)}, u32[]{:S(2)}) copy-start(f32[4,192,256]{2,1,0:T(8,128)} %get-tuple-element.92) | copy-start | bytes 2359300
  550.5 4.9 copy-start.4
  550.5 4.9 copy-start.5

commit v4 on v3

--- a/solution.py
+++ b/solution.py
@@ -99,29 +99,64 @@
     return jnp.where(r == 0, jnp.broadcast_to(v, (rows, v.shape[1])), 0.0)
 
 
-def project_kernel(tile, lens, x, wv, wg, wc, vec, values, gating, nsum, mixing):
-    s, t = pl.program_id(0), pl.program_id(1)
-    count = lens[s]
-    valid = live(tile, t * tile, count)
-    std, _ = standardize(x[0].astype(F32))
-    normed = (std * vec[0:1] + vec[1:2]).astype(BF)
-    values[0] = ((mm(normed, joined(wv)) + vec[6:7]) * valid).astype(BF)
-    gating[0] = (mm(normed, joined(wg)) + vec[7:8]).astype(BF)
-    part = top_row(jnp.sum(normed.astype(F32) * valid, axis=0, keepdims=True))
-
-    @pl.when(t == 0)
+def mix_kernel(
+    tile, tiles, slots, scale, lens, x, wv, wg, wc, vec, table, f0, f1, f2, f3,
+    gating, nsum, mixing, spec, conv, gated, vals, gats,
+):
+    i = pl.program_id(0)
+    own, n = vals.shape[1], vals.shape[2]
+    blocks, cb = vals.shape[0], vals.shape[3]
+
+    @pl.when(i < own * tiles)
     def _():
-        nsum[0] = part
-
-    @pl.when(t > 0)
+        s, t = i // tiles, lax.rem(i, tiles)
+        here = pl.ds(t * tile, tile)
+        count = lens[s]
+        valid = live(tile, t * tile, count)
+        std, _ = standardize(x[0].astype(F32))
+        normed = (std * vec[0:1] + vec[1:2]).astype(BF)
+        v = ((mm(normed, joined(wv)) + vec[6:7]) * valid).astype(BF)
+        g = (mm(normed, joined(wg)) + vec[7:8]).astype(BF)
+        gating[0] = g
+        for c in range(blocks):
+            vals[c, s, here] = v[:, c * cb : (c + 1) * cb]
+            gats[c, s, here] = g[:, c * cb : (c + 1) * cb]
+        part = top_row(jnp.sum(normed.astype(F32) * valid, axis=0, keepdims=True))
+
+        @pl.when(t == 0)
+        def _():
+            nsum[s] = part
+
+        @pl.when(t > 0)
+        def _():
+            nsum[s] += part
+
+        @pl.when(t == tiles - 1)
+        def _():
+            length = count.astype(F32)
+            cond = two_part_dot(nsum[s], joined(wc), ((1,), (0,))) + length * vec[8:9]
+            mixing[s] = jnp.tanh(cond / length)
+
+    @pl.when(i >= own * tiles)
     def _():
-        nsum[0] += part
-
-    @pl.when(t == pl.num_programs(1) - 1)
-    def _():
-        length = count.astype(F32)
-        cond = two_part_dot(nsum[0], joined(wc), ((1,), (0,))) + length * vec[8:9]
-        mixing[0] = jnp.tanh(cond / length)
+        c = i - own * tiles
+        columns = pl.ds(pl.multiple_of(c * cb, cb), cb)
+        raw = [mm(table[...], vals[c, s]) for s in range(own)]
+        edge = lax.broadcasted_iota(jnp.int32, (n, 1), 0) == 0
+        outs = []
+        for s in range(own):
+            v = raw[s]
+            spec[s] = v.astype(BF)
+            sr, si = v[:n], v[n:]
+            fr, fi, _, _ = filters_of((f0, f1, f2, f3), slots, mixing[s, 0:1, columns])
+            fr2 = jnp.where(edge, fi, fr)
+            fi = jnp.where(edge, 0.0, fi)
+            prod = jnp.concatenate([(fr * sr - fi * si).astype(BF), (fr2 * si + fi * sr).astype(BF)])
+            outs.append(mm_tn(table[...], prod))
+        for s in range(own):
+            out = outs[s] * scale
+            conv[s] = out.astype(BF)
+            gated[s] = (out * gats[c, s].astype(F32)).astype(BF)
 
 
 def filters_of(refs, slots, mix):
@@ -129,35 +164,31 @@
     return base_r + mix * mod_r, base_i + mix * mod_i, mod_r, mod_i
 
 
-def spectral_kernel(slots, scale, values, gating, mixing, table, f0, f1, f2, f3, spec, conv, gated):
-    own = values.shape[0]
-    n = values.shape[1]
-    raw = [mm(table[...], values[s]) for s in range(own)]
-    edge = lax.broadcasted_iota(jnp.int32, (n, 1), 0) == 0
-    outs = []
-    for s in range(own):
-        v = raw[s]
-        spec[s] = v.astype(BF)
-        sr, si = v[:n], v[n:]
-        fr, fi, _, _ = filters_of((f0, f1, f2, f3), slots, mixing[s, 0:1])
-        fr2 = jnp.where(edge, fi, fr)
-        fi = jnp.where(edge, 0.0, fi)
-        prod = jnp.concatenate([(fr * sr - fi * si).astype(BF), (fr2 * si + fi * sr).astype(BF)])
-        outs.append(mm_tn(table[...], prod))
-    for s in range(own):
-        out = outs[s] * scale
-        conv[s] = out.astype(BF)
-        gated[s] = (out * gating[s].astype(F32)).astype(BF)
-
-
-def feed_kernel(tile, n_tp, lens, x, gated, w_out, wg, wu, wd, vec, middle, n2, act, side, hidden, out):
+def feed_kernel(tile, n_tp, lens, x, gated, w_out, hg, hu, hd, vec, middle, n2, act, side, hidden, out, wg, wu, wd, sems):
     s, t = pl.program_id(0), pl.program_id(1)
+    begin = (s == 0) & (t == 0)
+    copies = [
+        pltpu.make_async_copy(src.at[:, :, g] if len(src.shape) == 5 else src, dst, sems.at[g])
+        for g, (src, dst) in enumerate(((hg, wg), (hu, wu), (hd, wd)))
+    ]
+
+    @pl.when(begin)
+    def _():
+        for copy in copies:
+            copy.start()
+
     valid = live(tile, t * tile, lens[s])
     mid = x[0].astype(F32) + valid * (mm_nt(gated[0], joined(w_out)) + vec[4:5])
     middle[0] = mid.astype(BF)
     std, _ = standardize(mid)
     normed = (std * vec[2:3] + vec[3:4]).astype(BF)
     n2[0] = normed
+
+    @pl.when(begin)
+    def _():
+        for copy in copies:
+            copy.wait()
+
     feed = jnp.zeros(mid.shape, F32)
     for p in range(n_tp):
         gate = mm(normed, joined(wg.at[:, p]))
@@ -179,11 +210,6 @@
     def _():
         e_acc[s] = jnp.zeros(e_acc.shape[1:], F32)
 
-    @pl.when(s == 0)
-    def _():
-        for acc in (acc_g, acc_u, acc_d):
-            acc[...] = jnp.zeros(acc.shape, F32)
-
     down, gate, up = joined(wd.at[:, 0]), joined(wg.at[:, 0]), joined(wu.at[:, 0])
     for i in range(n // tile):
         here = pl.ds(i * tile, tile)
@@ -195,19 +221,37 @@
     for i in range(n // tile):
         here = pl.ds(i * tile, tile)
         e_acc[s, here] += mm_nt(ggs[here], gate) + mm_nt(ugs[here], up)
-    normed = n2[0]
-    acc_g[...] += mm_tn(normed, ggs[...])
-    acc_u[...] += mm_tn(normed, ugs[...])
-    acc_d[...] += mm_tn(hidden[0, 0], fgs[...])
+    own = e_acc.shape[0]
+    sides = ((acc_g, d_gate, n2.at[0], ggs), (acc_u, d_up, n2.at[0], ugs), (acc_d, d_down, hidden.at[0, 0], fgs))
+
+    def put(out, v):
+        out[:, 0] = v.astype(BF).reshape(out.shape[0], out.shape[2], out.shape[3])
+
+    if own == 1:
+        for acc, out, left, right in sides:
+            put(out, mm_tn(left[...], right[...]))
+    else:
+
+        @pl.when(s == 0)
+        def _():
+            for acc, out, left, right in sides:
+                acc[...] = mm_tn(left[...], right[...])
+
+        @pl.when(s == own - 1)
+        def _():
+            for acc, out, left, right in sides:
+                put(out, acc[...] + mm_tn(left[...], right[...]))
+
+    if own > 2:
+
+        @pl.when((s > 0) & (s < own - 1))
+        def _():
+            for acc, out, left, right in sides:
+                acc[...] += mm_tn(left[...], right[...])
 
     @pl.when(p == pl.num_programs(0) - 1)
     def _():
         e_out[0] = e_acc[s].astype(BF)
-
-    @pl.when(s == pl.num_programs(1) - 1)
-    def _():
-        for acc, out in zip((acc_g, acc_u, acc_d), (d_gate, d_up, d_down)):
-            out[:, 0] = acc[...].astype(BF).reshape(out.shape[0], out.shape[2], out.shape[3])
 
 
 def eights(v):
@@ -359,64 +403,55 @@
     return jax.ShapeDtypeStruct(shape, dtype)
 
 
-def project(x, lens, aw, vec):
-    own, n, width = x.shape
-    tile = min(512, n)
-    nd, r = aw.shape[0], width // aw.shape[0]
-    tok = pl.BlockSpec((1, tile, width), lambda s, t, *_: (s, t, 0))
-    one = pl.BlockSpec((1, 8, width), lambda s, t, *_: (s, 0, 0))
-    weights = [once((nd, r, width), (0, g, 0)) for g in range(3)]
-    sd = shape_of(x.shape, BF)
-    row = shape_of((own, 8, width), F32)
-    return call(
-        functools.partial(project_kernel, tile),
-        (own, n // tile),
-        lens,
-        [x, aw, aw, aw, vec],
-        [tok] + weights + [once(vec.shape, (0, 0))],
-        [sd, sd, row, row],
-        (tok, tok, one, one),
-        [],
-        4 * own * n * width * width,
-        "project",
-    )
-
-
 def filter_specs(fw, n_dp, rows, cb, first):
     return [
         pl.BlockSpec((n_dp, rows, cb), lambda *g, i=i: (0, first + i, g[0])) for i in range(4)
     ]
 
 
-def spectral(values, gating, mixing, lens, table, fw, first, rows, slots, scale):
-    own, n, width = values.shape
+def mix(x, lens, aw, vec, table, fw, first, rows, slots, scale):
+    own, n, width = x.shape
+    tile = min(512, n)
+    tiles = n // tile
+    steps = own * tiles
     cb = min(256, width)
+    blocks = width // cb
+    nd, r = aw.shape[0], width // aw.shape[0]
     n_dp = fw.shape[0]
-    tok = pl.BlockSpec((own, n, cb), lambda c, *_: (0, 0, c))
-    both = pl.BlockSpec((own, 2 * n, cb), lambda c, *_: (0, 0, c))
-    one = pl.BlockSpec((own, 8, cb), lambda c, *_: (0, 0, c))
-
-    def kernel(lens, *refs):
-        spectral_kernel(slots, scale, *refs)
-
+
+    def tok(i, *_):
+        j = jnp.minimum(i, steps - 1)
+        return j // tiles, lax.rem(j, tiles), 0
+
+    def chan(i):
+        return jnp.maximum(i - steps, 0)
+
+    token = pl.BlockSpec((1, tile, width), tok)
+    whole = pl.BlockSpec((own, 8, width), lambda *_: (0, 0, 0))
+    column = pl.BlockSpec((own, n, cb), lambda i, *_: (0, 0, chan(i)))
+    double = pl.BlockSpec((own, 2 * n, cb), lambda i, *_: (0, 0, chan(i)))
+    weights = [once((nd, r, width), (0, g, 0)) for g in range(3)]
+    filters = [pl.BlockSpec((n_dp, rows, cb), lambda i, *_, k=k: (0, first + k, chan(i))) for k in range(4)]
+    sd = shape_of(x.shape, BF)
+    row = shape_of((own, 8, width), F32)
     return call(
-        kernel,
-        (width // cb,),
+        functools.partial(mix_kernel, tile, tiles, slots, scale),
+        (steps + blocks,),
         lens,
-        [values, gating, mixing, table] + [fw] * 4,
-        [tok, tok, one, once(table.shape, (0, 0))] + filter_specs(fw, n_dp, rows, cb, first),
-        [shape_of((own, 2 * n, width), BF), shape_of(values.shape, BF), shape_of(values.shape, BF)],
-        (both, tok, tok),
-        [],
-        8 * own * n * n * width,
-        "spectral",
+        [x, aw, aw, aw, vec, table] + [fw] * 4,
+        [token] + weights + [once(vec.shape, (0, 0)), once(table.shape, (0, 0))] + filters,
+        [sd, row, row, shape_of((own, 2 * n, width), BF), sd, sd],
+        (token, whole, whole, double, column, column),
+        [pltpu.VMEM((blocks, own, n, cb), BF), pltpu.VMEM((blocks, own, n, cb), BF)],
+        4 * own * n * width * width + 8 * own * n * n * width,
+        "mix",
     )
 
 
 def feed(x, gated, lens, aw, ws, n_tp, hid, vec):
     own, n, width = x.shape
-    tile = min(512, n)
     local = n // n_tp
+    tile = max(256, local)
     r = width // aw.shape[0]
     tok = pl.BlockSpec((1, tile, width), lambda s, t, *_: (s, t, 0))
     wide = pl.BlockSpec((1, n_tp, tile, hid), lambda s, t, *_: (s, 0, t, 0))
@@ -427,10 +462,10 @@
         (own, n // tile),
         lens,
         [x, gated, aw] + [w[0] for w in ws] + [vec],
-        [tok, tok, once((aw.shape[0], r, width), (0, 3, 0))] + [once(w[1], w[2]) for w in ws] + [once(vec.shape, (0, 0))],
+        [tok, tok, once((aw.shape[0], r, width), (0, 3, 0))] + [pl.BlockSpec(memory_space=pl.ANY)] * 3 + [once(vec.shape, (0, 0))],
         [shape_of(x.shape, BF), shape_of(x.shape, BF), big, big, big, shape_of((n_tp, own, local, width), BF)],
         (tok, tok, wide, wide, wide, parts),
-        [],
+        [pltpu.VMEM(tuple(v for v in w[1] if v is not None), BF) for w in ws] + [pltpu.SemaphoreType.DMA((3,))],
         2 * own * n * width * (width + 3 * n_tp * hid),
         "feed",
         limit=60,
@@ -748,7 +783,7 @@
     @pl.loop(0, rows // size)
     def _(i):
         at = pl.ds(i * size, size)
-        dst[at] = (dst[at].astype(F32) + src[at].astype(F32)).astype(BF)
+        dst[at] = dst[at] + src[at]
 
 
 def lane_place(rows, cols, offset):
@@ -1459,8 +1494,7 @@
     c_own = to_owner(cotangent)
     flat_len = lax.dynamic_slice_in_dim(lengths.reshape(-1), z * own, own, 0)
     first = 4 * vec // rows
-    values, gating, nsum, mixing = project(x_own, flat_len, a_view, vectors)
-    spec, conv, gated = spectral(values, gating, mixing, flat_len, table, aw, first, rows, slots, scale)
+    gating, nsum, mixing, spec, conv, gated = mix(x_own, flat_len, a_view, vectors, table, aw, first, rows, slots, scale)
     middle, n2, act, side, hidden, out = feed(x_own, gated, flat_len, a_view, ws, n_tp, hid, vectors)
     layer_out = to_slots(out)
     e, *d_ff = feed_back(c_own, n2, act, side, hidden, flat_len, ws)

time: 570 us -> 563 us (0.988)
    pallas_call x7 -> x6, Pallas kernels: 224 us -> 221 us  [call(): pl.pallas_call(kernel, grid_spec=spec, out_shape=tuple(outs), compiler_pa...]
where the time goes in v4:
time: 563 us; the launch traced here: 558 us
  Pallas kernels  502 us (89%)
  local copies, waits for them, and re-layouts  38.4 us (7%)
  starting transfers between devices  9.48 us (2%)
  other arithmetic  6.82 us (1%)
    pallas_call x6, Pallas kernels, call(): pl.pallas_call(kernel, grid_spec=spec, out_shape=tuple(outs), compiler_pa...  221 us
    pallas_call x1, Pallas kernels, scatter_grads(): pl.pallas_call(functools.partial(scatter_kernel, n_dp, n_tp, cut, mirror)...  148 us
    pallas_call x1, Pallas kernels, gather_weights(): pl.pallas_call(functools.partial(gather_kernel, n_dp, n_tp, cut, a_rows,...  133 us
    unnamed x42, local copies, waits for them, and re-layouts  21.7 us
  transfers between devices with their start and end apart: 2, of which 0 were waited for; matrix products, arithmetic and copies ran while one was open for 1% of the time, Pallas kernels for 31%

profile of v4, /device:TPU:0, one launch (start us, length us, event | category | flops | bytes accessed | tf_op | source)
XLA Modules:
  0.0 558.2 jit_solution(9421204555847492321)
XLA Ops:
  3.4 4.2 copy.58
  8.0 1.3 copy-done.2
  9.3 133.4 %gather_weights.1 = (bf16[8,4,3,96,768]{4,3,2,1,0:T(8,128)(2,1)}, bf16[8,912,768]{2,1,0:T(8,128)(2,1)}, bf16[2,1024,768]{2,1,0:T(8,128)(2,1)}) custom-call(bf16[8,96,768]{2,1,0:T(8,128)(2,1)S(1)} %bitcast.74, bf16[8,96,768]{2,1,0:T(8,128)(2,1)S(1)} %bitcast.75, bf16[8,96,768]{2,1,0:T(8,128)(2,1)S(1)} %bitcast.76, bf16[576,128]{1,0:T(8,128)(2,1)S(1)} %fusion.7.a_in, ...), custom_call_target="tpu_custom_call" | custom-call | tf_op jit(solution)/shard_map/gather_weights/pallas_call | solution.py:964
  142.7 4.2 all-to-all-start.1
  149.2 32.1 %mix.1 = (bf16[2,1024,768]{2,1,0:T(8,128)(2,1)}, f32[2,8,768]{2,1,0:T(8,128)}, f32[2,8,768]{2,1,0:T(8,128)}, bf16[2,2048,768]{2,1,0:T(8,128)(2,1)}, bf16[2,1024,...) custom-call(s32[2]{0:T(128)} %dynamic_slice.6.lens, bf16[2,1024,768]{2,1,0:T(8,128)(2,1)} %get-tuple-element.54.x, ...), custom_call_target="tpu_custom_call" | custom-call | flops 17716740096 | bytes 101662720 | tf_op jit(solution)/shard_map/mix/pallas_call | solution.py:386
  181.3 51.4 %feed.1 = (bf16[2,1024,768]{2,1,0:T(8,128)(2,1)}, bf16[2,1024,768]{2,1,0:T(8,128)(2,1)}, bf16[2,4,1024,768]{3,2,1,0:T(8,128)(2,1)}, bf16[2,4,1024,768]{3,2,1,0:T...) custom-call(s32[2]{0:T(128)} %dynamic_slice.6.lens, ...), custom_call_target="tpu_custom_call" | custom-call | flops 31406948352 | bytes 107200512 | tf_op jit(solution)/shard_map/feed/pallas_call | solution.py:386
  232.7 1.7 copy-done.3
  234.5 5.2 all-to-all-start
  239.7 4.0 copy.53
  243.7 71.8 %feed_back.1 = (bf16[2,1024,768]{2,1,0:T(8,128)(2,1)}, bf16[8,4,96,768]{3,2,1,0:T(8,128)(2,1)}, bf16[8,4,96,768]{3,2,1,0:T(8,128)(2,1)}, bf16[8,4,96,768]{3,2,1,0:T(8,128)(2,1)}) custom-call(s32[2]{0:T(128)} %dynamic_slice.6.lens, bf16[2,1024,768]{2,1,0:T(8,128)(2,1)} %bitcast.80, bf16[2,1024,768]{2,1,0:T(8,128)(2,1)} %get-tuple-element.60.n2, ...), custom_call_target="tpu_custom_call" | custom-call | flops 57982058496 | bytes 103809024 | tf_op jit(solution)/shard_map/feed_back/pallas_call | solution.py:386
  315.5 16.7 %branch_back.1 = (bf16[2,1024,768]{2,1,0:T(8,128)(2,1)}, bf16[2,1024,768]{2,1,0:T(8,128)(2,1)}, bf16[2,1024,768]{2,1,0:T(8,128)(2,1)}, bf16[8,96,768]{2,1,0:T(8,128)(2,1)}, f32[8,768]{1,0:T(8,128)}) custom-call(s32[2]{0:T(128)} %dynamic_slice.6.lens, bf16[2,1024,768]{2,1,0:T(8,128)(2,1)} %get-tuple-element.64.e, ...), custom_call_target="tpu_custom_call" | custom-call | flops 4831838208 | bytes 37625856 | tf_op jit(solution)/shard_map/branch_back/pallas_call | solution.py:386
  332.2 25.6 %spectral_back.1 = (bf16[2,1024,768]{2,1,0:T(8,128)(2,1)}, bf16[8,512,768]{2,1,0:T(8,128)(2,1)}, f32[2,8,768]{2,1,0:T(8,128)}) custom-call(s32[2]{0:T(128)} %dynamic_slice.6.lens, bf16[2,1024,768]{2,1,0:T(8,128)(2,1)} %get-tuple-element.73.cg, bf16[2,2048,768]{2,1,0:T(8,128)(2,1)} %get-tuple-element.74.spec, f32[2,8,768]{2,1,0:T(8,128)} %get-tuple-element.75.mixing, ...), custom_call_target="tpu_custom_call" | custom-call | flops 12884901888 | bytes 67993600 | tf_op jit(solution)/shard_map/spectral_back/pallas_call | solution.py:386
  357.8 23.2 %input_back.1 = (bf16[2,1024,768]{2,1,0:T(8,128)(2,1)}, bf16[8,384,768]{2,1,0:T(8,128)(2,1)}, f32[16,768]{1,0:T(8,128)}) custom-call(s32[2]{0:T(128)} %dynamic_slice.6.lens, bf16[2,1024,768]{2,1,0:T(8,128)(2,1)} %get-tuple-element.76.vg, bf16[2,1024,768]{2,1,0:T(8,128)(2,1)} %get-tuple-element.77.gtg, bf16[2,1024,768]{2,1,0:T(8,128)(2,1)} %get-tuple-element.54.x, ...), custom_call_target="tpu_custom_call" | custom-call | flops 9663676416 | bytes 55468032 | tf_op jit(solution)/shard_map/input_back/pallas_call | solution.py:386
  381.0 148.2 %scatter_grads.1 = (bf16[8,3,96,768]{3,2,1,0:T(8,128)(2,1)}, f32[576,128]{1,0:T(8,128)}, f32[4,192,256]{2,1,0:T(8,128)}, f32[16,768]{1,0:T(8,128)}, bf16[4,2,256,768]{3,2,1,0:T(8,128)(2,1)}) custom-call(bf16[4,2,4,96,768]{4,3,2,1,0:T(8,128)(2,1)} %bitcast.83, bf16[4,2,4,96,768]{4,3,2,1,0:T(8,128)(2,1)} %bitcast.84, bf16[4,2,4,96,768]{4,3,2,1,0:T(8,128)(2,1)} %bitcast.85, ...), custom_call_target="tpu_custom_call" | custom-call | tf_op jit(solution)/shard_map/scatter_grads/pallas_call | solution.py:1347
  529.3 1.1 fusion.10
  530.3 0.9 slice.76
  532.0 3.6 fusion.9
  535.6 1.7 bitcast_convert_fusion.2
  537.2 1.6 copy.56
  539.6 6.9 %copy.55 = bf16[4,256,2,768]{3,2,1,0:T(2,128)(2,1)} copy(bf16[4,256,2,768]{3,1,2,0:T(8,128)(2,1)} %bitcast.89) | data formatting | bytes 6291456
  547.4 4.9 copy.54
  552.3 2.7 bitcast_convert_fusion
  555.0 1.4 dynamic-slice.2
  556.4 1.7 dynamic-slice_bitcast_fusion
  (53 shorter events, 7.5 us)
Async XLA Ops:
  3.2 4.4 copy-start.6
  3.2 4.5 copy-start.8
  3.3 4.5 copy-start.9
  3.3 4.5 copy-start.11
  3.3 4.5 copy-start.12
  3.3 4.5 copy-start.13
  3.3 4.5 copy-start.14
  3.3 4.5 copy-start.15
  3.3 4.5 copy-start.16
  3.3 4.5 copy-start.17
  3.4 4.6 copy-start
  3.4 4.6 copy-start.1
  8.0 1.3 copy-start.2
  142.7 5.8 %copy-start.10 = (s32[4,2]{0,1:T(2,128)S(1)}, s32[4,2]{0,1:T(2,128)}, u32[]{:S(2)}) copy-start(s32[4,2]{0,1:T(2,128)} %param.19) | copy-start | bytes 100
  142.7 90.0 %all-to-all-start.1 = ((bf16[4,2,1,256,768]{4,1,3,2,0:T(2,128)(2,1)}), bf16[4,2,1,256,768]{4,1,3,2,0:T(2,128)(2,1)S(1)}, u32[]{:S(2)}, u32[]{:S(2)}) async-start(bf16[4,2,1,256,768]{4,1,3,2,0:T(2,128)(2,1)} %bitcast.87), calls=%async_computation.1 | async-start | bytes 6291456 | tf_op jit(solution)/shard_map/all_to_all | solution.py:1488
  232.7 1.7 copy-start.3
  234.5 97.8 %all-to-all-start = ((bf16[4,512,768]{2,1,0:T(8,128)(2,1)}), bf16[4,512,768]{2,1,0:T(8,128)(2,1)S(1)}, u32[]{:S(2)}, u32[]{:S(2)}) async-start(bf16[4,512,768]{2,1,0:T(8,128)(2,1)} %bitcast.88), calls=%async_computation | async-start | bytes 6291456 | tf_op jit(solution)/shard_map/all_to_all | solution.py:1491
  539.6 6.9 %copy-start.7 = (f32[4,192,256]{2,1,0:T(8,128)S(1)}, f32[4,192,256]{2,1,0:T(8,128)}, u32[]{:S(2)}) copy-start(f32[4,192,256]{2,1,0:T(8,128)} %get-tuple-element.90) | copy-start | bytes 2359300
  547.4 4.9 copy-start.4
  547.4 4.9 copy-start.5

commit v5 on v4

--- a/solution.py
+++ b/solution.py
@@ -411,7 +411,7 @@
 
 def mix(x, lens, aw, vec, table, fw, first, rows, slots, scale):
     own, n, width = x.shape
-    tile = min(512, n)
+    tile = min(1024, n)
     tiles = n // tile
     steps = own * tiles
     cb = min(256, width)

time: 563 us -> 562 us (level)
  no operation moved by 1% of the time
where the time goes in v5:
time: 562 us; the launch traced here: 558 us
  Pallas kernels  502 us (89%)
  local copies, waits for them, and re-layouts  38.4 us (7%)
  starting transfers between devices  9.29 us (2%)
  other arithmetic  6.82 us (1%)
    pallas_call x6, Pallas kernels, call(): pl.pallas_call(kernel, grid_spec=spec, out_shape=tuple(outs), compiler_pa...  220 us
    pallas_call x1, Pallas kernels, scatter_grads(): pl.pallas_call(functools.partial(scatter_kernel, n_dp, n_tp, cut, mirror)...  148 us
    pallas_call x1, Pallas kernels, gather_weights(): pl.pallas_call(functools.partial(gather_kernel, n_dp, n_tp, cut, a_rows,...  133 us
    unnamed x42, local copies, waits for them, and re-layouts  21.7 us
  transfers between devices with their start and end apart: 2, of which 0 were waited for; matrix products, arithmetic and copies ran while one was open for 1% of the time, Pallas kernels for 31%

profile of v5, /device:TPU:0, one launch (start us, length us, event | category | flops | bytes accessed | tf_op | source)
XLA Modules:
  0.0 557.6 jit_solution(17306418072670405031)
XLA Ops:
  3.4 4.2 copy.58
  8.0 1.3 copy-done.2
  9.3 133.4 %gather_weights.1 = (bf16[8,4,3,96,768]{4,3,2,1,0:T(8,128)(2,1)}, bf16[8,912,768]{2,1,0:T(8,128)(2,1)}, bf16[2,1024,768]{2,1,0:T(8,128)(2,1)}) custom-call(bf16[8,96,768]{2,1,0:T(8,128)(2,1)S(1)} %bitcast.74, bf16[8,96,768]{2,1,0:T(8,128)(2,1)S(1)} %bitcast.75, bf16[8,96,768]{2,1,0:T(8,128)(2,1)S(1)} %bitcast.76, bf16[576,128]{1,0:T(8,128)(2,1)S(1)} %fusion.7.a_in, ...), custom_call_target="tpu_custom_call" | custom-call | tf_op jit(solution)/shard_map/gather_weights/pallas_call | solution.py:964
  142.7 4.2 all-to-all-start.1
  149.2 31.4 %mix.1 = (bf16[2,1024,768]{2,1,0:T(8,128)(2,1)}, f32[2,8,768]{2,1,0:T(8,128)}, f32[2,8,768]{2,1,0:T(8,128)}, bf16[2,2048,768]{2,1,0:T(8,128)(2,1)}, bf16[2,1024,...) custom-call(s32[2]{0:T(128)} %dynamic_slice.6.lens, bf16[2,1024,768]{2,1,0:T(8,128)(2,1)} %get-tuple-element.54.x, ...), custom_call_target="tpu_custom_call" | custom-call | flops 17716740096 | bytes 101662720 | tf_op jit(solution)/shard_map/mix/pallas_call | solution.py:386
  180.6 51.6 %feed.1 = (bf16[2,1024,768]{2,1,0:T(8,128)(2,1)}, bf16[2,1024,768]{2,1,0:T(8,128)(2,1)}, bf16[2,4,1024,768]{3,2,1,0:T(8,128)(2,1)}, bf16[2,4,1024,768]{3,2,1,0:T...) custom-call(s32[2]{0:T(128)} %dynamic_slice.6.lens, ...), custom_call_target="tpu_custom_call" | custom-call | flops 31406948352 | bytes 107200512 | tf_op jit(solution)/shard_map/feed/pallas_call | solution.py:386
  232.2 1.7 copy-done.3
  234.0 5.1 all-to-all-start
  239.0 4.0 copy.53
  243.1 71.8 %feed_back.1 = (bf16[2,1024,768]{2,1,0:T(8,128)(2,1)}, bf16[8,4,96,768]{3,2,1,0:T(8,128)(2,1)}, bf16[8,4,96,768]{3,2,1,0:T(8,128)(2,1)}, bf16[8,4,96,768]{3,2,1,0:T(8,128)(2,1)}) custom-call(s32[2]{0:T(128)} %dynamic_slice.6.lens, bf16[2,1024,768]{2,1,0:T(8,128)(2,1)} %bitcast.80, bf16[2,1024,768]{2,1,0:T(8,128)(2,1)} %get-tuple-element.60.n2, ...), custom_call_target="tpu_custom_call" | custom-call | flops 57982058496 | bytes 103809024 | tf_op jit(solution)/shard_map/feed_back/pallas_call | solution.py:386
  314.8 16.7 %branch_back.1 = (bf16[2,1024,768]{2,1,0:T(8,128)(2,1)}, bf16[2,1024,768]{2,1,0:T(8,128)(2,1)}, bf16[2,1024,768]{2,1,0:T(8,128)(2,1)}, bf16[8,96,768]{2,1,0:T(8,128)(2,1)}, f32[8,768]{1,0:T(8,128)}) custom-call(s32[2]{0:T(128)} %dynamic_slice.6.lens, bf16[2,1024,768]{2,1,0:T(8,128)(2,1)} %get-tuple-element.64.e, ...), custom_call_target="tpu_custom_call" | custom-call | flops 4831838208 | bytes 37625856 | tf_op jit(solution)/shard_map/branch_back/pallas_call | solution.py:386
  331.6 25.6 %spectral_back.1 = (bf16[2,1024,768]{2,1,0:T(8,128)(2,1)}, bf16[8,512,768]{2,1,0:T(8,128)(2,1)}, f32[2,8,768]{2,1,0:T(8,128)}) custom-call(s32[2]{0:T(128)} %dynamic_slice.6.lens, bf16[2,1024,768]{2,1,0:T(8,128)(2,1)} %get-tuple-element.73.cg, bf16[2,2048,768]{2,1,0:T(8,128)(2,1)} %get-tuple-element.74.spec, f32[2,8,768]{2,1,0:T(8,128)} %get-tuple-element.75.mixing, ...), custom_call_target="tpu_custom_call" | custom-call | flops 12884901888 | bytes 67993600 | tf_op jit(solution)/shard_map/spectral_back/pallas_call | solution.py:386
  357.1 23.2 %input_back.1 = (bf16[2,1024,768]{2,1,0:T(8,128)(2,1)}, bf16[8,384,768]{2,1,0:T(8,128)(2,1)}, f32[16,768]{1,0:T(8,128)}) custom-call(s32[2]{0:T(128)} %dynamic_slice.6.lens, bf16[2,1024,768]{2,1,0:T(8,128)(2,1)} %get-tuple-element.76.vg, bf16[2,1024,768]{2,1,0:T(8,128)(2,1)} %get-tuple-element.77.gtg, bf16[2,1024,768]{2,1,0:T(8,128)(2,1)} %get-tuple-element.54.x, ...), custom_call_target="tpu_custom_call" | custom-call | flops 9663676416 | bytes 55468032 | tf_op jit(solution)/shard_map/input_back/pallas_call | solution.py:386
  380.4 148.3 %scatter_grads.1 = (bf16[8,3,96,768]{3,2,1,0:T(8,128)(2,1)}, f32[576,128]{1,0:T(8,128)}, f32[4,192,256]{2,1,0:T(8,128)}, f32[16,768]{1,0:T(8,128)}, bf16[4,2,256,768]{3,2,1,0:T(8,128)(2,1)}) custom-call(bf16[4,2,4,96,768]{4,3,2,1,0:T(8,128)(2,1)} %bitcast.83, bf16[4,2,4,96,768]{4,3,2,1,0:T(8,128)(2,1)} %bitcast.84, bf16[4,2,4,96,768]{4,3,2,1,0:T(8,128)(2,1)} %bitcast.85, ...), custom_call_target="tpu_custom_call" | custom-call | tf_op jit(solution)/shard_map/scatter_grads/pallas_call | solution.py:1347
  528.6 1.1 fusion.10
  529.7 0.9 slice.76
  531.3 3.6 fusion.9
  534.9 1.7 bitcast_convert_fusion.2
  536.6 1.6 copy.56
  538.9 6.9 %copy.55 = bf16[4,256,2,768]{3,2,1,0:T(2,128)(2,1)} copy(bf16[4,256,2,768]{3,1,2,0:T(8,128)(2,1)} %bitcast.89) | data formatting | bytes 6291456
  546.7 4.9 copy.54
  551.6 2.7 bitcast_convert_fusion
  554.3 1.4 dynamic-slice.2
  555.7 1.7 dynamic-slice_bitcast_fusion
  (53 shorter events, 7.5 us)
Async XLA Ops:
  3.2 4.4 copy-start.6
  3.2 4.5 copy-start.8
  3.3 4.5 copy-start.9
  3.3 4.5 copy-start.11
  3.3 4.5 copy-start.12
  3.3 4.5 copy-start.13
  3.3 4.5 copy-start.14
  3.3 4.5 copy-start.15
  3.3 4.5 copy-start.16
  3.3 4.5 copy-start.17
  3.4 4.6 copy-start
  3.4 4.6 copy-start.1
  8.0 1.3 copy-start.2
  142.7 5.8 %copy-start.10 = (s32[4,2]{0,1:T(2,128)S(1)}, s32[4,2]{0,1:T(2,128)}, u32[]{:S(2)}) copy-start(s32[4,2]{0,1:T(2,128)} %param.19) | copy-start | bytes 100
  142.7 89.5 %all-to-all-start.1 = ((bf16[4,2,1,256,768]{4,1,3,2,0:T(2,128)(2,1)}), bf16[4,2,1,256,768]{4,1,3,2,0:T(2,128)(2,1)S(1)}, u32[]{:S(2)}, u32[]{:S(2)}) async-start(bf16[4,2,1,256,768]{4,1,3,2,0:T(2,128)(2,1)} %bitcast.87), calls=%async_computation.1 | async-start | bytes 6291456 | tf_op jit(solution)/shard_map/all_to_all | solution.py:1488
  232.2 1.7 copy-start.3
  234.0 97.6 %all-to-all-start = ((bf16[4,512,768]{2,1,0:T(8,128)(2,1)}), bf16[4,512,768]{2,1,0:T(8,128)(2,1)S(1)}, u32[]{:S(2)}, u32[]{:S(2)}) async-start(bf16[4,512,768]{2,1,0:T(8,128)(2,1)} %bitcast.88), calls=%async_computation | async-start | bytes 6291456 | tf_op jit(solution)/shard_map/all_to_all | solution.py:1491
  538.9 6.9 %copy-start.7 = (f32[4,192,256]{2,1,0:T(8,128)S(1)}, f32[4,192,256]{2,1,0:T(8,128)}, u32[]{:S(2)}) copy-start(f32[4,192,256]{2,1,0:T(8,128)} %get-tuple-element.90) | copy-start | bytes 2359300
  546.7 4.9 copy-start.4
  546.7 4.9 copy-start.5
